TPU v7x, 32 devices: a whole 2x2x4 slice. The times are simulated.
32 devices in a mesh: ha: 4 (over y, x), wa: 4 (over z), ta: 2 (over core).
Axes of the slice: x: 2, y: 2, z: 4, core: 2. Of those that a mesh axis runs over, the one named last changes fastest.
Arguments:
- hidden_states: bfloat16 [2, 96, 32, 5120], P(None, 'ha', 'wa', 'ta'), may hold values from -60 to 60
- queries: bfloat16 [2, 96, 32, 5120], P(None, 'ha', 'wa', 'ta'), may hold values from -120 to 120
- keys_values: bfloat16 [2, 2, 96, 32, 5120], P(None, None, 'ha', 'wa', 'ta'), may hold values from -16 to 16
- out_weight: bfloat16 [5120, 5120], P('ta', 'wa'), may hold values from -0.078125 to 0.078125
- mod_table: float32 [50, 3, 5120], P(None, None, 'ta'), may hold values from -4 to 4
- windows: int32 [40, 2], P('ta'), may hold values from 0 to 1, as said below
- step_index: int32 [1], replicated, may hold values from 0 to 49
Outputs:
- residual_out: bfloat16 [2, 96, 32, 5120], P(None, 'ha', 'wa', 'ta')
- ffn_input: bfloat16 [2, 96, 32, 5120], P(None, 'ha', 'wa', 'ta')
Inputs may be any that keep to these rules, and one draw needn't show every extreme that they name: `windows`: some head has both radii equal to 1.
All inputs are finite; a program needn't handle non-finite values.
Results may differ from a plain program's by a relative error of at most 0.0085.
Values may be sent and summed in bfloat16 or wider, within the bound.
No kernel may reach another device: no remote copies, remote signals or barrier semaphores. Data moves between devices by JAX's collectives and lax.ppermute only.
A program may use at most 128 MiB of HBM per device.

v0:
```python
from functools import partial
import math

import jax
import jax.numpy as jnp
from jax import lax
from jax.experimental import pallas as pl
from jax.experimental.pallas import tpu as pltpu
from jax.sharding import PartitionSpec as P

D = 5120
HD = 128
TILE = 8
LANES = 128
LEVEL_STEP = 32

EPSILON = 1e-06
VMEM_LIMIT = 32 * 1024 * 1024
MOST_VMEM = 56 * 1024 * 1024
SMALL = pl.CostEstimate(flops=1, bytes_accessed=1, transcendentals=0)


def kernel_params(limit=VMEM_LIMIT):
    return pltpu.CompilerParams(dimension_semantics=("arbitrary",), vmem_limit_bytes=limit)


def attention_kernel(windows, edges, *refs, q_count, columns_only, group):
    q_refs = refs[:q_count]
    kv_ref, top_ref, bottom_ref = refs[q_count : q_count + 3]
    refs = refs[q_count + 3 :]
    out_refs, stat_refs = refs[:q_count], refs[q_count:]
    frames, tokens, head_size = q_refs[0].shape
    span = top_ref.shape[2]
    tiles = tokens // span
    step = pl.program_id(0)
    head = jnp.minimum(step, group - 1)
    radius_row = windows[head, 0]
    radius_col = windows[head, 1]
    scale = 1.0 / math.sqrt(HD)

    @pl.when(step == 0)
    def _():
        for stat_ref in stat_refs:
            stat_ref[...] = jnp.zeros_like(stat_ref)

    def near(which, tile, wide):
        if not wide:
            return kv_ref[which, :, tile * span : (tile + 1) * span, :].reshape(-1, head_size)
        pieces = []
        if tile == 0:
            pieces.append(top_ref[which])
        low = max(tile - 1, 0) * span
        high = min(tile + 2, tiles) * span
        pieces.append(kv_ref[which, :, low:high, :])
        if tile == tiles - 1:
            pieces.append(bottom_ref[which])
        block = pieces[0] if len(pieces) == 1 else jnp.concatenate(pieces, axis=1)
        return block.reshape(-1, head_size)

    def attend(wide):
        lane = lax.broadcasted_iota(jnp.int32, (frames, span, LANES), 2)
        for tile in range(tiles):
            rows = slice(tile * span, (tile + 1) * span)
            keys = near(0, tile, wide)
            values = near(1, tile, wide)
            bias = None
            if wide and (tile == 0 or tile == tiles - 1):
                place = lax.rem(
                    lax.broadcasted_iota(jnp.int32, (1, keys.shape[0]), 1), 3 * span
                )
                low = jnp.where(edges[0] == 0, span, 0) if tile == 0 else 0
                high = jnp.where(edges[1] == 0, 2 * span, 3 * span) if tile == tiles - 1 else 3 * span
                bias = jnp.where((place >= low) & (place < high), 0.0, -jnp.inf)
            for q_ref, out_ref, stat_ref in zip(q_refs, out_refs, stat_refs):
                query = q_ref[:, rows, :].reshape(-1, head_size)
                scores = (
                    lax.dot_general(
                        query, keys, (((1,), (1,)), ((), ())), preferred_element_type=jnp.float32
                    )
                    * scale
                )
                if bias is not None:
                    scores = scores + bias
                highest = jnp.max(scores, axis=1, keepdims=True)
                expo = jnp.exp(scores - highest)
                total = jnp.sum(expo, axis=1, keepdims=True)
                output = jnp.dot(
                    expo.astype(jnp.bfloat16), values, preferred_element_type=jnp.float32
                ) * (1.0 / total)
                out_ref[:, rows, :] = output.astype(jnp.bfloat16).reshape(frames, span, head_size)
                level = (highest + jnp.log(total)).reshape(frames, span, 1)
                stat_ref[:, rows, :] = jnp.where(lane == step, level, stat_ref[:, rows, :])

    active = step < group
    if columns_only:

        @pl.when(active & (radius_col == 0))
        def _():
            for out_ref in out_refs:
                out_ref[...] = jnp.zeros_like(out_ref)

        active = active & (radius_col != 0)

    @pl.when(active & (radius_row == 0))
    def _():
        attend(False)

    @pl.when(active & (radius_row != 0))
    def _():
        attend(True)

    @pl.when(step == group)
    def _():
        for out_ref, stat_ref in zip(out_refs, stat_refs):
            level = stat_ref[...]
            high = level.astype(jnp.bfloat16).astype(jnp.float32)
            middle = (level - high).astype(jnp.bfloat16).astype(jnp.float32)
            low = level - high - middle
            packed = high + pltpu.roll(middle, LEVEL_STEP, 2) + pltpu.roll(low, 2 * LEVEL_STEP, 2)
            out_ref[...] = packed.astype(jnp.bfloat16)


def attention(windows, edges, query_blocks, keys_values, top, bottom, columns_only):
    frames, tokens, features = query_blocks[0].shape
    group = windows.shape[0]
    head_size = features // group
    span = top.shape[2]
    q_count = len(query_blocks)

    def head_of(step):
        return jnp.minimum(step, group - 1)

    q_spec = pl.BlockSpec((frames, tokens, head_size), lambda h, *_: (0, 0, head_of(h)))
    kv_spec = pl.BlockSpec((2, frames, tokens, head_size), lambda h, *_: (0, 0, 0, head_of(h)))
    halo_spec = pl.BlockSpec((2, frames, span, head_size), lambda h, *_: (0, 0, 0, head_of(h)))
    out_spec = pl.BlockSpec((frames, tokens, head_size), lambda h, *_: (0, 0, h))
    return pl.pallas_call(
        partial(attention_kernel, q_count=q_count, columns_only=columns_only, group=group),
        grid_spec=pltpu.PrefetchScalarGridSpec(
            num_scalar_prefetch=2,
            grid=(group + 1,),
            in_specs=[q_spec] * q_count + [kv_spec, halo_spec, halo_spec],
            out_specs=[out_spec] * q_count,
            scratch_shapes=[pltpu.VMEM((frames, tokens, LANES), jnp.float32)] * q_count,
        ),
        out_shape=[jax.ShapeDtypeStruct((frames, tokens, (group + 1) * head_size), jnp.bfloat16)]
        * q_count,
        compiler_params=kernel_params(),
        cost_estimate=SMALL,
        name="attend_neighbours" if columns_only else "attend_own",
    )(windows, edges, *query_blocks, keys_values, top, bottom)


def combine_kernel(windows, edges, own, left, right, own_stat, left_stat, right_stat, out, *, heads):
    first = pl.program_id(0) * heads
    frames, tokens, width = own.shape
    head_size = width // heads

    for index in range(heads):
        head = first + index
        columns = slice(index * head_size, (index + 1) * head_size)
        radius_col = windows[head, 1]

        @pl.when(radius_col == 0)
        def _(columns=columns):
            out[:, :, columns] = own[:, :, columns]

        @pl.when(radius_col != 0)
        def _(columns=columns, head=head):
            lane = lax.broadcasted_iota(jnp.int32, (LANES, head_size), 0)
            pick = jnp.where(
                (lax.rem(lane, LEVEL_STEP) == head) & (lane < 3 * LEVEL_STEP), 1.0, 0.0
            ).astype(jnp.bfloat16)

            def level(ref):
                return jnp.dot(
                    ref[...].reshape(-1, LANES), pick, preferred_element_type=jnp.float32
                ).reshape(frames, tokens, head_size)

            own_level = level(own_stat)
            left_level = jnp.where(edges[2] == 0, -jnp.inf, level(left_stat))
            right_level = jnp.where(edges[3] == 0, -jnp.inf, level(right_stat))
            highest = jnp.maximum(own_level, jnp.maximum(left_level, right_level))
            weights = [jnp.exp(x - highest) for x in (own_level, left_level, right_level)]
            mixed = sum(
                ref[:, :, columns].astype(jnp.float32) * weight
                for ref, weight in zip((own, left, right), weights)
            )
            out[:, :, columns] = (mixed / (weights[0] + weights[1] + weights[2])).astype(
                jnp.bfloat16
            )


def combine(windows, edges, outputs, features, order):
    frames, tokens, _ = outputs[0].shape
    head_count = windows.shape[0]
    heads = head_count // order
    width = features // order
    spec = pl.BlockSpec((frames, tokens, width), lambda h, *_: (0, 0, h))
    stat_spec = pl.BlockSpec(
        (frames, tokens, features // head_count), lambda h, *_: (0, 0, head_count)
    )
    return pl.pallas_call(
        partial(combine_kernel, heads=heads),
        grid_spec=pltpu.PrefetchScalarGridSpec(
            num_scalar_prefetch=2,
            grid=(order,),
            in_specs=[spec] * 3 + [stat_spec] * 3,
            out_specs=pl.BlockSpec(
                (frames, tokens, width), lambda h, windows, edges: (0, 0, h ^ edges[4])
            ),
        ),
        out_shape=jax.ShapeDtypeStruct((frames, tokens, features), jnp.bfloat16),
        compiler_params=kernel_params(),
        cost_estimate=SMALL,
        name="combine",
    )(windows, edges, *outputs, *outputs)


def project_kernel(place, attended, *refs, slots, carried, start, column):
    arrays = 1 + max(piece[0] for slot in slots for piece in slot)
    pieces, refs = refs[:arrays], refs[arrays:]
    if carried:
        carry, refs = refs[0], refs[1:]
    out, rows, weight, rows_sem, weight_sem = refs
    columns = weight.shape[1]
    depth = weight.shape[2]
    rows_copy = pltpu.make_async_copy(
        attended.at[:, start : start + depth], rows, rows_sem.at[0]
    )
    rows_copy.start()
    for index, slot in enumerate(slots):
        for block in range(columns):
            low = 0
            for number, (array, size, share, turned) in enumerate(slot):
                first = pl.multiple_of((place[0] ^ share if turned else share) * size, size)
                pltpu.make_async_copy(
                    pieces[array].at[pl.ds(first, size), block * column : (block + 1) * column],
                    weight.at[index, block, low : low + size],
                    weight_sem.at[index, block, number],
                ).start()
                low += size
    rows_copy.wait()
    for index, slot in enumerate(slots):

        def body(block, _, index=index, slot=slot):
            low = 0
            for number, (_, size, _, _) in enumerate(slot):
                piece = weight.at[index, block, low : low + size]
                pltpu.make_async_copy(piece, piece, weight_sem.at[index, block, number]).wait()
                low += size
            total = jnp.dot(rows[...], weight[index, block], preferred_element_type=jnp.float32)
            here = pl.ds(pl.multiple_of(block * column, column), column)
            if carried:
                total = total + carry[index, :, here]
            out[index, :, here] = total.astype(out.dtype)
            return 0

        lax.fori_loop(0, columns, body, 0)


def project(place, attended, arrays, slots, carry, start, dtype):
    tokens = attended.shape[0]
    width = arrays[0].shape[1]
    column = 256 if width % 256 == 0 else width
    columns = width // column
    depth = sum(piece[1] for piece in slots[0])
    anywhere = pl.BlockSpec(memory_space=pl.ANY)
    inside = pl.BlockSpec(memory_space=pltpu.VMEM)
    return pl.pallas_call(
        partial(
            project_kernel, slots=slots, carried=carry is not None, start=start, column=column
        ),
        in_specs=[pl.BlockSpec(memory_space=pltpu.SMEM), anywhere]
        + [anywhere] * len(arrays)
        + ([] if carry is None else [inside]),
        out_specs=inside,
        out_shape=jax.ShapeDtypeStruct((len(slots), tokens, width), dtype),
        scratch_shapes=[
            pltpu.VMEM((tokens, depth), attended.dtype),
            pltpu.VMEM((len(slots), columns, depth, column), attended.dtype),
            pltpu.SemaphoreType.DMA((1,)),
            pltpu.SemaphoreType.DMA((len(slots), columns, max(len(slot) for slot in slots))),
        ],
        compiler_params=pltpu.CompilerParams(vmem_limit_bytes=VMEM_LIMIT),
        cost_estimate=SMALL,
        name="project",
    )(place, attended, *arrays, *([] if carry is None else [carry]))


def mix_kernel(
    place, own_part, other_part, own_hidden, other_hidden, own_gate, other_gate, *refs
):
    mixed_ref, sums_ref = refs[-2:]
    step = pl.program_id(0)
    mine = place[3 * step] != 0
    hidden = jnp.where(
        mine, own_hidden[...].astype(jnp.float32), other_hidden[...].astype(jnp.float32)
    )
    gate = jnp.where(mine, own_gate[...], other_gate[...])
    mixed = hidden + gate * (
        own_part[0].astype(jnp.float32) + other_part[0].astype(jnp.float32)
    )
    mixed_ref[...] = mixed
    lane = lax.broadcasted_iota(jnp.int32, sums_ref.shape, 1)
    first = jnp.sum(mixed, axis=1, keepdims=True)
    second = jnp.sum(mixed * mixed, axis=1, keepdims=True)
    sums = jnp.where(lane == 0, first, jnp.where(lane == 1, second, 0.0))

    @pl.when(step == 0)
    def _():
        sums_ref[...] = sums + refs[0][...] if len(refs) == 4 else sums

    @pl.when(step != 0)
    def _():
        sums_ref[...] = sums_ref[...] + sums


def mix(place, own_part, other_part, own_hidden, other_hidden, own_gate, other_gate, carry):
    count, tokens, width = own_part.shape
    blocks = own_hidden.shape[1] // width
    part = pl.BlockSpec((1, tokens, width), lambda i, place: (i, 0, 0))
    hidden = pl.BlockSpec((tokens, width), lambda i, place: (0, place[3 * i + 1]))
    gate = pl.BlockSpec((1, width), lambda i, place: (0, place[3 * i + 1]))
    sums = pl.BlockSpec((tokens, LANES), lambda i, place: (0, 0))
    mixed = pl.BlockSpec((tokens, width), lambda i, place: (0, place[3 * i + 2]))
    return pl.pallas_call(
        mix_kernel,
        grid_spec=pltpu.PrefetchScalarGridSpec(
            num_scalar_prefetch=1,
            grid=(count,),
            in_specs=[part, part, hidden, hidden, gate, gate]
            + ([sums, pl.BlockSpec(memory_space=pl.ANY)] if carry else []),
            out_specs=[mixed, sums],
        ),
        out_shape=[
            jax.ShapeDtypeStruct((tokens, (blocks + 1) * width), jnp.float32),
            jax.ShapeDtypeStruct((tokens, LANES), jnp.float32),
        ],
        input_output_aliases={8: 0} if carry else {},
        compiler_params=kernel_params(MOST_VMEM),
        cost_estimate=SMALL,
        name="mix",
    )(
        *(place, own_part, other_part, own_hidden, other_hidden, own_gate, other_gate),
        *((carry[1], carry[0]) if carry else ()),
    )


def finish_kernel(place, own_part, other_part, *refs):
    count, _, width = own_part.shape
    sides, refs = refs[: 4 * count], refs[4 * count :]
    scale, shift_by, sums, mixed_ref, residual, ffn = refs
    blocks = residual.shape[1] // width
    first = sums[:, 0:1]
    second = sums[:, 1:2]
    late = []
    for index in range(count):
        own_hidden, other_hidden, own_gate, other_gate = sides[4 * index : 4 * index + 4]
        mine = place[3 * index] != 0
        hidden = jnp.where(
            mine, own_hidden[...].astype(jnp.float32), other_hidden[...].astype(jnp.float32)
        )
        gate = jnp.where(mine, own_gate[...], other_gate[...])
        mixed = hidden + gate * (
            own_part[index].astype(jnp.float32) + other_part[index].astype(jnp.float32)
        )
        first = first + jnp.sum(mixed, axis=1, keepdims=True)
        second = second + jnp.sum(mixed * mixed, axis=1, keepdims=True)
        late.append(mixed)
    average = first / D
    variance = second / D - average * average
    inverse = lax.rsqrt(variance + EPSILON)
    for block in range(blocks):
        columns = slice(block * width, (block + 1) * width)
        mixed = mixed_ref[:, columns]
        for index in range(count):
            here = (place[3 * index] != 0) & (place[3 * index + 1] == block)
            mixed = jnp.where(here, late[index], mixed)
        residual[:, columns] = mixed.astype(jnp.bfloat16)
        ffn[:, columns] = (
            (mixed - average) * inverse * (1.0 + scale[:, columns]) + shift_by[:, columns]
        ).astype(jnp.bfloat16)


def finish(place, own_part, other_part, own_hidden, other_hidden, own_gate, other_gate, scale, shift_by, carry):
    count, tokens, width = own_part.shape
    features = own_hidden.shape[1]
    rows = 64 if tokens % 64 == 0 else tokens
    part = pl.BlockSpec((count, rows, width), lambda i, place: (0, i, 0))
    whole = pl.BlockSpec((1, features), lambda i, place: (0, 0))
    sums = pl.BlockSpec((rows, LANES), lambda i, place: (i, 0))
    row = pl.BlockSpec((rows, features), lambda i, place: (i, 0))
    side_specs = []
    for index in range(count):
        hidden = pl.BlockSpec(
            (rows, width), lambda i, place, index=index: (i, place[3 * index + 1])
        )
        gate = pl.BlockSpec((1, width), lambda i, place, index=index: (0, place[3 * index + 1]))
        side_specs += [hidden, hidden, gate, gate]
    return pl.pallas_call(
        finish_kernel,
        grid_spec=pltpu.PrefetchScalarGridSpec(
            num_scalar_prefetch=1,
            grid=(tokens // rows,),
            in_specs=[part, part, *side_specs, whole, whole, sums, row],
            out_specs=[row, row],
        ),
        out_shape=[jax.ShapeDtypeStruct((tokens, features), jnp.bfloat16)] * 2,
        compiler_params=kernel_params(MOST_VMEM),
        cost_estimate=SMALL,
        name="finish",
    )(
        place, own_part, other_part,
        *((own_hidden, other_hidden, own_gate, other_gate) * count),
        scale, shift_by, carry[1], carry[0],
    )


def shift(block, axis, step):
    count = lax.axis_size(axis)
    pairs = [(i, i + step) for i in range(count) if 0 <= i + step < count]
    return lax.ppermute(block, axis, pairs)


def turn(block, axis, step):
    count = lax.axis_size(axis)
    return lax.ppermute(block, axis, [(i, (i + step) % count) for i in range(count)])


def swap(block, axis, bit):
    count = lax.axis_size(axis)
    return lax.ppermute(block, axis, [(i, i ^ bit) for i in range(count)])


class Tokens:
    def __init__(self, queries, keys_values, windows, order):
        self.features = queries.shape[3]
        n_ha, n_wa = lax.axis_size("ha"), lax.axis_size("wa")
        ha, wa = lax.axis_index("ha"), lax.axis_index("wa")
        turned = ha if order > 1 else 0 * ha
        self.edges = jnp.stack([ha > 0, ha < n_ha - 1, wa > 0, wa < n_wa - 1, turned]).astype(
            jnp.int32
        )
        self.windows = windows
        self.order = order
        self.queries = self.flat(queries)
        self.keys_values = self.flat(keys_values)

    def flat(self, block):
        return block.reshape(block.shape[:-3] + (-1, self.features))

    def attend(self, query_blocks, halos, columns_only):
        return attention(
            self.windows, self.edges, query_blocks, self.keys_values, *halos, columns_only
        )

    def combine(self, near, back):
        attended = combine(
            self.windows, self.edges, [near, *back], self.features, self.order
        )
        return attended.reshape(-1, self.features)


def edge_rows(keys_values):
    rows = keys_values.shape[2]
    return lax.optimization_barrier(
        (keys_values[:, :, rows - TILE :], keys_values[:, :, :TILE])
    )


def together(*blocks):
    return lax.optimization_barrier(blocks)


def paired(hidden, queries, keys_values, windows, out_weight, picked):
    ha, wa, ta = lax.axis_index("ha"), lax.axis_index("wa"), lax.axis_index("ta")
    n_wa = lax.axis_size("wa")
    blocks = n_wa // 2
    depth = out_weight.shape[0] // 4
    width = out_weight.shape[1]
    cut = depth // 2

    share = lax.optimization_barrier(lax.dynamic_slice_in_dim(out_weight, ha * depth, depth, 0))
    first = turn(share, "wa", 1)
    last_rows, first_rows = edge_rows(keys_values)
    tokens = Tokens(queries, keys_values, windows, 4)
    top = shift(last_rows, "ha", 1)
    bottom = shift(first_rows, "ha", -1)
    from_left = shift(queries, "wa", 1)
    from_right = shift(queries, "wa", -1)

    first, top, bottom = together(first, top, bottom)
    first_x = swap(first, "ha", 1)
    first_y = swap(first, "ha", 2)
    second = turn(first, "wa", 1)
    halos = tokens.flat(top), tokens.flat(bottom)
    (near,) = tokens.attend([tokens.queries], halos, False)

    near, first_x, first_y, from_left, from_right = together(
        near, first_x, first_y, from_left, from_right
    )
    first_far_x = swap(first_y[:cut], "ha", 1)
    first_far_y = swap(first_x[cut:], "ha", 2)

    first_far_x, first_far_y, second, from_left, from_right = together(
        first_far_x, first_far_y, second, from_left, from_right
    )
    third = turn(second, "wa", 1)
    second_x = swap(second, "ha", 1)
    second_y = swap(second, "ha", 2)
    for_left, for_right = tokens.attend(
        [tokens.flat(from_left), tokens.flat(from_right)], halos, True
    )

    for_left, for_right, first_far_x = together(for_left, for_right, first_far_x)
    left = shift(for_right, "wa", 1)
    right = shift(for_left, "wa", -1)

    third, second_x, second_y, first_far_x, hidden, gate = together(
        third, second_x, second_y, first_far_x, hidden, picked[0:1]
    )
    third_x = swap(third, "ha", 1)
    third_y = swap(third, "ha", 2)
    other_hidden = swap(hidden, "ta", 1)

    third_x, third_y, second_x, other_hidden = together(third_x, third_y, second_x, other_hidden)
    third_far = swap(third_y, "ha", 1)
    second_far = swap(second_x, "ha", 2)

    left, right, third_x, gate = together(left, right, third_x, gate)
    other_gate = swap(gate, "ta", 1)
    attended = tokens.combine(near, [left, right])

    place = ha.reshape(1)
    sums = project(
        place,
        attended,
        [out_weight, first, first_x, first_y, first_far_x, first_far_y],
        [
            [(0, depth, number, True) for number in range(4)],
            [(number, depth, 0, False) for number in range(1, 4)]
            + [(4, cut, 0, False), (5, depth - cut, 0, False)],
        ],
        None,
        0,
        jnp.bfloat16,
    )
    other_sums = [swap(sums[:1], "ta", 1), swap(sums[1:], "ta", 1)]
    late = project(
        place,
        attended,
        [second, second_x, second_y, third, third_x, third_y],
        [[(start + number, depth, 0, False) for number in range(3)] for start in (0, 3)],
        None,
        0,
        jnp.float32,
    )

    def placed(distance):
        block = lax.rem(wa - distance + n_wa, n_wa)
        mine = block // blocks == ta
        inner = lax.rem(block, blocks)
        return jnp.stack([mine.astype(jnp.int32), inner, jnp.where(mine, inner, blocks)])

    sides = hidden, other_hidden, gate, other_gate
    carry = None
    for distance in range(2):
        part = sums[distance : distance + 1]
        carry = mix(placed(distance), part, other_sums[distance], *sides, carry)

    second_far, third_far, late, *carry = together(second_far, third_far, late, *carry)
    late = project(
        place,
        attended,
        [second_far, third_far],
        [[(0, depth, 0, False)], [(1, depth, 0, False)]],
        late,
        3 * depth,
        jnp.bfloat16,
    )
    other_late = swap(late, "ta", 1)
    places = jnp.concatenate([placed(2), placed(3)])
    return finish(places, late, other_late, *sides, picked[2:3], picked[1:2], carry)


def gathered(hidden, queries, keys_values, windows, out_weight, picked):
    work = Tokens(queries, keys_values, windows, 1)
    last_rows, first_rows = edge_rows(keys_values)
    halos = work.flat(shift(last_rows, "ha", 1)), work.flat(shift(first_rows, "ha", -1))
    visitors = [work.flat(shift(queries, "wa", 1)), work.flat(shift(queries, "wa", -1))]
    (near,) = work.attend([work.queries], halos, False)
    for_left, for_right = work.attend(visitors, halos, True)
    attended = work.combine(near, [shift(for_right, "wa", 1), shift(for_left, "wa", -1)])
    n_ha, n_wa, n_ta = lax.axis_size("ha"), lax.axis_size("wa"), lax.axis_size("ta")
    ha, ta = lax.axis_index("ha"), lax.axis_index("ta")
    tokens, features = attended.shape
    depth = features // n_ha
    width = out_weight.shape[1]
    share = lax.dynamic_slice_in_dim(out_weight, ha * depth, depth, 0)
    weights = lax.all_gather(share, ("ha", "wa"), axis=0, tiled=False).reshape(
        n_ha, n_wa, depth, width
    )
    partial_sums = jnp.einsum(
        "thk,hwkc->wtc",
        attended.reshape(tokens, n_ha, depth),
        weights,
        preferred_element_type=jnp.float32,
    ).astype(jnp.bfloat16)
    blocks = n_wa // n_ta
    summed = None
    for step in range(n_ta):
        target = lax.rem(ta + step, n_ta)
        piece = lax.dynamic_slice_in_dim(partial_sums, target * blocks, blocks, 0)
        if step:
            piece = turn(piece, "ta", step)
        piece = piece.astype(jnp.float32)
        summed = piece if summed is None else summed + piece
    summed = jnp.transpose(summed, (1, 0, 2)).reshape(tokens, -1)
    mixed = hidden.astype(jnp.float32) + picked[0] * summed
    sum_first, sum_second = lax.psum((jnp.sum(mixed, axis=1), jnp.sum(mixed * mixed, axis=1)), "ta")
    average = (sum_first / D)[:, None]
    variance = (sum_second / D)[:, None] - average * average
    normed = (mixed - average) * lax.rsqrt(variance + EPSILON)
    ffn_input = (normed * (1.0 + picked[2]) + picked[1]).astype(jnp.bfloat16)
    return mixed.astype(jnp.bfloat16), ffn_input


def shards(hidden_states, queries, keys_values, out_weight, mod_table, windows, step_index):
    tokens = math.prod(queries.shape[:3])
    width = hidden_states.shape[3]
    picked = lax.dynamic_index_in_dim(mod_table, step_index[0], 0, keepdims=False)
    sizes = lax.axis_size("ha"), lax.axis_size("wa"), lax.axis_size("ta")
    tuned = sizes == (4, 4, 2) and out_weight.shape[0] % (20 * LANES) == 0
    residual_out, ffn_input = (paired if tuned else gathered)(
        hidden_states.reshape(tokens, width), queries, keys_values, windows, out_weight, picked
    )
    return residual_out.reshape(hidden_states.shape), ffn_input.reshape(hidden_states.shape)


def solution(mesh):
    return jax.shard_map(
        shards,
        mesh=mesh,
        in_specs=(
            P(None, "ha", "wa", "ta"),
            P(None, "ha", "wa", "ta"),
            P(None, None, "ha", "wa", "ta"),
            P("ta", "wa"),
            P(None, None, "ta"),
            P("ta", None),
            P(),
        ),
        out_specs=(P(None, "ha", "wa", "ta"), P(None, "ha", "wa", "ta")),
        check_vma=False,
    )
```

profile of v0, /device:TPU:17, one launch (start us, length us, event | category | flops | bytes accessed | tf_op | source)
XLA Modules:
  0.0 266.8 jit_solution(10664961520899660131)
XLA Ops:
  5.4 3.2 %collective-permute-start.1 = (bf16[2,2,8,8,2560]{4,3,2,1,0:T(8,128)(2,1)S(1)}, bf16[2,2,8,8,2560]{4,3,2,1,0:T(8,128)(2,1)S(1)}, u32[]{:S(2)}, u32[]{:S(2)}) collective-permute-start(bf16[2,2,8,8,2560]{4,3,2,1,0:T(8,128)(2,1)S(1)} %get-tuple-element.47), channel_id=1, source_target_pairs={{0,8},{8,16},{16,24},{1,9},{9,17},{17,25},{2,10},{10,18},{18,26},{... | collective-permute-start | bytes 3932168 | tf_op jit(solution)/shard_map/ppermute | solution.py:423
  11.9 3.4 %collective-permute-start.6 = (bf16[2,24,8,2560]{3,2,1,0:T(8,128)(2,1)}, bf16[2,24,8,2560]{3,2,1,0:T(8,128)(2,1)}, u32[]{:S(2)}, u32[]{:S(2)}) collective-permute-start(bf16[2,24,8,2560]{3,2,1,0:T(8,128)(2,1)} %param.8), channel_id=1, source_target_pairs={{2,0},{4,2},{6,4},{3,1},{5,3},{7,5},{10,8},{12,10},{14,12},{11,9},... | collective-permute-start | bytes 5898248 | tf_op jit(solution)/shard_map/ppermute | solution.py:423
  15.2 20.4 %collective-permute-done.1 = bf16[2,2,8,8,2560]{4,3,2,1,0:T(8,128)(2,1)S(1)} collective-permute-done((bf16[2,2,8,8,2560]{4,3,2,1,0:T(8,128)(2,1)S(1)}, bf16[2,2,8,8,2560]{4,3,2,1,0:T(8,128)(2,1)S(1)}, u32[]{:S(2)}, u32[]{:S(2)}) %collective-permute-start.1) | collective-permute-done | bytes 1310752 | tf_op jit(solution)/shard_map/ppermute | solution.py:423
  35.7 30.1 %collective-permute-done.2 = bf16[2,2,8,8,2560]{4,3,2,1,0:T(8,128)(2,1)S(1)} collective-permute-done((bf16[2,2,8,8,2560]{4,3,2,1,0:T(8,128)(2,1)S(1)}, bf16[2,2,8,8,2560]{4,3,2,1,0:T(8,128)(2,1)S(1)}, u32[]{:S(2)}, u32[]{:S(2)}) %collective-permute-start.2) | collective-permute-done | bytes 1310752 | tf_op jit(solution)/shard_map/ppermute | solution.py:423
  67.2 2.1 copy-done
  69.3 21.8 %attend_own.1.own.own_stat = bf16[2,192,2688]{2,1,0:T(8,128)(2,1)S(1)} custom-call(s32[20,2]{1,0:T(8,128)S(1)} %copy.12.windows, s32[5]{0:T(128)S(1)} %stack.98.edges, bf16[2,192,2560]{2,1,0:T(8,128)(2,1)} %bitcast.11.refs_0_, bf16[2,2,192,2560]{3,2,1,0:T(8,128)(2,1)S(1)} %bitcast.40, bf16[2,2,64,2560]{3,2,1,0:T(8,128)(2,1)S(1)} %bitcast.44, ...), custom_call_target="tpu_custom_call" | custom-call | flops 1 | bytes 1 | tf_op jit(solution)/shard_map/attend_own/pallas_call | solution.py:137
  92.4 9.1 %collective-permute-done.3.refs_2_ = bf16[640,1280]{1,0:T(8,128)(2,1)} collective-permute-done((bf16[640,1280]{1,0:T(8,128)(2,1)}, bf16[640,1280]{1,0:T(8,128)(2,1)}, u32[]{:S(2)}, u32[]{:S(2)}) %collective-permute-start.3) | collective-permute-done | bytes 1638432 | tf_op jit(solution)/shard_map/ppermute | solution.py:433
  105.5 10.8 %collective-permute-done.9.refs_0_ = bf16[640,1280]{1,0:T(8,128)(2,1)} collective-permute-done((bf16[640,1280]{1,0:T(8,128)(2,1)}, bf16[640,1280]{1,0:T(8,128)(2,1)}, u32[]{:S(2)}, u32[]{:S(2)}) %collective-permute-start.9) | collective-permute-done | bytes 1638432 | tf_op jit(solution)/shard_map/ppermute | solution.py:428
  116.3 2.7 %collective-permute-done.7.refs_4_ = bf16[320,1280]{1,0:T(8,128)(2,1)S(1)} collective-permute-done((bf16[320,1280]{1,0:T(8,128)(2,1)S(1)}, bf16[320,1280]{1,0:T(8,128)(2,1)S(1)}, u32[]{:S(2)}, u32[]{:S(2)}) %collective-permute-start.7) | collective-permute-done | bytes 819232 | tf_op jit(solution)/shard_map/ppermute | solution.py:433
  119.0 2.6 collective-permute-done.8.refs_5_
  124.1 2.1 copy-done.1
  126.2 31.7 %attend_neighbours.1 = (bf16[2,192,2688]{2,1,0:T(8,128)(2,1)S(1)}, bf16[2,192,2688]{2,1,0:T(8,128)(2,1)S(1)}) custom-call(s32[20,2]{1,0:T(8,128)S(1)} %copy.12.windows, s32[5]{0:T(128)S(1)} %stack.98.edges, bf16[2,192,2560]{2,1,0:T(8,128)(2,1)} %bitcast.15.refs_0_, bf16[2,192,2560]{2,1,0:T(8,128)(2,1)} %bitcast.16.refs_1_, ...), custom_call_target="tpu_custom_call" | custom-call | flops 1 | bytes 1 | tf_op jit(solution)/shard_map/attend_neighbours/pallas_call | solution.py:137
  157.9 2.7 %collective-permute-start.10 = (bf16[2,192,2688]{2,1,0:T(8,128)(2,1)S(1)}, bf16[2,192,2688]{2,1,0:T(8,128)(2,1)S(1)}, u32[]{:S(2)}, u32[]{:S(2)}) collective-permute-start(bf16[2,192,2688]{2,1,0:T(8,128)(2,1)S(1)} %get-tuple-element.62), channel_id=1, source_target_pairs={{0,2},{2,4},{4,6},{1,3},{3,5},{5,7},{8,10},{10,12},{12,14},{9,11},... | collective-permute-start | bytes 6193160 | tf_op jit(solution)/shard_map/ppermute | solution.py:423
  160.5 2.8 %collective-permute-start.11 = (bf16[2,192,2688]{2,1,0:T(8,128)(2,1)S(1)}, bf16[2,192,2688]{2,1,0:T(8,128)(2,1)S(1)}, u32[]{:S(2)}, u32[]{:S(2)}) collective-permute-start(bf16[2,192,2688]{2,1,0:T(8,128)(2,1)S(1)} %get-tuple-element.63), channel_id=1, source_target_pairs={{2,0},{4,2},{6,4},{3,1},{5,3},{7,5},{10,8},{12,10},{14,12},{11,9},... | collective-permute-start | bytes 6193160 | tf_op jit(solution)/shard_map/ppermute | solution.py:423
  167.6 35.6 %collective-permute-done.15.refs_4_ = bf16[640,1280]{1,0:T(8,128)(2,1)S(1)} collective-permute-done((bf16[640,1280]{1,0:T(8,128)(2,1)}, bf16[640,1280]{1,0:T(8,128)(2,1)S(1)}, u32[]{:S(2)}, u32[]{:S(2)}) %collective-permute-start.15) | collective-permute-done | bytes 1638432 | tf_op jit(solution)/shard_map/ppermute | solution.py:433
  206.4 2.4 collective-permute-done.11.right.right_stat
  208.7 7.2 %combine.1 = bf16[2,192,2560]{2,1,0:T(8,128)(2,1)S(1)} custom-call(s32[20,2]{1,0:T(8,128)S(1)} %copy.12.windows, s32[5]{0:T(128)S(1)} %stack.98.edges, bf16[2,192,2688]{2,1,0:T(8,128)(2,1)S(1)} %copy-done.3, bf16[2,192,2688]{2,1,0:T(8,128)(2,1)S(1)} %collective-permute-done.10.left.left_stat, ...), custom_call_target="tpu_custom_call" | custom-call | flops 1 | bytes 1 | tf_op jit(solution)/shard_map/combine/pallas_call | solution.py:203
  216.0 8.3 %project.4 = bf16[2,384,1280]{2,1,0:T(8,128)(2,1)S(1)} custom-call(s32[1]{0:T(128)} %bitcast.6.place, bf16[384,2560]{1,0:T(8,128)(2,1)S(1)} %bitcast.37, bf16[2560,1280]{1,0:T(8,128)(2,1)S(1)} %bitcast.43, bf16[640,1280]{1,0:T(8,128)(2,1)} %collective-permute-done.refs_1_, bf16[640,1280]{1,0:T(8,128)(2,1)} %collective-permute-done.3.refs_2_, ...), custom_call_target="tpu_custom_call" | custom-call | flops 1 | bytes 1 | tf_op jit(solution)/shard_map/project/pallas_call | solution.py:270
  228.7 7.4 %project.3.refs_2_ = f32[2,384,1280]{2,1,0:T(8,128)S(1)} custom-call(s32[1]{0:T(128)} %bitcast.6.place, bf16[384,2560]{1,0:T(8,128)(2,1)S(1)} %bitcast.38, bf16[640,1280]{1,0:T(8,128)(2,1)} %collective-permute-done.9.refs_0_, bf16[640,1280]{1,0:T(8,128)(2,1)} %collective-permute-done.13.refs_1_, bf16[640,1280]{1,0:T(8,128)(2,1)} %collective-permute-done.14.refs_2_, ...), custom_call_target="tpu_custom_call" | custom-call | flops 1 | bytes 1 | tf_op jit(solution)/shard_map/project/pallas_call | solution.py:270
  236.6 4.6 %mix.2 = (f32[384,3840]{1,0:T(8,128)}, f32[384,128]{1,0:T(8,128)}) custom-call(s32[3]{0:T(128)} %pad_add_fusion.1.place, bf16[1,384,1280]{2,1,0:T(8,128)(2,1)} %copy-done.10, bf16[1,384,1280]{2,1,0:T(8,128)(2,1)} %collective-permute-done.22.other_part, bf16[384,2560]{1,0:T(8,128)(2,1)} %bitcast.48, bf16[384,2560]{1,0:T(8,128)(2,1)} %copy-done.9, ...), custom_call_target="tpu_custom_call" | custom-call | flops 1 | bytes 1 | tf_op jit(solution)/shard_map/mix/pallas_call | solution.py:327
  241.3 4.7 %mix.3 = (f32[384,3840]{1,0:T(8,128)}, f32[384,128]{1,0:T(8,128)}) custom-call(s32[3]{0:T(128)} %pad_add_fusion.place, bf16[1,384,1280]{2,1,0:T(8,128)(2,1)} %get-tuple-element.95.own_part, bf16[1,384,1280]{2,1,0:T(8,128)(2,1)} %collective-permute-done.20.other_part, bf16[384,2560]{1,0:T(8,128)(2,1)} %bitcast.49, ...), custom_call_target="tpu_custom_call", output_to_operand_aliasing={{0}: (8, {})} | custom-call | flops 1 | bytes 1 | tf_op jit(solution)/shard_map/mix/pallas_call | solution.py:327
  246.0 5.7 %project.5.own_part = bf16[2,384,1280]{2,1,0:T(8,128)(2,1)} custom-call(s32[1]{0:T(128)} %bitcast.6.place, bf16[384,2560]{1,0:T(8,128)(2,1)S(1)} %bitcast.39, bf16[640,1280]{1,0:T(8,128)(2,1)} %collective-permute-done.18.refs_0_, bf16[640,1280]{1,0:T(8,128)(2,1)} %collective-permute-done.19.refs_1_, f32[2,384,1280]{2,1,0:T(8,128)S(1)} %project.3.refs_2_), custom_call_target="tpu_custom_call" | custom-call | flops 1 | bytes 1 | tf_op jit(solution)/shard_map/project/pallas_call | solution.py:270
  253.0 3.2 %collective-permute-done.23.other_part = bf16[2,384,1280]{2,1,0:T(8,128)(2,1)S(1)} collective-permute-done((bf16[2,384,1280]{2,1,0:T(8,128)(2,1)}, bf16[2,384,1280]{2,1,0:T(8,128)(2,1)S(1)}, u32[]{:S(2)}, u32[]{:S(2)}) %collective-permute-start.23) | collective-permute-done | bytes 1966112 | tf_op jit(solution)/shard_map/ppermute | solution.py:433
  257.4 9.2 %finish.1 = (bf16[384,2560]{1,0:T(8,128)(2,1)}, bf16[384,2560]{1,0:T(8,128)(2,1)}) custom-call(s32[6]{0:T(128)} %concatenate.3.place, bf16[2,384,1280]{2,1,0:T(8,128)(2,1)} %project.5.own_part, bf16[2,384,1280]{2,1,0:T(8,128)(2,1)} %copy-done.11, bf16[384,2560]{1,0:T(8,128)(2,1)} %bitcast.50, bf16[384,2560]{1,0:T(8,128)(2,1)} %copy-done.9, ...), custom_call_target="tpu_custom_call" | custom-call | flops 1 | bytes 1 | tf_op jit(solution)/shard_map/finish/pallas_call | solution.py:401
  (79 shorter events, 31.4 us)
Async XLA Ops:
  2.2 63.6 %collective-permute-start = (bf16[640,1280]{1,0:T(8,128)(2,1)S(1)}, bf16[640,1280]{1,0:T(8,128)(2,1)}, u32[]{:S(2)}, u32[]{:S(2)}) collective-permute-start(bf16[640,1280]{1,0:T(8,128)(2,1)S(1)} %constant_dynamic-slice_fusion), channel_id=1, source_target_pairs={{0,2},{2,4},{4,6},{6,0},{1,3},{3,5},{5,7},{7,1},{8,10},{10,12},{12... | collective-permute-start | bytes 4915208 | tf_op jit(solution)/shard_map/ppermute | solution.py:428
  5.4 30.2 %collective-permute-start.1 = (bf16[2,2,8,8,2560]{4,3,2,1,0:T(8,128)(2,1)S(1)}, bf16[2,2,8,8,2560]{4,3,2,1,0:T(8,128)(2,1)S(1)}, u32[]{:S(2)}, u32[]{:S(2)}) collective-permute-start(bf16[2,2,8,8,2560]{4,3,2,1,0:T(8,128)(2,1)S(1)} %get-tuple-element.47), channel_id=1, source_target_pairs={{0,8},{8,16},{16,24},{1,9},{9,17},{17,25},{2,10},{10,18},{18,26},{... | collective-permute-start | bytes 3932168 | tf_op jit(solution)/shard_map/ppermute | solution.py:423
  8.6 57.2 %collective-permute-start.2 = (bf16[2,2,8,8,2560]{4,3,2,1,0:T(8,128)(2,1)S(1)}, bf16[2,2,8,8,2560]{4,3,2,1,0:T(8,128)(2,1)S(1)}, u32[]{:S(2)}, u32[]{:S(2)}) collective-permute-start(bf16[2,2,8,8,2560]{4,3,2,1,0:T(8,128)(2,1)S(1)} %get-tuple-element.48), channel_id=1, source_target_pairs={{8,0},{16,8},{24,16},{9,1},{17,9},{25,17},{10,2},{18,10},{26,18},{... | collective-permute-start | bytes 3932168 | tf_op jit(solution)/shard_map/ppermute | solution.py:423
  9.9 82.5 %collective-permute-start.5 = (bf16[2,24,8,2560]{3,2,1,0:T(8,128)(2,1)}, bf16[2,24,8,2560]{3,2,1,0:T(8,128)(2,1)}, u32[]{:S(2)}, u32[]{:S(2)}) collective-permute-start(bf16[2,24,8,2560]{3,2,1,0:T(8,128)(2,1)} %param.8), channel_id=1, source_target_pairs={{0,2},{2,4},{4,6},{1,3},{3,5},{5,7},{8,10},{10,12},{12,14},{9,11},... | collective-permute-start | bytes 5898248 | tf_op jit(solution)/shard_map/ppermute | solution.py:423
  11.9 80.5 %collective-permute-start.6 = (bf16[2,24,8,2560]{3,2,1,0:T(8,128)(2,1)}, bf16[2,24,8,2560]{3,2,1,0:T(8,128)(2,1)}, u32[]{:S(2)}, u32[]{:S(2)}) collective-permute-start(bf16[2,24,8,2560]{3,2,1,0:T(8,128)(2,1)} %param.8), channel_id=1, source_target_pairs={{2,0},{4,2},{6,4},{3,1},{5,3},{7,5},{10,8},{12,10},{14,12},{11,9},... | collective-permute-start | bytes 5898248 | tf_op jit(solution)/shard_map/ppermute | solution.py:423
  65.8 35.7 %collective-permute-start.3 = (bf16[640,1280]{1,0:T(8,128)(2,1)}, bf16[640,1280]{1,0:T(8,128)(2,1)}, u32[]{:S(2)}, u32[]{:S(2)}) collective-permute-start(bf16[640,1280]{1,0:T(8,128)(2,1)} %collective-permute-done.refs_1_), channel_id=1, source_target_pairs={{0,8},{8,0},{16,24},{24,16},{1,9},{9,1},{17,25},{25,17},{2,10},{10... | collective-permute-start | bytes 4915208 | tf_op jit(solution)/shard_map/ppermute | solution.py:433
  66.9 34.8 %collective-permute-start.4 = (bf16[640,1280]{1,0:T(8,128)(2,1)}, bf16[640,1280]{1,0:T(8,128)(2,1)}, u32[]{:S(2)}, u32[]{:S(2)}) collective-permute-start(bf16[640,1280]{1,0:T(8,128)(2,1)} %collective-permute-done.refs_1_), channel_id=1, source_target_pairs={{0,16},{8,24},{16,0},{24,8},{1,17},{9,25},{17,1},{25,9},{2,18},{10... | collective-permute-start | bytes 4915208 | tf_op jit(solution)/shard_map/ppermute | solution.py:433
  66.9 49.3 %collective-permute-start.9 = (bf16[640,1280]{1,0:T(8,128)(2,1)}, bf16[640,1280]{1,0:T(8,128)(2,1)}, u32[]{:S(2)}, u32[]{:S(2)}) collective-permute-start(bf16[640,1280]{1,0:T(8,128)(2,1)} %collective-permute-done.refs_1_), channel_id=1, source_target_pairs={{0,2},{2,4},{4,6},{6,0},{1,3},{3,5},{5,7},{7,1},{8,10},{10,12},{12... | collective-permute-start | bytes 4915208 | tf_op jit(solution)/shard_map/ppermute | solution.py:428
  102.9 16.1 %collective-permute-start.7 = (bf16[320,1280]{1,0:T(8,128)(2,1)S(1)}, bf16[320,1280]{1,0:T(8,128)(2,1)S(1)}, u32[]{:S(2)}, u32[]{:S(2)}) collective-permute-start(bf16[320,1280]{1,0:T(8,128)(2,1)S(1)} %slice.40), channel_id=1, source_target_pairs={{0,8},{8,0},{16,24},{24,16},{1,9},{9,1},{17,25},{25,17},{2,10},{10... | collective-permute-start | bytes 2457608 | tf_op jit(solution)/shard_map/ppermute | solution.py:433
  105.2 16.4 %collective-permute-start.8 = (bf16[320,1280]{1,0:T(8,128)(2,1)S(1)}, bf16[320,1280]{1,0:T(8,128)(2,1)S(1)}, u32[]{:S(2)}, u32[]{:S(2)}) collective-permute-start(bf16[320,1280]{1,0:T(8,128)(2,1)S(1)} %slice.41), channel_id=1, source_target_pairs={{0,16},{8,24},{16,0},{24,8},{1,17},{9,25},{17,1},{25,9},{2,18},{10... | collective-permute-start | bytes 2457608 | tf_op jit(solution)/shard_map/ppermute | solution.py:433
  122.5 42.5 %collective-permute-start.12 = (bf16[640,1280]{1,0:T(8,128)(2,1)}, bf16[640,1280]{1,0:T(8,128)(2,1)}, u32[]{:S(2)}, u32[]{:S(2)}) collective-permute-start(bf16[640,1280]{1,0:T(8,128)(2,1)} %collective-permute-done.9.refs_0_), channel_id=1, source_target_pairs={{0,2},{2,4},{4,6},{6,0},{1,3},{3,5},{5,7},{7,1},{8,10},{10,12},{12... | collective-permute-start | bytes 4915208 | tf_op jit(solution)/shard_map/ppermute | solution.py:428
  122.9 42.0 %collective-permute-start.13 = (bf16[640,1280]{1,0:T(8,128)(2,1)}, bf16[640,1280]{1,0:T(8,128)(2,1)}, u32[]{:S(2)}, u32[]{:S(2)}) collective-permute-start(bf16[640,1280]{1,0:T(8,128)(2,1)} %collective-permute-done.9.refs_0_), channel_id=1, source_target_pairs={{0,8},{8,0},{16,24},{24,16},{1,9},{9,1},{17,25},{25,17},{2,10},{10... | collective-permute-start | bytes 4915208 | tf_op jit(solution)/shard_map/ppermute | solution.py:433
  122.9 42.0 %collective-permute-start.14 = (bf16[640,1280]{1,0:T(8,128)(2,1)}, bf16[640,1280]{1,0:T(8,128)(2,1)}, u32[]{:S(2)}, u32[]{:S(2)}) collective-permute-start(bf16[640,1280]{1,0:T(8,128)(2,1)} %collective-permute-done.9.refs_0_), channel_id=1, source_target_pairs={{0,16},{8,24},{16,0},{24,8},{1,17},{9,25},{17,1},{25,9},{2,18},{10... | collective-permute-start | bytes 4915208 | tf_op jit(solution)/shard_map/ppermute | solution.py:433
  157.9 48.5 %collective-permute-start.10 = (bf16[2,192,2688]{2,1,0:T(8,128)(2,1)S(1)}, bf16[2,192,2688]{2,1,0:T(8,128)(2,1)S(1)}, u32[]{:S(2)}, u32[]{:S(2)}) collective-permute-start(bf16[2,192,2688]{2,1,0:T(8,128)(2,1)S(1)} %get-tuple-element.62), channel_id=1, source_target_pairs={{0,2},{2,4},{4,6},{1,3},{3,5},{5,7},{8,10},{10,12},{12,14},{9,11},... | collective-permute-start | bytes 6193160 | tf_op jit(solution)/shard_map/ppermute | solution.py:423
  160.5 48.2 %collective-permute-start.11 = (bf16[2,192,2688]{2,1,0:T(8,128)(2,1)S(1)}, bf16[2,192,2688]{2,1,0:T(8,128)(2,1)S(1)}, u32[]{:S(2)}, u32[]{:S(2)}) collective-permute-start(bf16[2,192,2688]{2,1,0:T(8,128)(2,1)S(1)} %get-tuple-element.63), channel_id=1, source_target_pairs={{2,0},{4,2},{6,4},{3,1},{5,3},{7,5},{10,8},{12,10},{14,12},{11,9},... | collective-permute-start | bytes 6193160 | tf_op jit(solution)/shard_map/ppermute | solution.py:423
  165.0 38.5 %collective-permute-start.17 = (bf16[384,2560]{1,0:T(8,128)(2,1)S(1)}, bf16[384,2560]{1,0:T(8,128)(2,1)S(1)}, u32[]{:S(2)}, u32[]{:S(2)}) collective-permute-start(bf16[384,2560]{1,0:T(8,128)(2,1)S(1)} %bitcast.52), channel_id=1, source_target_pairs={{0,1},{1,0},{2,3},{3,2},{4,5},{5,4},{6,7},{7,6},{8,9},{9,8},{10,11... | collective-permute-start | bytes 5898248 | tf_op jit(solution)/shard_map/ppermute | solution.py:433
  165.5 37.7 %collective-permute-start.15 = (bf16[640,1280]{1,0:T(8,128)(2,1)}, bf16[640,1280]{1,0:T(8,128)(2,1)S(1)}, u32[]{:S(2)}, u32[]{:S(2)}) collective-permute-start(bf16[640,1280]{1,0:T(8,128)(2,1)} %collective-permute-done.12.refs_3_), channel_id=1, source_target_pairs={{0,8},{8,0},{16,24},{24,16},{1,9},{9,1},{17,25},{25,17},{2,10},{10... | collective-permute-start | bytes 4915208 | tf_op jit(solution)/shard_map/ppermute | solution.py:433
  166.6 36.9 %collective-permute-start.16 = (bf16[640,1280]{1,0:T(8,128)(2,1)}, bf16[640,1280]{1,0:T(8,128)(2,1)}, u32[]{:S(2)}, u32[]{:S(2)}) collective-permute-start(bf16[640,1280]{1,0:T(8,128)(2,1)} %collective-permute-done.12.refs_3_), channel_id=1, source_target_pairs={{0,16},{8,24},{16,0},{24,8},{1,17},{9,25},{17,1},{25,9},{2,18},{10... | collective-permute-start | bytes 4915208 | tf_op jit(solution)/shard_map/ppermute | solution.py:433
  203.6 42.5 %collective-permute-start.18 = (bf16[640,1280]{1,0:T(8,128)(2,1)}, bf16[640,1280]{1,0:T(8,128)(2,1)}, u32[]{:S(2)}, u32[]{:S(2)}) collective-permute-start(bf16[640,1280]{1,0:T(8,128)(2,1)} %collective-permute-done.13.refs_1_), channel_id=1, source_target_pairs={{0,16},{8,24},{16,0},{24,8},{1,17},{9,25},{17,1},{25,9},{2,18},{10... | collective-permute-start | bytes 4915208 | tf_op jit(solution)/shard_map/ppermute | solution.py:433
  204.6 41.4 %collective-permute-start.19 = (bf16[640,1280]{1,0:T(8,128)(2,1)}, bf16[640,1280]{1,0:T(8,128)(2,1)}, u32[]{:S(2)}, u32[]{:S(2)}) collective-permute-start(bf16[640,1280]{1,0:T(8,128)(2,1)} %collective-permute-done.16.refs_5_), channel_id=1, source_target_pairs={{0,8},{8,0},{16,24},{24,16},{1,9},{9,1},{17,25},{25,17},{2,10},{10... | collective-permute-start | bytes 4915208 | tf_op jit(solution)/shard_map/ppermute | solution.py:433
  225.4 10.6 %collective-permute-start.22 = (bf16[1,384,1280]{2,1,0:T(8,128)(2,1)S(1)}, bf16[1,384,1280]{2,1,0:T(8,128)(2,1)}, u32[]{:S(2)}, u32[]{:S(2)}) collective-permute-start(bf16[1,384,1280]{2,1,0:T(8,128)(2,1)S(1)} %get-tuple-element.94.own_part), channel_id=1, source_target_pairs={{0,1},{1,0},{2,3},{3,2},{4,5},{5,4},{6,7},{7,6},{8,9},{9,8},{10,11... | collective-permute-start | bytes 2949128 | tf_op jit(solution)/shard_map/ppermute | solution.py:433
  225.4 15.9 %collective-permute-start.20 = (bf16[1,384,1280]{2,1,0:T(8,128)(2,1)}, bf16[1,384,1280]{2,1,0:T(8,128)(2,1)}, u32[]{:S(2)}, u32[]{:S(2)}) collective-permute-start(bf16[1,384,1280]{2,1,0:T(8,128)(2,1)} %get-tuple-element.95.own_part), channel_id=1, source_target_pairs={{0,1},{1,0},{2,3},{3,2},{4,5},{5,4},{6,7},{7,6},{8,9},{9,8},{10,11... | collective-permute-start | bytes 2949128 | tf_op jit(solution)/shard_map/ppermute | solution.py:433
  226.6 9.5 %collective-permute-start.21 = (f32[1,2560]{1,0:T(1,128)S(1)}, f32[1,2560]{1,0:T(1,128)S(1)}, u32[]{:S(2)}, u32[]{:S(2)}) collective-permute-start(f32[1,2560]{1,0:T(1,128)S(1)} %get-tuple-element.80.own_gate.refs_2_.refs_6_), channel_id=1, source_target_pairs={{0,1},{1,0},{2,3},{3,2},{4,5},{5,4},{6,7},{7,6},{8,9},{9,8},{10,11... | collective-permute-start | bytes 30728 | tf_op jit(solution)/shard_map/ppermute | solution.py:433
  251.7 4.4 %collective-permute-start.23 = (bf16[2,384,1280]{2,1,0:T(8,128)(2,1)}, bf16[2,384,1280]{2,1,0:T(8,128)(2,1)S(1)}, u32[]{:S(2)}, u32[]{:S(2)}) collective-permute-start(bf16[2,384,1280]{2,1,0:T(8,128)(2,1)} %project.5.own_part), channel_id=1, source_target_pairs={{0,1},{1,0},{2,3},{3,2},{4,5},{5,4},{6,7},{7,6},{8,9},{9,8},{10,11... | collective-permute-start | bytes 5898248 | tf_op jit(solution)/shard_map/ppermute | solution.py:433
  (17 other events, 485.3 us)
where the time goes:
time: 268 us; the launch traced here: 267 us
  waiting for transfers between devices  118 us (44%)
  Pallas kernels  101 us (38%)
  starting transfers between devices  25.8 us (10%)
  local copies, waits for them, and re-layouts  19.1 us (7%)
    ppermute x6, waiting for transfers between devices, shift(): return lax.ppermute(block, axis, pairs)  53.8 us
    ppermute x15, waiting for transfers between devices, swap(): return lax.ppermute(block, axis, [(i, i ^ bit) for i in range(count)])  53.7 us
    pallas_call x2, Pallas kernels, attention(): pl.pallas_call(partial(attention_kernel, q_count=q_count, columns_only=co...  53.5 us
    pallas_call x3, Pallas kernels, project(): pl.pallas_call(partial(project_kernel, slots=slots, carried=carry is not...  21.4 us
    ppermute x6, starting transfers between devices, shift(): return lax.ppermute(block, axis, pairs)  15.2 us
    ppermute x3, waiting for transfers between devices, turn(): lax.ppermute(block, axis, [(i, (i + step) % count) for i in range(count)])  10.8 us
    unnamed x35, local copies, waits for them, and re-layouts  9.86 us
    pallas_call x2, Pallas kernels, mix(): pl.pallas_call(mix_kernel, grid_spec=pltpu.PrefetchScalarGridSpec(num_sca...  9.37 us
  transfers between devices with their start and end apart: 24, of which 12 were waited for; matrix products, arithmetic and copies ran while one was open for 3% of the time, Pallas kernels for 32%

commit v1 on v0

--- a/solution.py
+++ b/solution.py
@@ -24,18 +24,102 @@
     return pltpu.CompilerParams(dimension_semantics=("arbitrary",), vmem_limit_bytes=limit)
 
 
-def attention_kernel(windows, edges, *refs, q_count, columns_only, group):
+class Plan:
+    def __init__(self, windows, order):
+        heads = windows.shape[0]
+        self.heads = heads
+        self.most = max(heads * 7 // 10, 1)
+        self.order = order
+        n_ha, n_wa = lax.axis_size("ha"), lax.axis_size("wa")
+        ha, wa = lax.axis_index("ha"), lax.axis_index("wa")
+        number = lax.broadcasted_iota(jnp.int32, (2, heads, heads), 1)
+        other = lax.broadcasted_iota(jnp.int32, (2, heads, heads), 2)
+        idle = jnp.where(windows.T > 0, 0, 1)
+        before = (idle[:, None, :] < idle[:, :, None]) | (
+            (idle[:, None, :] == idle[:, :, None]) & (other < number)
+        )
+        position = jnp.sum(before.astype(jnp.int32), axis=2)
+        sorted_heads = jnp.sum(jnp.where(position[:, None, :] == number, other, 0), axis=2)
+        turned = ha if order > 1 else 0 * ha
+        edges = jnp.stack([ha > 0, ha < n_ha - 1, wa > 0, wa < n_wa - 1, turned]).astype(jnp.int32)
+        self.vector = jnp.concatenate(
+            [windows.T.reshape(-1), position.reshape(-1), sorted_heads.reshape(-1), edges]
+        )
+        counts = lax.pmax(jnp.sum(1.0 - idle, axis=1), "ta")
+        self.more_rows = counts[0] > self.most
+        self.more_cols = counts[1] > self.most
+
+    def row_radius(self, vector, head):
+        return vector[head]
+
+    def col_radius(self, vector, head):
+        return vector[self.heads + head]
+
+    def row_position(self, vector, head):
+        return vector[2 * self.heads + head]
+
+    def col_position(self, vector, head):
+        return vector[3 * self.heads + head]
+
+    def row_head(self, vector, position):
+        return vector[4 * self.heads + position]
+
+    def col_head(self, vector, position):
+        return vector[5 * self.heads + position]
+
+    def edge(self, vector, number):
+        return vector[6 * self.heads + number]
+
+
+def pack_kernel(vector, source, *refs, head_of, first, rows):
+    outs, sem = refs[:-1], refs[-1]
+    copies = []
+    for number, (out, (low, size)) in enumerate(zip(outs, rows)):
+        for slot in range(out.shape[-1] // HD):
+            start = pl.multiple_of(head_of(vector, first + slot) * HD, HD)
+            lead = (slice(None),) * (len(source.shape) - 2)
+            copies.append(
+                pltpu.make_async_copy(
+                    source.at[(*lead, pl.ds(low, size), pl.ds(start, HD))],
+                    out.at[(*lead, slice(None), pl.ds(slot * HD, HD))],
+                    sem.at[number, slot],
+                )
+            )
+    for copy in copies:
+        copy.start()
+    for copy in copies:
+        copy.wait()
+
+
+def pack(vector, source, head_of, first, count, rows):
+    anywhere = pl.BlockSpec(memory_space=pl.ANY)
+    return pl.pallas_call(
+        partial(pack_kernel, head_of=head_of, first=first, rows=rows),
+        in_specs=[pl.BlockSpec(memory_space=pltpu.SMEM), anywhere],
+        out_specs=[anywhere] * len(rows),
+        out_shape=[
+            jax.ShapeDtypeStruct((*source.shape[:-2], size, count * HD), source.dtype)
+            for _, size in rows
+        ],
+        scratch_shapes=[pltpu.SemaphoreType.DMA((len(rows), count))],
+        compiler_params=pltpu.CompilerParams(vmem_limit_bytes=VMEM_LIMIT),
+        cost_estimate=SMALL,
+        name="pack",
+    )(vector, source)
+
+
+def attention_kernel(vector, *refs, plan, head_of, q_count, visiting, group):
     q_refs = refs[:q_count]
-    kv_ref, top_ref, bottom_ref = refs[q_count : q_count + 3]
-    refs = refs[q_count + 3 :]
-    out_refs, stat_refs = refs[:q_count], refs[q_count:]
+    kv_ref, top_ref, bottom_ref, top_rest, bottom_rest = refs[q_count : q_count + 5]
+    refs = refs[q_count + 5 :]
+    out_refs, stat_refs, halo = refs[:q_count], refs[q_count : 2 * q_count], refs[2 * q_count]
     frames, tokens, head_size = q_refs[0].shape
     span = top_ref.shape[2]
     tiles = tokens // span
     step = pl.program_id(0)
-    head = jnp.minimum(step, group - 1)
-    radius_row = windows[head, 0]
-    radius_col = windows[head, 1]
+    head = head_of(vector, step)
+    radius_row = plan.row_radius(vector, head)
+    radius_col = plan.col_radius(vector, head)
     scale = 1.0 / math.sqrt(HD)
 
     @pl.when(step == 0)
@@ -48,12 +132,12 @@
             return kv_ref[which, :, tile * span : (tile + 1) * span, :].reshape(-1, head_size)
         pieces = []
         if tile == 0:
-            pieces.append(top_ref[which])
+            pieces.append(halo[0, which])
         low = max(tile - 1, 0) * span
         high = min(tile + 2, tiles) * span
         pieces.append(kv_ref[which, :, low:high, :])
         if tile == tiles - 1:
-            pieces.append(bottom_ref[which])
+            pieces.append(halo[1, which])
         block = pieces[0] if len(pieces) == 1 else jnp.concatenate(pieces, axis=1)
         return block.reshape(-1, head_size)
 
@@ -68,8 +152,11 @@
                 place = lax.rem(
                     lax.broadcasted_iota(jnp.int32, (1, keys.shape[0]), 1), 3 * span
                 )
-                low = jnp.where(edges[0] == 0, span, 0) if tile == 0 else 0
-                high = jnp.where(edges[1] == 0, 2 * span, 3 * span) if tile == tiles - 1 else 3 * span
+                low, high = 0, 3 * span
+                if tile == 0:
+                    low = jnp.where(plan.edge(vector, 0) == 0, span, 0)
+                if tile == tiles - 1:
+                    high = jnp.where(plan.edge(vector, 1) == 0, 2 * span, 3 * span)
                 bias = jnp.where((place >= low) & (place < high), 0.0, -jnp.inf)
             for q_ref, out_ref, stat_ref in zip(q_refs, out_refs, stat_refs):
                 query = q_ref[:, rows, :].reshape(-1, head_size)
@@ -92,7 +179,7 @@
                 stat_ref[:, rows, :] = jnp.where(lane == step, level, stat_ref[:, rows, :])
 
     active = step < group
-    if columns_only:
+    if visiting:
 
         @pl.when(active & (radius_col == 0))
         def _():
@@ -104,6 +191,18 @@
     @pl.when(active & (radius_row == 0))
     def _():
         attend(False)
+
+    always = plan.row_position(vector, head) < plan.most
+
+    @pl.when(active & (radius_row != 0) & always)
+    def _():
+        halo[0] = top_ref[...]
+        halo[1] = bottom_ref[...]
+
+    @pl.when(active & (radius_row != 0) & jnp.logical_not(always))
+    def _():
+        halo[0] = top_rest[...]
+        halo[1] = bottom_rest[...]
 
     @pl.when(active & (radius_row != 0))
     def _():
@@ -120,109 +219,136 @@
             out_ref[...] = packed.astype(jnp.bfloat16)
 
 
-def attention(windows, edges, query_blocks, keys_values, top, bottom, columns_only):
+def attention(plan, vector, query_blocks, keys_values, halos, first=None):
     frames, tokens, features = query_blocks[0].shape
-    group = windows.shape[0]
-    head_size = features // group
-    span = top.shape[2]
+    group = features // HD
+    span = halos[0].shape[2]
     q_count = len(query_blocks)
-
-    def head_of(step):
+    visiting = first is not None
+
+    def slot_of(step):
         return jnp.minimum(step, group - 1)
 
-    q_spec = pl.BlockSpec((frames, tokens, head_size), lambda h, *_: (0, 0, head_of(h)))
-    kv_spec = pl.BlockSpec((2, frames, tokens, head_size), lambda h, *_: (0, 0, 0, head_of(h)))
-    halo_spec = pl.BlockSpec((2, frames, span, head_size), lambda h, *_: (0, 0, 0, head_of(h)))
-    out_spec = pl.BlockSpec((frames, tokens, head_size), lambda h, *_: (0, 0, h))
+    def head_of(vector, step):
+        return plan.col_head(vector, first + slot_of(step)) if visiting else slot_of(step)
+
+    def kv_index(step, vector):
+        return 0, 0, 0, head_of(vector, step)
+
+    def halo_index(step, vector):
+        position = plan.row_position(vector, head_of(vector, step))
+        return 0, 0, 0, jnp.minimum(position, plan.most - 1)
+
+    def rest_index(step, vector):
+        position = plan.row_position(vector, head_of(vector, step))
+        return 0, 0, 0, jnp.maximum(position - plan.most, 0)
+
+    q_spec = pl.BlockSpec((frames, tokens, HD), lambda step, _: (0, 0, slot_of(step)))
+    kv_spec = pl.BlockSpec((2, frames, tokens, HD), kv_index)
+    halo_spec = pl.BlockSpec((2, frames, span, HD), halo_index)
+    rest_spec = pl.BlockSpec((2, frames, span, HD), rest_index)
+    out_spec = pl.BlockSpec((frames, tokens, HD), lambda step, _: (0, 0, step))
     return pl.pallas_call(
-        partial(attention_kernel, q_count=q_count, columns_only=columns_only, group=group),
+        partial(
+            attention_kernel,
+            plan=plan,
+            head_of=head_of,
+            q_count=q_count,
+            visiting=visiting,
+            group=group,
+        ),
         grid_spec=pltpu.PrefetchScalarGridSpec(
-            num_scalar_prefetch=2,
+            num_scalar_prefetch=1,
             grid=(group + 1,),
-            in_specs=[q_spec] * q_count + [kv_spec, halo_spec, halo_spec],
+            in_specs=[q_spec] * q_count + [kv_spec] + [halo_spec] * 2 + [rest_spec] * 2,
             out_specs=[out_spec] * q_count,
-            scratch_shapes=[pltpu.VMEM((frames, tokens, LANES), jnp.float32)] * q_count,
+            scratch_shapes=[pltpu.VMEM((frames, tokens, LANES), jnp.float32)] * q_count
+            + [pltpu.VMEM((2, 2, frames, span, HD), jnp.bfloat16)],
         ),
-        out_shape=[jax.ShapeDtypeStruct((frames, tokens, (group + 1) * head_size), jnp.bfloat16)]
+        out_shape=[jax.ShapeDtypeStruct((frames, tokens, (group + 1) * HD), jnp.bfloat16)]
         * q_count,
         compiler_params=kernel_params(),
         cost_estimate=SMALL,
-        name="attend_neighbours" if columns_only else "attend_own",
-    )(windows, edges, *query_blocks, keys_values, top, bottom)
-
-
-def combine_kernel(windows, edges, own, left, right, own_stat, left_stat, right_stat, out, *, heads):
+        name="attend_visitors" if visiting else "attend_own",
+    )(vector, *query_blocks, keys_values, *halos)
+
+
+def combine_kernel(vector, own, own_stat, left, right, left_rest, right_rest, out, *, plan, heads):
     first = pl.program_id(0) * heads
-    frames, tokens, width = own.shape
-    head_size = width // heads
+    frames, tokens, _ = own.shape
+
+    def level(stat, number):
+        lane = lax.broadcasted_iota(jnp.int32, (LANES, HD), 0)
+        pick = jnp.where(
+            (lax.rem(lane, LEVEL_STEP) == number) & (lane < 3 * LEVEL_STEP), 1.0, 0.0
+        ).astype(jnp.bfloat16)
+        return jnp.dot(
+            stat.reshape(-1, LANES), pick, preferred_element_type=jnp.float32
+        ).reshape(frames, tokens, HD)
 
     for index in range(heads):
         head = first + index
-        columns = slice(index * head_size, (index + 1) * head_size)
-        radius_col = windows[head, 1]
-
-        @pl.when(radius_col == 0)
+        columns = slice(index * HD, (index + 1) * HD)
+        across = plan.col_radius(vector, head) != 0
+        position = plan.col_position(vector, head)
+
+        @pl.when(jnp.logical_not(across))
         def _(columns=columns):
             out[:, :, columns] = own[:, :, columns]
 
-        @pl.when(radius_col != 0)
-        def _(columns=columns, head=head):
-            lane = lax.broadcasted_iota(jnp.int32, (LANES, head_size), 0)
-            pick = jnp.where(
-                (lax.rem(lane, LEVEL_STEP) == head) & (lane < 3 * LEVEL_STEP), 1.0, 0.0
-            ).astype(jnp.bfloat16)
-
-            def level(ref):
-                return jnp.dot(
-                    ref[...].reshape(-1, LANES), pick, preferred_element_type=jnp.float32
-                ).reshape(frames, tokens, head_size)
-
-            own_level = level(own_stat)
-            left_level = jnp.where(edges[2] == 0, -jnp.inf, level(left_stat))
-            right_level = jnp.where(edges[3] == 0, -jnp.inf, level(right_stat))
-            highest = jnp.maximum(own_level, jnp.maximum(left_level, right_level))
-            weights = [jnp.exp(x - highest) for x in (own_level, left_level, right_level)]
-            mixed = sum(
-                ref[:, :, columns].astype(jnp.float32) * weight
-                for ref, weight in zip((own, left, right), weights)
-            )
+        def join(sides, slot, columns, head):
+            here = pl.ds(pl.multiple_of(slot * HD, HD), HD)
+            levels = [level(own_stat[...], head)]
+            values = [own[:, :, columns]]
+            for number, side in enumerate(sides):
+                value = level(side[:, :, side.shape[2] - LANES :], slot)
+                levels.append(jnp.where(plan.edge(vector, 2 + number) == 0, -jnp.inf, value))
+                values.append(side[:, :, here])
+            highest = jnp.maximum(levels[0], jnp.maximum(levels[1], levels[2]))
+            weights = [jnp.exp(x - highest) for x in levels]
+            mixed = sum(value.astype(jnp.float32) * weight for value, weight in zip(values, weights))
             out[:, :, columns] = (mixed / (weights[0] + weights[1] + weights[2])).astype(
                 jnp.bfloat16
             )
 
-
-def combine(windows, edges, outputs, features, order):
-    frames, tokens, _ = outputs[0].shape
-    head_count = windows.shape[0]
-    heads = head_count // order
-    width = features // order
-    spec = pl.BlockSpec((frames, tokens, width), lambda h, *_: (0, 0, h))
-    stat_spec = pl.BlockSpec(
-        (frames, tokens, features // head_count), lambda h, *_: (0, 0, head_count)
-    )
+        @pl.when(across & (position < plan.most))
+        def _(position=position, columns=columns, head=head):
+            join((left, right), position, columns, head)
+
+        @pl.when(across & (position >= plan.most))
+        def _(position=position, columns=columns, head=head):
+            join((left_rest, right_rest), position - plan.most, columns, head)
+
+
+def combine(plan, vector, near, sides):
+    frames, tokens, _ = near.shape
+    heads = plan.heads // plan.order
+    spec = pl.BlockSpec((frames, tokens, heads * HD), lambda h, _: (0, 0, h))
+    stat_spec = pl.BlockSpec((frames, tokens, HD), lambda h, _: (0, 0, plan.heads))
     return pl.pallas_call(
-        partial(combine_kernel, heads=heads),
+        partial(combine_kernel, plan=plan, heads=heads),
         grid_spec=pltpu.PrefetchScalarGridSpec(
-            num_scalar_prefetch=2,
-            grid=(order,),
-            in_specs=[spec] * 3 + [stat_spec] * 3,
+            num_scalar_prefetch=1,
+            grid=(plan.order,),
+            in_specs=[spec, stat_spec]
+            + [pl.BlockSpec(side.shape, lambda h, _: (0, 0, 0)) for side in sides],
             out_specs=pl.BlockSpec(
-                (frames, tokens, width), lambda h, windows, edges: (0, 0, h ^ edges[4])
+                (frames, tokens, heads * HD), lambda h, vector: (0, 0, h ^ plan.edge(vector, 4))
             ),
         ),
-        out_shape=jax.ShapeDtypeStruct((frames, tokens, features), jnp.bfloat16),
+        out_shape=jax.ShapeDtypeStruct((frames, tokens, plan.heads * HD), jnp.bfloat16),
         compiler_params=kernel_params(),
         cost_estimate=SMALL,
         name="combine",
-    )(windows, edges, *outputs, *outputs)
+    )(vector, near, near, *sides)
 
 
 def project_kernel(place, attended, *refs, slots, carried, start, column):
     arrays = 1 + max(piece[0] for slot in slots for piece in slot)
     pieces, refs = refs[:arrays], refs[arrays:]
     if carried:
-        carry, refs = refs[0], refs[1:]
-    out, rows, weight, rows_sem, weight_sem = refs
+        carry, refs = refs[: len(slots)], refs[len(slots) :]
+    outs, (rows, weight, rows_sem, weight_sem) = refs[: len(slots)], refs[len(slots) :]
     columns = weight.shape[1]
     depth = weight.shape[2]
     rows_copy = pltpu.make_async_copy(
@@ -252,8 +378,8 @@
             total = jnp.dot(rows[...], weight[index, block], preferred_element_type=jnp.float32)
             here = pl.ds(pl.multiple_of(block * column, column), column)
             if carried:
-                total = total + carry[index, :, here]
-            out[index, :, here] = total.astype(out.dtype)
+                total = total + carry[index][0, :, here]
+            outs[index][0, :, here] = total.astype(outs[index].dtype)
             return 0
 
         lax.fori_loop(0, columns, body, 0)
@@ -273,9 +399,9 @@
         ),
         in_specs=[pl.BlockSpec(memory_space=pltpu.SMEM), anywhere]
         + [anywhere] * len(arrays)
-        + ([] if carry is None else [inside]),
-        out_specs=inside,
-        out_shape=jax.ShapeDtypeStruct((len(slots), tokens, width), dtype),
+        + ([] if carry is None else [inside] * len(slots)),
+        out_specs=[inside] * len(slots),
+        out_shape=[jax.ShapeDtypeStruct((1, tokens, width), dtype)] * len(slots),
         scratch_shapes=[
             pltpu.VMEM((tokens, depth), attended.dtype),
             pltpu.VMEM((len(slots), columns, depth, column), attended.dtype),
@@ -285,7 +411,7 @@
         compiler_params=pltpu.CompilerParams(vmem_limit_bytes=VMEM_LIMIT),
         cost_estimate=SMALL,
         name="project",
-    )(place, attended, *arrays, *([] if carry is None else [carry]))
+    )(place, attended, *arrays, *([] if carry is None else carry))
 
 
 def mix_kernel(
@@ -347,8 +473,9 @@
     )
 
 
-def finish_kernel(place, own_part, other_part, *refs):
-    count, _, width = own_part.shape
+def finish_kernel(place, *refs, count):
+    own_part, other_part, refs = refs[:count], refs[count : 2 * count], refs[2 * count :]
+    width = own_part[0].shape[2]
     sides, refs = refs[: 4 * count], refs[4 * count :]
     scale, shift_by, sums, mixed_ref, residual, ffn = refs
     blocks = residual.shape[1] // width
@@ -363,7 +490,7 @@
         )
         gate = jnp.where(mine, own_gate[...], other_gate[...])
         mixed = hidden + gate * (
-            own_part[index].astype(jnp.float32) + other_part[index].astype(jnp.float32)
+            own_part[index][0].astype(jnp.float32) + other_part[index][0].astype(jnp.float32)
         )
         first = first + jnp.sum(mixed, axis=1, keepdims=True)
         second = second + jnp.sum(mixed * mixed, axis=1, keepdims=True)
@@ -384,10 +511,11 @@
 
 
 def finish(place, own_part, other_part, own_hidden, other_hidden, own_gate, other_gate, scale, shift_by, carry):
-    count, tokens, width = own_part.shape
+    count = len(own_part)
+    _, tokens, width = own_part[0].shape
     features = own_hidden.shape[1]
     rows = 64 if tokens % 64 == 0 else tokens
-    part = pl.BlockSpec((count, rows, width), lambda i, place: (0, i, 0))
+    part = pl.BlockSpec((1, rows, width), lambda i, place: (0, i, 0))
     whole = pl.BlockSpec((1, features), lambda i, place: (0, 0))
     sums = pl.BlockSpec((rows, LANES), lambda i, place: (i, 0))
     row = pl.BlockSpec((rows, features), lambda i, place: (i, 0))
@@ -399,11 +527,11 @@
         gate = pl.BlockSpec((1, width), lambda i, place, index=index: (0, place[3 * index + 1]))
         side_specs += [hidden, hidden, gate, gate]
     return pl.pallas_call(
-        finish_kernel,
+        partial(finish_kernel, count=count),
         grid_spec=pltpu.PrefetchScalarGridSpec(
             num_scalar_prefetch=1,
             grid=(tokens // rows,),
-            in_specs=[part, part, *side_specs, whole, whole, sums, row],
+            in_specs=[part] * (2 * count) + [*side_specs, whole, whole, sums, row],
             out_specs=[row, row],
         ),
         out_shape=[jax.ShapeDtypeStruct((tokens, features), jnp.bfloat16)] * 2,
@@ -411,7 +539,7 @@
         cost_estimate=SMALL,
         name="finish",
     )(
-        place, own_part, other_part,
+        place, *own_part, *other_part,
         *((own_hidden, other_hidden, own_gate, other_gate) * count),
         scale, shift_by, carry[1], carry[0],
     )
@@ -435,38 +563,60 @@
 
 class Tokens:
     def __init__(self, queries, keys_values, windows, order):
-        self.features = queries.shape[3]
-        n_ha, n_wa = lax.axis_size("ha"), lax.axis_size("wa")
-        ha, wa = lax.axis_index("ha"), lax.axis_index("wa")
-        turned = ha if order > 1 else 0 * ha
-        self.edges = jnp.stack([ha > 0, ha < n_ha - 1, wa > 0, wa < n_wa - 1, turned]).astype(
-            jnp.int32
+        self.plan = Plan(windows, order)
+        self.queries = queries.reshape(queries.shape[0], -1, queries.shape[3])
+        self.keys_values = keys_values.reshape(*keys_values.shape[:2], -1, keys_values.shape[4])
+        self.span = TILE * queries.shape[2]
+        self.parts = (0, self.plan.most), (self.plan.most, self.plan.heads - self.plan.most)
+
+    def edge_rows(self, vector, part):
+        low = self.queries.shape[1] - self.span
+        rows = [(low, self.span), (0, self.span)]
+        return pack(vector, self.keys_values, self.plan.row_head, *self.parts[part], rows)
+
+    def leaving(self, vector, part):
+        rows = [(0, self.queries.shape[1])]
+        return pack(vector, self.queries, self.plan.col_head, *self.parts[part], rows)[0]
+
+    def halos(self, rows):
+        return shift(rows[0], "ha", 1), shift(rows[1], "ha", -1)
+
+    def rest_halos(self, vector):
+        shape = (*self.keys_values.shape[:2], self.span, self.parts[1][1] * HD)
+        return lax.cond(
+            self.plan.more_rows,
+            lambda vector: self.halos(self.edge_rows(vector, 1)),
+            lambda vector: (jnp.zeros(shape, jnp.bfloat16),) * 2,
+            vector,
         )
-        self.windows = windows
-        self.order = order
-        self.queries = self.flat(queries)
-        self.keys_values = self.flat(keys_values)
-
-    def flat(self, block):
-        return block.reshape(block.shape[:-3] + (-1, self.features))
-
-    def attend(self, query_blocks, halos, columns_only):
-        return attention(
-            self.windows, self.edges, query_blocks, self.keys_values, *halos, columns_only
+
+    def stay(self, vector, halos):
+        return attention(self.plan, vector, [self.queries], self.keys_values, halos)[0]
+
+    def visit(self, vector, visitors, halos, part=0):
+        first = self.parts[part][0]
+        return attention(self.plan, vector, visitors, self.keys_values, halos, first)
+
+    def rest_sides(self, vector, halos):
+        shape = (*self.queries.shape[:2], (self.parts[1][1] + 1) * HD)
+
+        def send(vector, *halos):
+            queries = self.leaving(vector, 1)
+            visitors = shift(queries, "wa", 1), shift(queries, "wa", -1)
+            for_left, for_right = self.visit(vector, visitors, halos, 1)
+            return shift(for_right, "wa", 1), shift(for_left, "wa", -1)
+
+        return lax.cond(
+            self.plan.more_cols,
+            send,
+            lambda vector, *halos: (jnp.zeros(shape, jnp.bfloat16),) * 2,
+            vector,
+            *halos,
         )
 
-    def combine(self, near, back):
-        attended = combine(
-            self.windows, self.edges, [near, *back], self.features, self.order
-        )
-        return attended.reshape(-1, self.features)
-
-
-def edge_rows(keys_values):
-    rows = keys_values.shape[2]
-    return lax.optimization_barrier(
-        (keys_values[:, :, rows - TILE :], keys_values[:, :, :TILE])
-    )
+    def combine(self, vector, near, sides):
+        attended = combine(self.plan, vector, near, sides)
+        return attended.reshape(-1, attended.shape[2])
 
 
 def together(*blocks):
@@ -483,19 +633,19 @@
 
     share = lax.optimization_barrier(lax.dynamic_slice_in_dim(out_weight, ha * depth, depth, 0))
     first = turn(share, "wa", 1)
-    last_rows, first_rows = edge_rows(keys_values)
     tokens = Tokens(queries, keys_values, windows, 4)
-    top = shift(last_rows, "ha", 1)
-    bottom = shift(first_rows, "ha", -1)
+    vector = tokens.plan.vector
+    top, bottom = tokens.halos(tokens.edge_rows(vector, 0))
+    queries = tokens.leaving(vector, 0)
     from_left = shift(queries, "wa", 1)
     from_right = shift(queries, "wa", -1)
 
-    first, top, bottom = together(first, top, bottom)
+    first, top, bottom, vector = together(first, top, bottom, vector)
     first_x = swap(first, "ha", 1)
     first_y = swap(first, "ha", 2)
     second = turn(first, "wa", 1)
-    halos = tokens.flat(top), tokens.flat(bottom)
-    (near,) = tokens.attend([tokens.queries], halos, False)
+    halos = top, bottom, *tokens.rest_halos(vector)
+    near = tokens.stay(vector, halos)
 
     near, first_x, first_y, from_left, from_right = together(
         near, first_x, first_y, from_left, from_right
@@ -509,20 +659,19 @@
     third = turn(second, "wa", 1)
     second_x = swap(second, "ha", 1)
     second_y = swap(second, "ha", 2)
-    for_left, for_right = tokens.attend(
-        [tokens.flat(from_left), tokens.flat(from_right)], halos, True
-    )
+    for_left, for_right = tokens.visit(vector, (from_left, from_right), halos)
 
     for_left, for_right, first_far_x = together(for_left, for_right, first_far_x)
     left = shift(for_right, "wa", 1)
     right = shift(for_left, "wa", -1)
 
-    third, second_x, second_y, first_far_x, hidden, gate = together(
-        third, second_x, second_y, first_far_x, hidden, picked[0:1]
+    third, second_x, second_y, first_far_x, hidden, gate, vector = together(
+        third, second_x, second_y, first_far_x, hidden, picked[0:1], vector
     )
     third_x = swap(third, "ha", 1)
     third_y = swap(third, "ha", 2)
     other_hidden = swap(hidden, "ta", 1)
+    rest_sides = tokens.rest_sides(vector, halos)
 
     third_x, third_y, second_x, other_hidden = together(third_x, third_y, second_x, other_hidden)
     third_far = swap(third_y, "ha", 1)
@@ -530,7 +679,7 @@
 
     left, right, third_x, gate = together(left, right, third_x, gate)
     other_gate = swap(gate, "ta", 1)
-    attended = tokens.combine(near, [left, right])
+    attended = tokens.combine(vector, near, [left, right, *rest_sides])
 
     place = ha.reshape(1)
     sums = project(
@@ -546,7 +695,7 @@
         0,
         jnp.bfloat16,
     )
-    other_sums = [swap(sums[:1], "ta", 1), swap(sums[1:], "ta", 1)]
+    other_sums = [swap(part, "ta", 1) for part in sums]
     late = project(
         place,
         attended,
@@ -566,10 +715,10 @@
     sides = hidden, other_hidden, gate, other_gate
     carry = None
     for distance in range(2):
-        part = sums[distance : distance + 1]
-        carry = mix(placed(distance), part, other_sums[distance], *sides, carry)
-
-    second_far, third_far, late, *carry = together(second_far, third_far, late, *carry)
+        carry = mix(placed(distance), sums[distance], other_sums[distance], *sides, carry)
+
+    second_far, third_far, *rest = together(second_far, third_far, *late, *carry)
+    late, carry = rest[:2], rest[2:]
     late = project(
         place,
         attended,
@@ -579,21 +728,23 @@
         3 * depth,
         jnp.bfloat16,
     )
-    other_late = swap(late, "ta", 1)
+    other_late = [swap(part, "ta", 1) for part in late]
     places = jnp.concatenate([placed(2), placed(3)])
     return finish(places, late, other_late, *sides, picked[2:3], picked[1:2], carry)
 
 
 def gathered(hidden, queries, keys_values, windows, out_weight, picked):
-    work = Tokens(queries, keys_values, windows, 1)
-    last_rows, first_rows = edge_rows(keys_values)
-    halos = work.flat(shift(last_rows, "ha", 1)), work.flat(shift(first_rows, "ha", -1))
-    visitors = [work.flat(shift(queries, "wa", 1)), work.flat(shift(queries, "wa", -1))]
-    (near,) = work.attend([work.queries], halos, False)
-    for_left, for_right = work.attend(visitors, halos, True)
-    attended = work.combine(near, [shift(for_right, "wa", 1), shift(for_left, "wa", -1)])
     n_ha, n_wa, n_ta = lax.axis_size("ha"), lax.axis_size("wa"), lax.axis_size("ta")
     ha, ta = lax.axis_index("ha"), lax.axis_index("ta")
+    work = Tokens(queries, keys_values, windows, 1)
+    vector = work.plan.vector
+    halos = *work.halos(work.edge_rows(vector, 0)), *work.rest_halos(vector)
+    sent = work.leaving(vector, 0)
+    visitors = shift(sent, "wa", 1), shift(sent, "wa", -1)
+    near = work.stay(vector, halos)
+    for_left, for_right = work.visit(vector, visitors, halos)
+    sides = shift(for_right, "wa", 1), shift(for_left, "wa", -1)
+    attended = work.combine(vector, near, [*sides, *work.rest_sides(vector, halos)])
     tokens, features = attended.shape
     depth = features // n_ha
     width = out_weight.shape[1]

time: 268 us -> 285 us (1.063)
  local copies, waits for them, and re-layouts: 19.1 us -> 27.3 us
  starting transfers between devices: 25.8 us -> 33.3 us
  blocking collectives: 0 us -> 4.55 us
  waiting for transfers between devices: 118 us -> 114 us
    ppermute x15 -> x16, waiting for transfers between devices: 53.7 us -> 33.9 us  [swap(): return lax.ppermute(block, axis, [(i, i ^ bit) for i in range(count)])]
    ppermute x3, waiting for transfers between devices: 10.8 us -> 30.5 us  [turn(): lax.ppermute(block, axis, [(i, (i + step) % count) for i in range(count)])]
    unnamed x35 -> x66, local copies, waits for them, and re-layouts: 9.86 us -> 18.7 us
    pmax x0 -> x1, blocking collectives: none -> 4.55 us  [__init__(): counts = lax.pmax(jnp.sum(1.0 - idle, axis=1), 'ta')]
    ppermute x6, waiting for transfers between devices: 53.8 us -> 49.4 us  [shift(): return lax.ppermute(block, axis, pairs)]
    ppermute x15 -> x16, starting transfers between devices: 8.6 us -> 12.8 us  [swap(): return lax.ppermute(block, axis, [(i, i ^ bit) for i in range(count)])]
    another operation x1 -> x4, local copies, waits for them, and re-layouts: 0.08 us -> 3.43 us  [__init__(): jnp.stack([ha > 0, ha < n_ha - 1, wa > 0, wa < n_wa - 1, turned])]
    pallas_call x4 -> x6, Pallas kernels: 69.9 us -> 67.5 us  [the longest x2 46.9 us: attention(): pl.pallas_call(partial(attention_kernel, plan=plan, head_of=head_of, q_co...]
  transfers between devices with their start and end apart: 24 -> 25, of which waited for: 12 -> 11; matrix products, arithmetic and copies ran while one was open for 3% -> 3% of each run, Pallas kernels for 32% -> 30%
where the time goes in v1:
time: 285 us; the launch traced here: 283 us
  waiting for transfers between devices  114 us (40%)
  Pallas kernels  98.9 us (35%)
  starting transfers between devices  33.3 us (12%)
  local copies, waits for them, and re-layouts  27.3 us (10%)
  blocking collectives  4.55 us (2%)
  between operations  3.14 us (1%)
    ppermute x6, waiting for transfers between devices, shift(): return lax.ppermute(block, axis, pairs)  49.4 us
    pallas_call x2, Pallas kernels, attention(): pl.pallas_call(partial(attention_kernel, plan=plan, head_of=head_of, q_co...  46.9 us
    ppermute x16, waiting for transfers between devices, swap(): return lax.ppermute(block, axis, [(i, i ^ bit) for i in range(count)])  33.9 us
    ppermute x3, waiting for transfers between devices, turn(): lax.ppermute(block, axis, [(i, (i + step) % count) for i in range(count)])  30.5 us
    pallas_call x3, Pallas kernels, project(): pl.pallas_call(partial(project_kernel, slots=slots, carried=carry is not...  22 us
    unnamed x66, local copies, waits for them, and re-layouts  18.7 us
    ppermute x6, starting transfers between devices, shift(): return lax.ppermute(block, axis, pairs)  16.9 us
    ppermute x16, starting transfers between devices, swap(): return lax.ppermute(block, axis, [(i, i ^ bit) for i in range(count)])  12.8 us
  transfers between devices with their start and end apart: 25, of which 11 were waited for; matrix products, arithmetic and copies ran while one was open for 3% of the time, Pallas kernels for 30%

profile of v1, /device:TPU:17, one launch (start us, length us, event | category | flops | bytes accessed | tf_op | source)
XLA Modules:
  0.0 283.1 jit_solution(1619412440475239107)
XLA Ops:
  5.1 2.4 pack.6
  7.5 3.2 %collective-permute-start.7 = (bf16[2,2,64,1792]{3,2,1,0:T(8,128)(2,1)S(1)}, bf16[2,2,64,1792]{3,2,1,0:T(8,128)(2,1)S(1)}, u32[]{:S(2)}, u32[]{:S(2)}) collective-permute-start(bf16[2,2,64,1792]{3,2,1,0:T(8,128)(2,1)S(1)} %get-tuple-element.91), channel_id=1, source_target_pairs={{0,8},{8,16},{16,24},{1,9},{9,17},{17,25},{2,10},{10,18},{18,26},{... | collective-permute-start | bytes 2752520 | tf_op jit(solution)/shard_map/ppermute | solution.py:551
  12.0 17.3 %collective-permute-done.7.refs_2_.refs_3_ = bf16[2,2,64,1792]{3,2,1,0:T(8,128)(2,1)S(1)} collective-permute-done((bf16[2,2,64,1792]{3,2,1,0:T(8,128)(2,1)S(1)}, bf16[2,2,64,1792]{3,2,1,0:T(8,128)(2,1)S(1)}, u32[]{:S(2)}, u32[]{:S(2)}) %collective-permute-start.7) | collective-permute-done | bytes 917536 | tf_op jit(solution)/shard_map/ppermute | solution.py:551
  29.3 21.6 %collective-permute-done.8.refs_3_.refs_4_ = bf16[2,2,64,1792]{3,2,1,0:T(8,128)(2,1)S(1)} collective-permute-done((bf16[2,2,64,1792]{3,2,1,0:T(8,128)(2,1)S(1)}, bf16[2,2,64,1792]{3,2,1,0:T(8,128)(2,1)S(1)}, u32[]{:S(2)}, u32[]{:S(2)}) %collective-permute-start.8) | collective-permute-done | bytes 917536 | tf_op jit(solution)/shard_map/ppermute | solution.py:551
  57.0 4.6 %pmax.7 = f32[2]{0:T(128)S(1)} all-reduce(f32[2]{0:T(128)S(1)} %subtract_reduce_fusion), channel_id=1, replica_groups=mesh['ha'=4,'wa'=4,'ta'=2] {'ta'}, use_global_device_ids=true, to_apply=%region_3.4 | all-reduce | flops 2 | bytes 16 | tf_op jit(solution)/shard_map/pmax | solution.py:48
  64.4 4.3 %collective-permute-start.11 = (bf16[2,192,1792]{2,1,0:T(8,128)(2,1)}, bf16[2,192,1792]{2,1,0:T(8,128)(2,1)S(1)}, u32[]{:S(2)}, u32[]{:S(2)}) collective-permute-start(bf16[2,192,1792]{2,1,0:T(8,128)(2,1)} %pack.7), channel_id=1, source_target_pairs={{0,2},{2,4},{4,6},{1,3},{3,5},{5,7},{8,10},{10,12},{12,14},{9,11},... | collective-permute-start | bytes 4128776 | tf_op jit(solution)/shard_map/ppermute | solution.py:551
  68.8 22.7 %attend_own.1.own.own_stat = bf16[2,192,2688]{2,1,0:T(8,128)(2,1)S(1)} custom-call(s32[125]{0:T(128)S(1)} %concatenate.7.vector, bf16[2,192,2560]{2,1,0:T(8,128)(2,1)} %bitcast.47, bf16[2,2,192,2560]{3,2,1,0:T(8,128)(2,1)} %bitcast.44, bf16[2,2,64,1792]{3,2,1,0:T(8,128)(2,1)} %copy-done.24, bf16[2,2,64,1792]{3,2,1,0:T(8,128)(2,1)} %copy-done.26, ...), custom_call_target="tpu_custom_call" | custom-call | flops 1 | bytes 1 | tf_op jit(solution)/shard_map/attend_own/pallas_call | solution.py:251
  91.5 6.7 %collective-permute-done.11.refs_0_ = bf16[2,192,1792]{2,1,0:T(8,128)(2,1)S(1)} collective-permute-done((bf16[2,192,1792]{2,1,0:T(8,128)(2,1)}, bf16[2,192,1792]{2,1,0:T(8,128)(2,1)S(1)}, u32[]{:S(2)}, u32[]{:S(2)}) %collective-permute-start.11) | collective-permute-done | bytes 1376288 | tf_op jit(solution)/shard_map/ppermute | solution.py:551
  102.9 30.5 %collective-permute-done.15.refs_0_ = bf16[640,1280]{1,0:T(8,128)(2,1)} collective-permute-done((bf16[640,1280]{1,0:T(8,128)(2,1)}, bf16[640,1280]{1,0:T(8,128)(2,1)}, u32[]{:S(2)}, u32[]{:S(2)}) %collective-permute-start.15) | collective-permute-done | bytes 1638432 | tf_op jit(solution)/shard_map/ppermute | solution.py:556
  136.3 2.2 collective-permute-start.16
  142.1 24.2 %attend_visitors.3 = (bf16[2,192,1920]{2,1,0:T(8,128)(2,1)S(1)}, bf16[2,192,1920]{2,1,0:T(8,128)(2,1)S(1)}) custom-call(s32[125]{0:T(128)S(1)} %concatenate.7.vector, bf16[2,192,1792]{2,1,0:T(8,128)(2,1)S(1)} %copy-done.12, bf16[2,192,1792]{2,1,0:T(8,128)(2,1)} %collective-permute-done.12.refs_1_, bf16[2,2,192,2560]{3,2,1,0:T(8,128)(2,1)} %bitcast.45, ...), custom_call_target="tpu_custom_call" | custom-call | flops 1 | bytes 1 | tf_op jit(solution)/shard_map/attend_visitors/pallas_call | solution.py:251
  168.6 3.0 %collective-permute-done.18.refs_2_ = bf16[640,1280]{1,0:T(8,128)(2,1)S(1)} collective-permute-done((bf16[640,1280]{1,0:T(8,128)(2,1)}, bf16[640,1280]{1,0:T(8,128)(2,1)S(1)}, u32[]{:S(2)}, u32[]{:S(2)}) %collective-permute-start.18) | collective-permute-done | bytes 1638432 | tf_op jit(solution)/shard_map/ppermute | solution.py:561
  172.2 2.6 collective-permute-start.23
  179.2 4.0 %collective-permute-start.19 = (bf16[2,192,1920]{2,1,0:T(8,128)(2,1)}, bf16[2,192,1920]{2,1,0:T(8,128)(2,1)S(1)}, u32[]{:S(2)}, u32[]{:S(2)}) collective-permute-start(bf16[2,192,1920]{2,1,0:T(8,128)(2,1)} %copy-done.20), channel_id=1, source_target_pairs={{0,2},{2,4},{4,6},{1,3},{3,5},{5,7},{8,10},{10,12},{12,14},{9,11},... | collective-permute-start | bytes 4423688 | tf_op jit(solution)/shard_map/ppermute | solution.py:551
  185.3 27.0 %collective-permute-done.22.refs_5_ = bf16[640,1280]{1,0:T(8,128)(2,1)} collective-permute-done((bf16[640,1280]{1,0:T(8,128)(2,1)S(1)}, bf16[640,1280]{1,0:T(8,128)(2,1)}, u32[]{:S(2)}, u32[]{:S(2)}) %collective-permute-start.22) | collective-permute-done | bytes 1638432 | tf_op jit(solution)/shard_map/ppermute | solution.py:561
  214.7 3.7 %collective-permute-done.20.right = bf16[2,192,1920]{2,1,0:T(8,128)(2,1)S(1)} collective-permute-done((bf16[2,192,1920]{2,1,0:T(8,128)(2,1)}, bf16[2,192,1920]{2,1,0:T(8,128)(2,1)S(1)}, u32[]{:S(2)}, u32[]{:S(2)}) %collective-permute-start.20) | collective-permute-done | bytes 1474592 | tf_op jit(solution)/shard_map/ppermute | solution.py:551
  220.0 7.0 %combine.1 = bf16[2,192,2560]{2,1,0:T(8,128)(2,1)S(1)} custom-call(s32[125]{0:T(128)S(1)} %concatenate.7.vector, bf16[2,192,2688]{2,1,0:T(8,128)(2,1)S(1)} %copy-done.1, bf16[2,192,2688]{2,1,0:T(8,128)(2,1)S(1)} %copy-done.1, bf16[2,192,1920]{2,1,0:T(8,128)(2,1)S(1)} %collective-permute-done.19.left, ...), custom_call_target="tpu_custom_call" | custom-call | flops 1 | bytes 1 | tf_op jit(solution)/shard_map/combine/pallas_call | solution.py:328
  227.1 2.9 %copy-done.2 = bf16[2560,1280]{1,0:T(8,128)(2,1)S(1)} copy-done((bf16[2560,1280]{1,0:T(8,128)(2,1)S(1)}, bf16[2560,1280]{1,0:T(8,128)(2,1)}, u32[]{:S(2)}) %copy-start.2) | copy-done | bytes 6553624
  229.9 9.5 %project.4 = (bf16[1,384,1280]{2,1,0:T(8,128)(2,1)S(1)}, bf16[1,384,1280]{2,1,0:T(8,128)(2,1)}) custom-call(s32[1]{0:T(128)} %bitcast.6.place, bf16[384,2560]{1,0:T(8,128)(2,1)S(1)} %bitcast.39, bf16[2560,1280]{1,0:T(8,128)(2,1)S(1)} %copy-done.2, bf16[640,1280]{1,0:T(8,128)(2,1)} %collective-permute-done.6.refs_1_, bf16[640,1280]{1,0:T(8,128)(2,1)S(1)} %copy-done.6, ...), custom_call_target="tpu_custom_call" | custom-call | flops 1 | bytes 1 | tf_op jit(solution)/shard_map/project/pallas_call | solution.py:396
  245.7 7.3 %project.3 = (f32[1,384,1280]{2,1,0:T(8,128)S(1)}, f32[1,384,1280]{2,1,0:T(8,128)S(1)}) custom-call(s32[1]{0:T(128)} %bitcast.6.place, bf16[384,2560]{1,0:T(8,128)(2,1)S(1)} %bitcast.40, bf16[640,1280]{1,0:T(8,128)(2,1)} %collective-permute-done.15.refs_0_, bf16[640,1280]{1,0:T(8,128)(2,1)} %collective-permute-done.17.refs_1_, ...), custom_call_target="tpu_custom_call" | custom-call | flops 1 | bytes 1 | tf_op jit(solution)/shard_map/project/pallas_call | solution.py:396
  253.5 4.6 %mix.2 = (f32[384,3840]{1,0:T(8,128)}, f32[384,128]{1,0:T(8,128)}) custom-call(s32[3]{0:T(128)} %pad_add_fusion.1.place, bf16[1,384,1280]{2,1,0:T(8,128)(2,1)} %copy-done.13, bf16[1,384,1280]{2,1,0:T(8,128)(2,1)} %collective-permute-done.28.other_part, bf16[384,2560]{1,0:T(8,128)(2,1)} %bitcast.15.own_hidden.refs_4_.refs_8_, ...), custom_call_target="tpu_custom_call" | custom-call | flops 1 | bytes 1 | tf_op jit(solution)/shard_map/mix/pallas_call | solution.py:453
  258.2 4.7 %mix.3 = (f32[384,3840]{1,0:T(8,128)}, f32[384,128]{1,0:T(8,128)}) custom-call(s32[3]{0:T(128)} %pad_add_fusion.place, bf16[1,384,1280]{2,1,0:T(8,128)(2,1)} %get-tuple-element.131.own_part, bf16[1,384,1280]{2,1,0:T(8,128)(2,1)} %collective-permute-done.26.other_part, ...), custom_call_target="tpu_custom_call", output_to_operand_aliasing={{0}: (8, {})} | custom-call | flops 1 | bytes 1 | tf_op jit(solution)/shard_map/mix/pallas_call | solution.py:453
  262.9 5.3 %project.5 = (bf16[1,384,1280]{2,1,0:T(8,128)(2,1)S(1)}, bf16[1,384,1280]{2,1,0:T(8,128)(2,1)}) custom-call(s32[1]{0:T(128)} %bitcast.6.place, bf16[384,2560]{1,0:T(8,128)(2,1)S(1)} %bitcast.41, bf16[640,1280]{1,0:T(8,128)(2,1)} %collective-permute-done.24.refs_0_, bf16[640,1280]{1,0:T(8,128)(2,1)} %collective-permute-done.25.refs_1_, ...), custom_call_target="tpu_custom_call" | custom-call | flops 1 | bytes 1 | tf_op jit(solution)/shard_map/project/pallas_call | solution.py:396
  273.5 9.4 %finish.1 = (bf16[384,2560]{1,0:T(8,128)(2,1)}, bf16[384,2560]{1,0:T(8,128)(2,1)}) custom-call(s32[6]{0:T(128)} %concatenate.6.place, bf16[1,384,1280]{2,1,0:T(8,128)(2,1)} %copy-done.14, bf16[1,384,1280]{2,1,0:T(8,128)(2,1)} %get-tuple-element.144.refs_1_, bf16[1,384,1280]{2,1,0:T(8,128)(2,1)} %copy-done.28, bf16[1,384,1280]{2,1,0:T(8,128)(2,1)} %copy-done.29, ...), custom_call_target="tpu_custom_call" | custom-call | flops 1 | bytes 1 | tf_op jit(solution)/shard_map/finish/pallas_call | solution.py:529
  (129 shorter events, 52.7 us)
Async XLA Ops:
  2.2 48.7 %collective-permute-start.6 = (bf16[640,1280]{1,0:T(8,128)(2,1)S(1)}, bf16[640,1280]{1,0:T(8,128)(2,1)}, u32[]{:S(2)}, u32[]{:S(2)}) collective-permute-start(bf16[640,1280]{1,0:T(8,128)(2,1)S(1)} %constant_dynamic-slice_fusion), channel_id=1, source_target_pairs={{0,2},{2,4},{4,6},{6,0},{1,3},{3,5},{5,7},{7,1},{8,10},{10,12},{12... | collective-permute-start | bytes 4915208 | tf_op jit(solution)/shard_map/ppermute | solution.py:556
  7.5 21.8 %collective-permute-start.7 = (bf16[2,2,64,1792]{3,2,1,0:T(8,128)(2,1)S(1)}, bf16[2,2,64,1792]{3,2,1,0:T(8,128)(2,1)S(1)}, u32[]{:S(2)}, u32[]{:S(2)}) collective-permute-start(bf16[2,2,64,1792]{3,2,1,0:T(8,128)(2,1)S(1)} %get-tuple-element.91), channel_id=1, source_target_pairs={{0,8},{8,16},{16,24},{1,9},{9,17},{17,25},{2,10},{10,18},{18,26},{... | collective-permute-start | bytes 2752520 | tf_op jit(solution)/shard_map/ppermute | solution.py:551
  10.7 40.2 %collective-permute-start.8 = (bf16[2,2,64,1792]{3,2,1,0:T(8,128)(2,1)S(1)}, bf16[2,2,64,1792]{3,2,1,0:T(8,128)(2,1)S(1)}, u32[]{:S(2)}, u32[]{:S(2)}) collective-permute-start(bf16[2,2,64,1792]{3,2,1,0:T(8,128)(2,1)S(1)} %get-tuple-element.92), channel_id=1, source_target_pairs={{8,0},{16,8},{24,16},{9,1},{17,9},{25,17},{10,2},{18,10},{26,18},{... | collective-permute-start | bytes 2752520 | tf_op jit(solution)/shard_map/ppermute | solution.py:551
  50.9 48.4 %collective-permute-start.10 = (bf16[640,1280]{1,0:T(8,128)(2,1)}, bf16[640,1280]{1,0:T(8,128)(2,1)S(1)}, u32[]{:S(2)}, u32[]{:S(2)}) collective-permute-start(bf16[640,1280]{1,0:T(8,128)(2,1)} %collective-permute-done.6.refs_1_), channel_id=1, source_target_pairs={{0,16},{8,24},{16,0},{24,8},{1,17},{9,25},{17,1},{25,9},{2,18},{10... | collective-permute-start | bytes 4915208 | tf_op jit(solution)/shard_map/ppermute | solution.py:561
  51.9 47.4 %collective-permute-start.9 = (bf16[640,1280]{1,0:T(8,128)(2,1)}, bf16[640,1280]{1,0:T(8,128)(2,1)S(1)}, u32[]{:S(2)}, u32[]{:S(2)}) collective-permute-start(bf16[640,1280]{1,0:T(8,128)(2,1)} %collective-permute-done.6.refs_1_), channel_id=1, source_target_pairs={{0,8},{8,0},{16,24},{24,16},{1,9},{9,1},{17,25},{25,17},{2,10},{10... | collective-permute-start | bytes 4915208 | tf_op jit(solution)/shard_map/ppermute | solution.py:561
  54.9 36.5 %collective-permute-start.12 = (bf16[2,192,1792]{2,1,0:T(8,128)(2,1)}, bf16[2,192,1792]{2,1,0:T(8,128)(2,1)}, u32[]{:S(2)}, u32[]{:S(2)}) collective-permute-start(bf16[2,192,1792]{2,1,0:T(8,128)(2,1)} %pack.7), channel_id=1, source_target_pairs={{2,0},{4,2},{6,4},{3,1},{5,3},{7,5},{10,8},{12,10},{14,12},{11,9},... | collective-permute-start | bytes 4128776 | tf_op jit(solution)/shard_map/ppermute | solution.py:551
  64.4 33.8 %collective-permute-start.11 = (bf16[2,192,1792]{2,1,0:T(8,128)(2,1)}, bf16[2,192,1792]{2,1,0:T(8,128)(2,1)S(1)}, u32[]{:S(2)}, u32[]{:S(2)}) collective-permute-start(bf16[2,192,1792]{2,1,0:T(8,128)(2,1)} %pack.7), channel_id=1, source_target_pairs={{0,2},{2,4},{4,6},{1,3},{3,5},{5,7},{8,10},{10,12},{12,14},{9,11},... | collective-permute-start | bytes 4128776 | tf_op jit(solution)/shard_map/ppermute | solution.py:551
  68.7 64.6 %collective-permute-start.15 = (bf16[640,1280]{1,0:T(8,128)(2,1)}, bf16[640,1280]{1,0:T(8,128)(2,1)}, u32[]{:S(2)}, u32[]{:S(2)}) collective-permute-start(bf16[640,1280]{1,0:T(8,128)(2,1)} %collective-permute-done.6.refs_1_), channel_id=1, source_target_pairs={{0,2},{2,4},{4,6},{6,0},{1,3},{3,5},{5,7},{7,1},{8,10},{10,12},{12... | collective-permute-start | bytes 4915208 | tf_op jit(solution)/shard_map/ppermute | solution.py:556
  101.8 31.6 %collective-permute-start.14 = (bf16[320,1280]{1,0:T(8,128)(2,1)S(1)}, bf16[320,1280]{1,0:T(8,128)(2,1)S(1)}, u32[]{:S(2)}, u32[]{:S(2)}) collective-permute-start(bf16[320,1280]{1,0:T(8,128)(2,1)S(1)} %slice.32), channel_id=1, source_target_pairs={{0,16},{8,24},{16,0},{24,8},{1,17},{9,25},{17,1},{25,9},{2,18},{10... | collective-permute-start | bytes 2457608 | tf_op jit(solution)/shard_map/ppermute | solution.py:561
  102.6 31.6 %collective-permute-start.13 = (bf16[320,1280]{1,0:T(8,128)(2,1)S(1)}, bf16[320,1280]{1,0:T(8,128)(2,1)S(1)}, u32[]{:S(2)}, u32[]{:S(2)}) collective-permute-start(bf16[320,1280]{1,0:T(8,128)(2,1)S(1)} %slice.31), channel_id=1, source_target_pairs={{0,8},{8,0},{16,24},{24,16},{1,9},{9,1},{17,25},{25,17},{2,10},{10... | collective-permute-start | bytes 2457608 | tf_op jit(solution)/shard_map/ppermute | solution.py:561
  135.2 36.4 %collective-permute-start.18 = (bf16[640,1280]{1,0:T(8,128)(2,1)}, bf16[640,1280]{1,0:T(8,128)(2,1)S(1)}, u32[]{:S(2)}, u32[]{:S(2)}) collective-permute-start(bf16[640,1280]{1,0:T(8,128)(2,1)} %collective-permute-done.15.refs_0_), channel_id=1, source_target_pairs={{0,16},{8,24},{16,0},{24,8},{1,17},{9,25},{17,1},{25,9},{2,18},{10... | collective-permute-start | bytes 4915208 | tf_op jit(solution)/shard_map/ppermute | solution.py:561
  136.0 36.2 %collective-permute-start.17 = (bf16[640,1280]{1,0:T(8,128)(2,1)}, bf16[640,1280]{1,0:T(8,128)(2,1)}, u32[]{:S(2)}, u32[]{:S(2)}) collective-permute-start(bf16[640,1280]{1,0:T(8,128)(2,1)} %collective-permute-done.15.refs_0_), channel_id=1, source_target_pairs={{0,8},{8,0},{16,24},{24,16},{1,9},{9,1},{17,25},{25,17},{2,10},{10... | collective-permute-start | bytes 4915208 | tf_op jit(solution)/shard_map/ppermute | solution.py:561
  136.3 35.9 %collective-permute-start.16 = (bf16[640,1280]{1,0:T(8,128)(2,1)}, bf16[640,1280]{1,0:T(8,128)(2,1)S(1)}, u32[]{:S(2)}, u32[]{:S(2)}) collective-permute-start(bf16[640,1280]{1,0:T(8,128)(2,1)} %collective-permute-done.15.refs_0_), channel_id=1, source_target_pairs={{0,2},{2,4},{4,6},{6,0},{1,3},{3,5},{5,7},{7,1},{8,10},{10,12},{12... | collective-permute-start | bytes 4915208 | tf_op jit(solution)/shard_map/ppermute | solution.py:556
  172.2 40.5 %collective-permute-start.23 = (bf16[384,2560]{1,0:T(8,128)(2,1)}, bf16[384,2560]{1,0:T(8,128)(2,1)}, u32[]{:S(2)}, u32[]{:S(2)}) collective-permute-start(bf16[384,2560]{1,0:T(8,128)(2,1)} %bitcast.15.own_hidden.refs_4_.refs_8_), channel_id=1, source_target_pairs={{0,1},{1,0},{2,3},{3,2},{4,5},{5,4},{6,7},{7,6},{8,9},{9,8},{10,11... | collective-permute-start | bytes 5898248 | tf_op jit(solution)/shard_map/ppermute | solution.py:561
  174.8 37.5 %collective-permute-start.22 = (bf16[640,1280]{1,0:T(8,128)(2,1)S(1)}, bf16[640,1280]{1,0:T(8,128)(2,1)}, u32[]{:S(2)}, u32[]{:S(2)}) collective-permute-start(bf16[640,1280]{1,0:T(8,128)(2,1)S(1)} %collective-permute-done.16.refs_3_), channel_id=1, source_target_pairs={{0,16},{8,24},{16,0},{24,8},{1,17},{9,25},{17,1},{25,9},{2,18},{10... | collective-permute-start | bytes 4915208 | tf_op jit(solution)/shard_map/ppermute | solution.py:561
  175.4 37.2 %collective-permute-start.21 = (bf16[640,1280]{1,0:T(8,128)(2,1)S(1)}, bf16[640,1280]{1,0:T(8,128)(2,1)}, u32[]{:S(2)}, u32[]{:S(2)}) collective-permute-start(bf16[640,1280]{1,0:T(8,128)(2,1)S(1)} %collective-permute-done.16.refs_3_), channel_id=1, source_target_pairs={{0,8},{8,0},{16,24},{24,16},{1,9},{9,1},{17,25},{25,17},{2,10},{10... | collective-permute-start | bytes 4915208 | tf_op jit(solution)/shard_map/ppermute | solution.py:561
  179.2 35.5 %collective-permute-start.19 = (bf16[2,192,1920]{2,1,0:T(8,128)(2,1)}, bf16[2,192,1920]{2,1,0:T(8,128)(2,1)S(1)}, u32[]{:S(2)}, u32[]{:S(2)}) collective-permute-start(bf16[2,192,1920]{2,1,0:T(8,128)(2,1)} %copy-done.20), channel_id=1, source_target_pairs={{0,2},{2,4},{4,6},{1,3},{3,5},{5,7},{8,10},{10,12},{12,14},{9,11},... | collective-permute-start | bytes 4423688 | tf_op jit(solution)/shard_map/ppermute | solution.py:551
  183.2 35.2 %collective-permute-start.20 = (bf16[2,192,1920]{2,1,0:T(8,128)(2,1)}, bf16[2,192,1920]{2,1,0:T(8,128)(2,1)S(1)}, u32[]{:S(2)}, u32[]{:S(2)}) collective-permute-start(bf16[2,192,1920]{2,1,0:T(8,128)(2,1)} %copy-done.19), channel_id=1, source_target_pairs={{2,0},{4,2},{6,4},{3,1},{5,3},{7,5},{10,8},{12,10},{14,12},{11,9},... | collective-permute-start | bytes 4423688 | tf_op jit(solution)/shard_map/ppermute | solution.py:551
  212.6 50.3 %collective-permute-start.24 = (bf16[640,1280]{1,0:T(8,128)(2,1)}, bf16[640,1280]{1,0:T(8,128)(2,1)}, u32[]{:S(2)}, u32[]{:S(2)}) collective-permute-start(bf16[640,1280]{1,0:T(8,128)(2,1)} %collective-permute-done.17.refs_1_), channel_id=1, source_target_pairs={{0,16},{8,24},{16,0},{24,8},{1,17},{9,25},{17,1},{25,9},{2,18},{10... | collective-permute-start | bytes 4915208 | tf_op jit(solution)/shard_map/ppermute | solution.py:561
  213.5 49.4 %collective-permute-start.25 = (bf16[640,1280]{1,0:T(8,128)(2,1)}, bf16[640,1280]{1,0:T(8,128)(2,1)}, u32[]{:S(2)}, u32[]{:S(2)}) collective-permute-start(bf16[640,1280]{1,0:T(8,128)(2,1)} %collective-permute-done.22.refs_5_), channel_id=1, source_target_pairs={{0,8},{8,0},{16,24},{24,16},{1,9},{9,1},{17,25},{25,17},{2,10},{10... | collective-permute-start | bytes 4915208 | tf_op jit(solution)/shard_map/ppermute | solution.py:561
  239.4 13.6 %collective-permute-start.28 = (bf16[1,384,1280]{2,1,0:T(8,128)(2,1)S(1)}, bf16[1,384,1280]{2,1,0:T(8,128)(2,1)}, u32[]{:S(2)}, u32[]{:S(2)}) collective-permute-start(bf16[1,384,1280]{2,1,0:T(8,128)(2,1)S(1)} %get-tuple-element.134.own_part), channel_id=1, source_target_pairs={{0,1},{1,0},{2,3},{3,2},{4,5},{5,4},{6,7},{7,6},{8,9},{9,8},{10,11... | collective-permute-start | bytes 2949128 | tf_op jit(solution)/shard_map/ppermute | solution.py:561
  241.1 17.1 %collective-permute-start.26 = (bf16[1,384,1280]{2,1,0:T(8,128)(2,1)}, bf16[1,384,1280]{2,1,0:T(8,128)(2,1)}, u32[]{:S(2)}, u32[]{:S(2)}) collective-permute-start(bf16[1,384,1280]{2,1,0:T(8,128)(2,1)} %get-tuple-element.131.own_part), channel_id=1, source_target_pairs={{0,1},{1,0},{2,3},{3,2},{4,5},{5,4},{6,7},{7,6},{8,9},{9,8},{10,11... | collective-permute-start | bytes 2949128 | tf_op jit(solution)/shard_map/ppermute | solution.py:561
  241.8 11.2 %collective-permute-start.27 = (f32[1,2560]{1,0:T(1,128)S(1)}, f32[1,2560]{1,0:T(1,128)S(1)}, u32[]{:S(2)}, u32[]{:S(2)}) collective-permute-start(f32[1,2560]{1,0:T(1,128)S(1)} %get-tuple-element.133.own_gate.refs_6_.refs_10_), channel_id=1, source_target_pairs={{0,1},{1,0},{2,3},{3,2},{4,5},{5,4},{6,7},{7,6},{8,9},{9,8},{10,11... | collective-permute-start | bytes 30728 | tf_op jit(solution)/shard_map/ppermute | solution.py:561
  268.4 4.1 %collective-permute-start.30 = (bf16[1,384,1280]{2,1,0:T(8,128)(2,1)}, bf16[1,384,1280]{2,1,0:T(8,128)(2,1)S(1)}, u32[]{:S(2)}, u32[]{:S(2)}) collective-permute-start(bf16[1,384,1280]{2,1,0:T(8,128)(2,1)} %get-tuple-element.144.refs_1_), channel_id=1, source_target_pairs={{0,1},{1,0},{2,3},{3,2},{4,5},{5,4},{6,7},{7,6},{8,9},{9,8},{10,11... | collective-permute-start | bytes 2949128 | tf_op jit(solution)/shard_map/ppermute | solution.py:561
  (34 other events, 402.0 us)

commit v2 on v1

--- a/solution.py
+++ b/solution.py
@@ -15,9 +15,9 @@
 LEVEL_STEP = 32
 
 EPSILON = 1e-06
-VMEM_LIMIT = 32 * 1024 * 1024
-MOST_VMEM = 56 * 1024 * 1024
+VMEM_LIMIT = 24 * 1024 * 1024
 SMALL = pl.CostEstimate(flops=1, bytes_accessed=1, transcendentals=0)
+LARGE = pl.CostEstimate(flops=20_000_000_000, bytes_accessed=1, transcendentals=0)
 
 
 def kernel_params(limit=VMEM_LIMIT):
@@ -268,7 +268,7 @@
         out_shape=[jax.ShapeDtypeStruct((frames, tokens, (group + 1) * HD), jnp.bfloat16)]
         * q_count,
         compiler_params=kernel_params(),
-        cost_estimate=SMALL,
+        cost_estimate=SMALL if visiting else LARGE,
         name="attend_visitors" if visiting else "attend_own",
     )(vector, *query_blocks, keys_values, *halos)
 
@@ -414,135 +414,149 @@
     )(place, attended, *arrays, *([] if carry is None else carry))
 
 
-def mix_kernel(
-    place, own_part, other_part, own_hidden, other_hidden, own_gate, other_gate, *refs
-):
-    mixed_ref, sums_ref = refs[-2:]
-    step = pl.program_id(0)
-    mine = place[3 * step] != 0
-    hidden = jnp.where(
-        mine, own_hidden[...].astype(jnp.float32), other_hidden[...].astype(jnp.float32)
-    )
-    gate = jnp.where(mine, own_gate[...], other_gate[...])
-    mixed = hidden + gate * (
-        own_part[0].astype(jnp.float32) + other_part[0].astype(jnp.float32)
-    )
-    mixed_ref[...] = mixed
-    lane = lax.broadcasted_iota(jnp.int32, sums_ref.shape, 1)
-    first = jnp.sum(mixed, axis=1, keepdims=True)
-    second = jnp.sum(mixed * mixed, axis=1, keepdims=True)
-    sums = jnp.where(lane == 0, first, jnp.where(lane == 1, second, 0.0))
-
-    @pl.when(step == 0)
+def pick_kernel(place, own_hidden, other_hidden, own_gate, other_gate, hidden, gate):
+    mine = place[2 * pl.program_id(0)] != 0
+
+    @pl.when(mine)
     def _():
-        sums_ref[...] = sums + refs[0][...] if len(refs) == 4 else sums
-
-    @pl.when(step != 0)
+        hidden[0] = own_hidden[...]
+        gate[0] = own_gate[...]
+
+    @pl.when(jnp.logical_not(mine))
     def _():
-        sums_ref[...] = sums_ref[...] + sums
-
-
-def mix(place, own_part, other_part, own_hidden, other_hidden, own_gate, other_gate, carry):
-    count, tokens, width = own_part.shape
-    blocks = own_hidden.shape[1] // width
-    part = pl.BlockSpec((1, tokens, width), lambda i, place: (i, 0, 0))
-    hidden = pl.BlockSpec((tokens, width), lambda i, place: (0, place[3 * i + 1]))
-    gate = pl.BlockSpec((1, width), lambda i, place: (0, place[3 * i + 1]))
-    sums = pl.BlockSpec((tokens, LANES), lambda i, place: (0, 0))
-    mixed = pl.BlockSpec((tokens, width), lambda i, place: (0, place[3 * i + 2]))
+        hidden[0] = other_hidden[...]
+        gate[0] = other_gate[...]
+
+
+def pick(place, own_hidden, other_hidden, own_gate, other_gate, width):
+    tokens, features = own_hidden.shape
+    count = 2 * features // width
+    hidden = pl.BlockSpec((tokens, width), lambda i, place: (0, place[2 * i + 1]))
+    gate = pl.BlockSpec((1, width), lambda i, place: (0, place[2 * i + 1]))
     return pl.pallas_call(
-        mix_kernel,
+        pick_kernel,
         grid_spec=pltpu.PrefetchScalarGridSpec(
             num_scalar_prefetch=1,
             grid=(count,),
-            in_specs=[part, part, hidden, hidden, gate, gate]
-            + ([sums, pl.BlockSpec(memory_space=pl.ANY)] if carry else []),
-            out_specs=[mixed, sums],
+            in_specs=[hidden, hidden, gate, gate],
+            out_specs=[
+                pl.BlockSpec((1, tokens, width), lambda i, place: (i, 0, 0)),
+                pl.BlockSpec((1, 1, width), lambda i, place: (i, 0, 0)),
+            ],
         ),
         out_shape=[
-            jax.ShapeDtypeStruct((tokens, (blocks + 1) * width), jnp.float32),
+            jax.ShapeDtypeStruct((count, tokens, width), jnp.bfloat16),
+            jax.ShapeDtypeStruct((count, 1, width), jnp.float32),
+        ],
+        compiler_params=kernel_params(),
+        cost_estimate=SMALL,
+        name="pick",
+    )(place, own_hidden, other_hidden, own_gate, other_gate)
+
+
+def mixed_blocks(hidden, gate, first, own_parts, other_parts):
+    return [
+        hidden[index].astype(jnp.float32)
+        + gate[first + index]
+        * (own_part[0].astype(jnp.float32) + other_part[0].astype(jnp.float32))
+        for index, (own_part, other_part) in enumerate(zip(own_parts, other_parts))
+    ]
+
+
+def mix_kernel(hidden, gate, *refs, count):
+    own_parts, other_parts, (mixed_ref, sums_ref) = (
+        refs[:count],
+        refs[count : 2 * count],
+        refs[2 * count :],
+    )
+    first = second = 0.0
+    for index, mixed in enumerate(mixed_blocks(hidden, gate, 0, own_parts, other_parts)):
+        mixed_ref[index] = mixed.astype(jnp.bfloat16)
+        first = first + jnp.sum(mixed, axis=1, keepdims=True)
+        second = second + jnp.sum(mixed * mixed, axis=1, keepdims=True)
+    lane = lax.broadcasted_iota(jnp.int32, sums_ref.shape, 1)
+    sums_ref[...] = jnp.where(lane == 0, first, jnp.where(lane == 1, second, 0.0))
+
+
+def mix(hidden, gate, own_parts, other_parts):
+    count = len(own_parts)
+    _, tokens, width = hidden.shape
+    rows = 64 if tokens % 64 == 0 else tokens
+    part = pl.BlockSpec((1, rows, width), lambda i: (0, i, 0))
+    several = pl.BlockSpec((count, rows, width), lambda i: (0, i, 0))
+    return pl.pallas_call(
+        partial(mix_kernel, count=count),
+        grid=(tokens // rows,),
+        in_specs=[several, pl.BlockSpec(gate.shape, lambda i: (0, 0, 0))] + [part] * (2 * count),
+        out_specs=[several, pl.BlockSpec((rows, LANES), lambda i: (i, 0))],
+        out_shape=[
+            jax.ShapeDtypeStruct((count, tokens, width), jnp.bfloat16),
             jax.ShapeDtypeStruct((tokens, LANES), jnp.float32),
         ],
-        input_output_aliases={8: 0} if carry else {},
-        compiler_params=kernel_params(MOST_VMEM),
+        compiler_params=kernel_params(),
         cost_estimate=SMALL,
         name="mix",
-    )(
-        *(place, own_part, other_part, own_hidden, other_hidden, own_gate, other_gate),
-        *((carry[1], carry[0]) if carry else ()),
-    )
-
-
-def finish_kernel(place, *refs, count):
-    own_part, other_part, refs = refs[:count], refs[count : 2 * count], refs[2 * count :]
-    width = own_part[0].shape[2]
-    sides, refs = refs[: 4 * count], refs[4 * count :]
-    scale, shift_by, sums, mixed_ref, residual, ffn = refs
-    blocks = residual.shape[1] // width
+    )(hidden, gate, *own_parts, *other_parts)
+
+
+def finish_kernel(place, hidden, gate, scale, shift_by, sums, *refs, count, blocks):
+    early, refs = refs[:blocks], refs[blocks:]
+    own_parts, other_parts, (residual, ffn) = (
+        refs[:count],
+        refs[count : 2 * count],
+        refs[2 * count :],
+    )
+    width = hidden.shape[2]
+    others = gate.shape[0] - count
+    late = mixed_blocks(hidden, gate, others, own_parts, other_parts)
     first = sums[:, 0:1]
     second = sums[:, 1:2]
-    late = []
-    for index in range(count):
-        own_hidden, other_hidden, own_gate, other_gate = sides[4 * index : 4 * index + 4]
-        mine = place[3 * index] != 0
-        hidden = jnp.where(
-            mine, own_hidden[...].astype(jnp.float32), other_hidden[...].astype(jnp.float32)
-        )
-        gate = jnp.where(mine, own_gate[...], other_gate[...])
-        mixed = hidden + gate * (
-            own_part[index][0].astype(jnp.float32) + other_part[index][0].astype(jnp.float32)
-        )
+    for mixed in late:
         first = first + jnp.sum(mixed, axis=1, keepdims=True)
         second = second + jnp.sum(mixed * mixed, axis=1, keepdims=True)
-        late.append(mixed)
     average = first / D
     variance = second / D - average * average
     inverse = lax.rsqrt(variance + EPSILON)
     for block in range(blocks):
         columns = slice(block * width, (block + 1) * width)
-        mixed = mixed_ref[:, columns]
+        mixed = early[block][0].astype(jnp.float32)
         for index in range(count):
-            here = (place[3 * index] != 0) & (place[3 * index + 1] == block)
-            mixed = jnp.where(here, late[index], mixed)
+            mixed = jnp.where(place[2 * block] == others + index, late[index], mixed)
         residual[:, columns] = mixed.astype(jnp.bfloat16)
         ffn[:, columns] = (
             (mixed - average) * inverse * (1.0 + scale[:, columns]) + shift_by[:, columns]
         ).astype(jnp.bfloat16)
 
 
-def finish(place, own_part, other_part, own_hidden, other_hidden, own_gate, other_gate, scale, shift_by, carry):
-    count = len(own_part)
-    _, tokens, width = own_part[0].shape
-    features = own_hidden.shape[1]
+def finish(place, hidden, gate, scale, shift_by, sums, early, own_parts, other_parts):
+    count = len(own_parts)
+    _, tokens, width = hidden.shape
+    blocks = place.shape[0] // 2
     rows = 64 if tokens % 64 == 0 else tokens
     part = pl.BlockSpec((1, rows, width), lambda i, place: (0, i, 0))
-    whole = pl.BlockSpec((1, features), lambda i, place: (0, 0))
-    sums = pl.BlockSpec((rows, LANES), lambda i, place: (i, 0))
-    row = pl.BlockSpec((rows, features), lambda i, place: (i, 0))
-    side_specs = []
-    for index in range(count):
-        hidden = pl.BlockSpec(
-            (rows, width), lambda i, place, index=index: (i, place[3 * index + 1])
-        )
-        gate = pl.BlockSpec((1, width), lambda i, place, index=index: (0, place[3 * index + 1]))
-        side_specs += [hidden, hidden, gate, gate]
+    several = pl.BlockSpec((count, rows, width), lambda i, place: (1, i, 0))
+    whole = pl.BlockSpec((1, blocks * width), lambda i, place: (0, 0))
+    row = pl.BlockSpec((rows, blocks * width), lambda i, place: (i, 0))
+    earlier = [
+        pl.BlockSpec((1, rows, width), lambda i, place, block=block: (place[2 * block + 1], i, 0))
+        for block in range(blocks)
+    ]
     return pl.pallas_call(
-        partial(finish_kernel, count=count),
+        partial(finish_kernel, count=count, blocks=blocks),
         grid_spec=pltpu.PrefetchScalarGridSpec(
             num_scalar_prefetch=1,
             grid=(tokens // rows,),
-            in_specs=[part] * (2 * count) + [*side_specs, whole, whole, sums, row],
+            in_specs=[several, pl.BlockSpec(gate.shape, lambda i, place: (0, 0, 0)), whole, whole]
+            + [pl.BlockSpec((rows, LANES), lambda i, place: (i, 0))]
+            + earlier
+            + [part] * (2 * count),
             out_specs=[row, row],
         ),
-        out_shape=[jax.ShapeDtypeStruct((tokens, features), jnp.bfloat16)] * 2,
-        compiler_params=kernel_params(MOST_VMEM),
+        out_shape=[jax.ShapeDtypeStruct((tokens, blocks * width), jnp.bfloat16)] * 2,
+        compiler_params=kernel_params(),
         cost_estimate=SMALL,
         name="finish",
-    )(
-        place, *own_part, *other_part,
-        *((own_hidden, other_hidden, own_gate, other_gate) * count),
-        scale, shift_by, carry[1], carry[0],
-    )
+    )(place, hidden, gate, scale, shift_by, sums, *[early] * blocks, *own_parts, *other_parts)
 
 
 def shift(block, axis, step):
@@ -653,37 +667,44 @@
     first_far_x = swap(first_y[:cut], "ha", 1)
     first_far_y = swap(first_x[cut:], "ha", 2)
 
-    first_far_x, first_far_y, second, from_left, from_right = together(
-        first_far_x, first_far_y, second, from_left, from_right
+    first_far_x, first_far_y, second, from_left, from_right, gate = together(
+        first_far_x, first_far_y, second, from_left, from_right, picked[0:1]
     )
     third = turn(second, "wa", 1)
     second_x = swap(second, "ha", 1)
     second_y = swap(second, "ha", 2)
+    other_gate = swap(gate, "ta", 1)
     for_left, for_right = tokens.visit(vector, (from_left, from_right), halos)
 
     for_left, for_right, first_far_x = together(for_left, for_right, first_far_x)
     left = shift(for_right, "wa", 1)
     right = shift(for_left, "wa", -1)
 
-    third, second_x, second_y, first_far_x, hidden, gate, vector = together(
-        third, second_x, second_y, first_far_x, hidden, picked[0:1], vector
+    third, second_x, second_y, first_far_x, other_gate, hidden, vector = together(
+        third, second_x, second_y, first_far_x, other_gate, hidden, vector
     )
     third_x = swap(third, "ha", 1)
     third_y = swap(third, "ha", 2)
     other_hidden = swap(hidden, "ta", 1)
     rest_sides = tokens.rest_sides(vector, halos)
 
-    third_x, third_y, second_x, other_hidden = together(third_x, third_y, second_x, other_hidden)
+    def block_of(distance):
+        return lax.rem(wa - distance + n_wa, n_wa)
+
+    owners = jnp.stack([block_of(distance) // blocks == ta for distance in range(n_wa)])
+    inner = jnp.stack([lax.rem(block_of(distance), blocks) for distance in range(n_wa)])
+    place = jnp.stack([owners.astype(jnp.int32), inner], axis=1).reshape(-1)
+    base, gates = pick(place, hidden, other_hidden, gate, other_gate, width)
+    left, right, base, gates = together(left, right, base, gates)
+    attended = tokens.combine(vector, near, [left, right, *rest_sides])
+
+    third_x, third_y, second_x, attended = together(third_x, third_y, second_x, attended)
     third_far = swap(third_y, "ha", 1)
     second_far = swap(second_x, "ha", 2)
 
-    left, right, third_x, gate = together(left, right, third_x, gate)
-    other_gate = swap(gate, "ta", 1)
-    attended = tokens.combine(vector, near, [left, right, *rest_sides])
-
-    place = ha.reshape(1)
+    turned = ha.reshape(1)
     sums = project(
-        place,
+        turned,
         attended,
         [out_weight, first, first_x, first_y, first_far_x, first_far_y],
         [
@@ -697,7 +718,7 @@
     )
     other_sums = [swap(part, "ta", 1) for part in sums]
     late = project(
-        place,
+        turned,
         attended,
         [second, second_x, second_y, third, third_x, third_y],
         [[(start + number, depth, 0, False) for number in range(3)] for start in (0, 3)],
@@ -705,22 +726,13 @@
         0,
         jnp.float32,
     )
-
-    def placed(distance):
-        block = lax.rem(wa - distance + n_wa, n_wa)
-        mine = block // blocks == ta
-        inner = lax.rem(block, blocks)
-        return jnp.stack([mine.astype(jnp.int32), inner, jnp.where(mine, inner, blocks)])
-
-    sides = hidden, other_hidden, gate, other_gate
-    carry = None
-    for distance in range(2):
-        carry = mix(placed(distance), sums[distance], other_sums[distance], *sides, carry)
-
-    second_far, third_far, *rest = together(second_far, third_far, *late, *carry)
-    late, carry = rest[:2], rest[2:]
+    early, totals = mix(base, gates, sums, other_sums)
+
+    second_far, third_far, early, totals, *late = together(
+        second_far, third_far, early, totals, *late
+    )
     late = project(
-        place,
+        turned,
         attended,
         [second_far, third_far],
         [[(0, depth, 0, False)], [(1, depth, 0, False)]],
@@ -729,8 +741,11 @@
         jnp.bfloat16,
     )
     other_late = [swap(part, "ta", 1) for part in late]
-    places = jnp.concatenate([placed(2), placed(3)])
-    return finish(places, late, other_late, *sides, picked[2:3], picked[1:2], carry)
+    mine = [lax.rem(wa - ta * blocks - block + 2 * n_wa, n_wa) for block in range(blocks)]
+    place = jnp.stack([value for slot in mine for value in (slot, jnp.minimum(slot, 1))])
+    return finish(
+        place, base, gates, picked[2:3], picked[1:2], totals, early, late, other_late
+    )
 
 
 def gathered(hidden, queries, keys_values, windows, out_weight, picked):

time: 285 us -> 317 us (1.11)
  Pallas kernels: 98.9 us -> 147 us
  waiting for transfers between devices: 114 us -> 99.4 us
  local copies, waits for them, and re-layouts: 27.3 us -> 19.1 us
  starting transfers between devices: 33.3 us -> 39 us
    pallas_call x2, Pallas kernels: 4.12 us -> 59.2 us  [pack(): pl.pallas_call(partial(pack_kernel, head_of=head_of, first=first, rows=ro...]
    ppermute x3, waiting for transfers between devices: 30.5 us -> 1.26 us  [turn(): lax.ppermute(block, axis, [(i, (i + step) % count) for i in range(count)])]
    unnamed x66 -> x46, local copies, waits for them, and re-layouts: 18.7 us -> 5.14 us
    ppermute x16, waiting for transfers between devices: 33.9 us -> 46.7 us  [swap(): return lax.ppermute(block, axis, [(i, i ^ bit) for i in range(count)])]
    ppermute x16, starting transfers between devices: 12.8 us -> 21.4 us  [swap(): return lax.ppermute(block, axis, [(i, i ^ bit) for i in range(count)])]
    pallas_call x3, Pallas kernels: 18.8 us -> 13.8 us  [the longest x1 7.1 us: finish(): pl.pallas_call(partial(finish_kernel, count=count, blocks=blocks), grid_s...]
  transfers between devices with their start and end apart: 25 -> 25, of which waited for: 11 -> 13; matrix products, arithmetic and copies ran while one was open for 3% -> 4% of each run, Pallas kernels for 30% -> 43%
where the time goes in v2:
time: 317 us; the launch traced here: 313 us
  Pallas kernels  147 us (46%)
  waiting for transfers between devices  99.4 us (31%)
  starting transfers between devices  39 us (12%)
  local copies, waits for them, and re-layouts  19.1 us (6%)
  blocking collectives  3.92 us (1%)
    pallas_call x2, Pallas kernels, pack(): pl.pallas_call(partial(pack_kernel, head_of=head_of, first=first, rows=ro...  59.2 us
    ppermute x6, waiting for transfers between devices, shift(): return lax.ppermute(block, axis, pairs)  51.5 us
    ppermute x16, waiting for transfers between devices, swap(): return lax.ppermute(block, axis, [(i, i ^ bit) for i in range(count)])  46.7 us
    pallas_call x2, Pallas kernels, attention(): pl.pallas_call(partial(attention_kernel, plan=plan, head_of=head_of, q_co...  46.4 us
    ppermute x16, starting transfers between devices, swap(): return lax.ppermute(block, axis, [(i, i ^ bit) for i in range(count)])  21.4 us
    pallas_call x3, Pallas kernels, project(): pl.pallas_call(partial(project_kernel, slots=slots, carried=carry is not...  20 us
    ppermute x6, starting transfers between devices, shift(): return lax.ppermute(block, axis, pairs)  16.1 us
    pallas_call x1, Pallas kernels, combine(): pl.pallas_call(partial(combine_kernel, plan=plan, heads=heads), grid_spec...  7.89 us
  transfers between devices with their start and end apart: 25, of which 13 were waited for; matrix products, arithmetic and copies ran while one was open for 4% of the time, Pallas kernels for 43%

profile of v2, /device:TPU:17, one launch (start us, length us, event | category | flops | bytes accessed | tf_op | source)
XLA Modules:
  0.0 313.1 jit_solution(8787562713106611717)
XLA Ops:
  0.6 2.7 constant_dynamic-slice_fusion
  6.2 57.5 %pack.6 = (bf16[2,2,64,1792]{3,2,1,0:T(8,128)(2,1)}, bf16[2,2,64,1792]{3,2,1,0:T(8,128)(2,1)}) custom-call(s32[125]{0:T(128)S(1)} %concatenate.10.vector, bf16[2,2,192,2560]{3,2,1,0:T(8,128)(2,1)} %bitcast.46), custom_call_target="tpu_custom_call" | custom-call | flops 1 | bytes 1 | tf_op jit(solution)/shard_map/pack/pallas_call | solution.py:96
  63.7 4.1 %collective-permute-start.7 = (bf16[2,2,64,1792]{3,2,1,0:T(8,128)(2,1)}, bf16[2,2,64,1792]{3,2,1,0:T(8,128)(2,1)}, u32[]{:S(2)}, u32[]{:S(2)}) collective-permute-start(bf16[2,2,64,1792]{3,2,1,0:T(8,128)(2,1)} %get-tuple-element.92), channel_id=1, source_target_pairs={{0,8},{8,16},{16,24},{1,9},{9,17},{17,25},{2,10},{10,18},{18,26},{... | collective-permute-start | bytes 2752520 | tf_op jit(solution)/shard_map/ppermute | solution.py:565
  72.8 3.4 %collective-permute-start.12 = (bf16[2,192,1792]{2,1,0:T(8,128)(2,1)}, bf16[2,192,1792]{2,1,0:T(8,128)(2,1)}, u32[]{:S(2)}, u32[]{:S(2)}) collective-permute-start(bf16[2,192,1792]{2,1,0:T(8,128)(2,1)} %pack.7), channel_id=1, source_target_pairs={{2,0},{4,2},{6,4},{3,1},{5,3},{7,5},{10,8},{12,10},{14,12},{11,9},... | collective-permute-start | bytes 4128776 | tf_op jit(solution)/shard_map/ppermute | solution.py:565
  76.2 3.9 %pmax.7 = f32[2]{0:T(128)S(1)} all-reduce(f32[2]{0:T(128)S(1)} %subtract_reduce_fusion), channel_id=1, replica_groups=mesh['ha'=4,'wa'=4,'ta'=2] {'ta'}, use_global_device_ids=true, to_apply=%region_3.4 | all-reduce | flops 2 | bytes 16 | tf_op jit(solution)/shard_map/pmax | solution.py:48
  81.4 4.4 %collective-permute-done.7.refs_2_.refs_3_ = bf16[2,2,64,1792]{3,2,1,0:T(8,128)(2,1)} collective-permute-done((bf16[2,2,64,1792]{3,2,1,0:T(8,128)(2,1)}, bf16[2,2,64,1792]{3,2,1,0:T(8,128)(2,1)}, u32[]{:S(2)}, u32[]{:S(2)}) %collective-permute-start.7) | collective-permute-done | bytes 917536 | tf_op jit(solution)/shard_map/ppermute | solution.py:565
  85.8 21.6 %collective-permute-done.8.refs_3_.refs_4_ = bf16[2,2,64,1792]{3,2,1,0:T(8,128)(2,1)} collective-permute-done((bf16[2,2,64,1792]{3,2,1,0:T(8,128)(2,1)}, bf16[2,2,64,1792]{3,2,1,0:T(8,128)(2,1)}, u32[]{:S(2)}, u32[]{:S(2)}) %collective-permute-start.8) | collective-permute-done | bytes 917536 | tf_op jit(solution)/shard_map/ppermute | solution.py:565
  110.3 22.5 %attend_own.1.own.own_stat = bf16[2,192,2688]{2,1,0:T(8,128)(2,1)S(1)} custom-call(s32[125]{0:T(128)S(1)} %concatenate.10.vector, bf16[2,192,2560]{2,1,0:T(8,128)(2,1)} %bitcast.51, bf16[2,2,192,2560]{3,2,1,0:T(8,128)(2,1)} %bitcast.48, bf16[2,2,64,1792]{3,2,1,0:T(8,128)(2,1)} %collective-permute-done.7.refs_2_.refs_3_, ...), custom_call_target="tpu_custom_call" | custom-call | flops 20000000000 | bytes 1 | tf_op jit(solution)/shard_map/attend_own/pallas_call | solution.py:251
  132.8 10.4 %collective-permute-done.10.refs_3_ = bf16[640,1280]{1,0:T(8,128)(2,1)} collective-permute-done((bf16[640,1280]{1,0:T(8,128)(2,1)}, bf16[640,1280]{1,0:T(8,128)(2,1)}, u32[]{:S(2)}, u32[]{:S(2)}) %collective-permute-start.10) | collective-permute-done | bytes 1638432 | tf_op jit(solution)/shard_map/ppermute | solution.py:575
  144.7 2.7 slice.31
  153.0 11.8 %collective-permute-done.13.refs_4_ = bf16[320,1280]{1,0:T(8,128)(2,1)} collective-permute-done((bf16[320,1280]{1,0:T(8,128)(2,1)}, bf16[320,1280]{1,0:T(8,128)(2,1)}, u32[]{:S(2)}, u32[]{:S(2)}) %collective-permute-start.13) | collective-permute-done | bytes 819232 | tf_op jit(solution)/shard_map/ppermute | solution.py:575
  168.0 4.9 %collective-permute-start.21 = (f32[1,2560]{1,0:T(1,128)S(1)}, f32[1,2560]{1,0:T(1,128)S(1)}, u32[]{:S(2)}, u32[]{:S(2)}) collective-permute-start(f32[1,2560]{1,0:T(1,128)S(1)} %get-tuple-element.113.own_gate), channel_id=1, source_target_pairs={{0,1},{1,0},{2,3},{3,2},{4,5},{5,4},{6,7},{7,6},{8,9},{9,8},{10,11... | collective-permute-start | bytes 30728 | tf_op jit(solution)/shard_map/ppermute | solution.py:575
  172.9 23.9 %attend_visitors.3 = (bf16[2,192,1920]{2,1,0:T(8,128)(2,1)S(1)}, bf16[2,192,1920]{2,1,0:T(8,128)(2,1)S(1)}) custom-call(s32[125]{0:T(128)S(1)} %concatenate.10.vector, bf16[2,192,1792]{2,1,0:T(8,128)(2,1)S(1)} %collective-permute-done.11.refs_0_, bf16[2,192,1792]{2,1,0:T(8,128)(2,1)} %collective-permute-done.12.refs_1_, bf16[2,2,192,2560]{3,2,1,0:T(8,128)(2,1)} %bitcast.49, ...), custom_call_target="tpu_custom_call" | custom-call | flops 1 | bytes 1 | tf_op jit(solution)/shard_map/attend_visitors/pallas_call | solution.py:251
  200.4 5.1 %collective-permute-start.22 = (bf16[384,2560]{1,0:T(8,128)(2,1)}, bf16[384,2560]{1,0:T(8,128)(2,1)}, u32[]{:S(2)}, u32[]{:S(2)}) collective-permute-start(bf16[384,2560]{1,0:T(8,128)(2,1)} %bitcast.24.own_hidden), channel_id=1, source_target_pairs={{0,1},{1,0},{2,3},{3,2},{4,5},{5,4},{6,7},{7,6},{8,9},{9,8},{10,11... | collective-permute-start | bytes 5898248 | tf_op jit(solution)/shard_map/ppermute | solution.py:575
  210.1 2.9 collective-permute-start.16
  218.0 4.7 %pick.1 = (bf16[4,384,1280]{2,1,0:T(8,128)(2,1)S(1)}, f32[4,1,1280]{2,1,0:T(1,128)S(1)}) custom-call(s32[8]{0:T(128)S(1)} %reshape.113.place, bf16[384,2560]{1,0:T(8,128)(2,1)} %bitcast.24.own_hidden, bf16[384,2560]{1,0:T(8,128)(2,1)} %collective-permute-done.22.other_hidden, f32[1,2560]{1,0:T(1,128)S(1)} %get-tuple-element.113.own_gate, ...), custom_call_target="tpu_custom_call" | custom-call | flops 1 | bytes 1 | tf_op jit(solution)/shard_map/pick/pallas_call | solution.py:436
  222.8 22.8 %collective-permute-done.16.left = bf16[2,192,1920]{2,1,0:T(8,128)(2,1)S(1)} collective-permute-done((bf16[2,192,1920]{2,1,0:T(8,128)(2,1)}, bf16[2,192,1920]{2,1,0:T(8,128)(2,1)S(1)}, u32[]{:S(2)}, u32[]{:S(2)}) %collective-permute-start.16) | collective-permute-done | bytes 1474592 | tf_op jit(solution)/shard_map/ppermute | solution.py:565
  248.3 7.9 %combine.1 = bf16[2,192,2560]{2,1,0:T(8,128)(2,1)S(1)} custom-call(s32[125]{0:T(128)} %copy-done.19, bf16[2,192,2688]{2,1,0:T(8,128)(2,1)S(1)} %attend_own.1.own.own_stat, bf16[2,192,2688]{2,1,0:T(8,128)(2,1)S(1)} %attend_own.1.own.own_stat, bf16[2,192,1920]{2,1,0:T(8,128)(2,1)S(1)} %collective-permute-done.16.left, ...), custom_call_target="tpu_custom_call" | custom-call | flops 1 | bytes 1 | tf_op jit(solution)/shard_map/combine/pallas_call | solution.py:328
  257.1 8.3 %project.3 = (bf16[1,384,1280]{2,1,0:T(8,128)(2,1)S(1)}, bf16[1,384,1280]{2,1,0:T(8,128)(2,1)S(1)}) custom-call(s32[1]{0:T(128)} %bitcast.9.place, bf16[384,2560]{1,0:T(8,128)(2,1)S(1)} %bitcast.41, bf16[2560,1280]{1,0:T(8,128)(2,1)S(1)} %bitcast.45, bf16[640,1280]{1,0:T(8,128)(2,1)} %collective-permute-done.6.refs_1_, bf16[640,1280]{1,0:T(8,128)(2,1)S(1)} %copy-done.3, ...), custom_call_target="tpu_custom_call" | custom-call | flops 1 | bytes 1 | tf_op jit(solution)/shard_map/project/pallas_call | solution.py:396
  266.9 7.1 %project.4 = (f32[1,384,1280]{2,1,0:T(8,128)S(1)}, f32[1,384,1280]{2,1,0:T(8,128)S(1)}) custom-call(s32[1]{0:T(128)} %bitcast.9.place, bf16[384,2560]{1,0:T(8,128)(2,1)S(1)} %bitcast.42, bf16[640,1280]{1,0:T(8,128)(2,1)} %collective-permute-done.15.refs_0_, bf16[640,1280]{1,0:T(8,128)(2,1)S(1)} %copy-done.5, bf16[640,1280]{1,0:T(8,128)(2,1)S(1)} %copy-done.7, ...), custom_call_target="tpu_custom_call" | custom-call | flops 1 | bytes 1 | tf_op jit(solution)/shard_map/project/pallas_call | solution.py:396
  276.1 16.8 %collective-permute-done.25.refs_0_ = bf16[640,1280]{1,0:T(8,128)(2,1)S(1)} collective-permute-done((bf16[640,1280]{1,0:T(8,128)(2,1)S(1)}, bf16[640,1280]{1,0:T(8,128)(2,1)S(1)}, u32[]{:S(2)}, u32[]{:S(2)}) %collective-permute-start.25) | collective-permute-done | bytes 1638432 | tf_op jit(solution)/shard_map/ppermute | solution.py:575
  293.3 4.6 %project.5 = (bf16[1,384,1280]{2,1,0:T(8,128)(2,1)S(1)}, bf16[1,384,1280]{2,1,0:T(8,128)(2,1)}) custom-call(s32[1]{0:T(128)} %bitcast.9.place, bf16[384,2560]{1,0:T(8,128)(2,1)S(1)} %bitcast.43, bf16[640,1280]{1,0:T(8,128)(2,1)S(1)} %collective-permute-done.25.refs_0_, bf16[640,1280]{1,0:T(8,128)(2,1)S(1)} %collective-permute-done.26.refs_1_, ...), custom_call_target="tpu_custom_call" | custom-call | flops 1 | bytes 1 | tf_op jit(solution)/shard_map/project/pallas_call | solution.py:396
  300.1 2.8 collective-permute-done.29.refs_4_
  306.0 7.1 %finish.1 = (bf16[384,2560]{1,0:T(8,128)(2,1)}, bf16[384,2560]{1,0:T(8,128)(2,1)}) custom-call(s32[4]{0:T(128)S(1)} %pad_add_fusion.1.place, bf16[4,384,1280]{2,1,0:T(8,128)(2,1)S(1)} %copy-done.1, f32[4,1,1280]{2,1,0:T(1,128)S(1)} %copy-done.9, f32[1,2560]{1,0:T(1,128)S(1)} %copy-done.11, f32[1,2560]{1,0:T(1,128)S(1)} %copy-done.10, ...), custom_call_target="tpu_custom_call" | custom-call | flops 1 | bytes 1 | tf_op jit(solution)/shard_map/finish/pallas_call | solution.py:544
  (113 shorter events, 49.5 us)
Async XLA Ops:
  3.4 104.1 %collective-permute-start.6 = (bf16[640,1280]{1,0:T(8,128)(2,1)}, bf16[640,1280]{1,0:T(8,128)(2,1)}, u32[]{:S(2)}, u32[]{:S(2)}) collective-permute-start(bf16[640,1280]{1,0:T(8,128)(2,1)} %constant_dynamic-slice_fusion), channel_id=1, source_target_pairs={{0,2},{2,4},{4,6},{6,0},{1,3},{3,5},{5,7},{7,1},{8,10},{10,12},{12... | collective-permute-start | bytes 4915208 | tf_op jit(solution)/shard_map/ppermute | solution.py:570
  63.7 22.1 %collective-permute-start.7 = (bf16[2,2,64,1792]{3,2,1,0:T(8,128)(2,1)}, bf16[2,2,64,1792]{3,2,1,0:T(8,128)(2,1)}, u32[]{:S(2)}, u32[]{:S(2)}) collective-permute-start(bf16[2,2,64,1792]{3,2,1,0:T(8,128)(2,1)} %get-tuple-element.92), channel_id=1, source_target_pairs={{0,8},{8,16},{16,24},{1,9},{9,17},{17,25},{2,10},{10,18},{18,26},{... | collective-permute-start | bytes 2752520 | tf_op jit(solution)/shard_map/ppermute | solution.py:565
  67.7 39.7 %collective-permute-start.8 = (bf16[2,2,64,1792]{3,2,1,0:T(8,128)(2,1)}, bf16[2,2,64,1792]{3,2,1,0:T(8,128)(2,1)}, u32[]{:S(2)}, u32[]{:S(2)}) collective-permute-start(bf16[2,2,64,1792]{3,2,1,0:T(8,128)(2,1)} %get-tuple-element.93), channel_id=1, source_target_pairs={{8,0},{16,8},{24,16},{9,1},{17,9},{25,17},{10,2},{18,10},{26,18},{... | collective-permute-start | bytes 2752520 | tf_op jit(solution)/shard_map/ppermute | solution.py:565
  70.8 62.0 %collective-permute-start.11 = (bf16[2,192,1792]{2,1,0:T(8,128)(2,1)}, bf16[2,192,1792]{2,1,0:T(8,128)(2,1)S(1)}, u32[]{:S(2)}, u32[]{:S(2)}) collective-permute-start(bf16[2,192,1792]{2,1,0:T(8,128)(2,1)} %pack.7), channel_id=1, source_target_pairs={{0,2},{2,4},{4,6},{1,3},{3,5},{5,7},{8,10},{10,12},{12,14},{9,11},... | collective-permute-start | bytes 4128776 | tf_op jit(solution)/shard_map/ppermute | solution.py:565
  72.8 59.9 %collective-permute-start.12 = (bf16[2,192,1792]{2,1,0:T(8,128)(2,1)}, bf16[2,192,1792]{2,1,0:T(8,128)(2,1)}, u32[]{:S(2)}, u32[]{:S(2)}) collective-permute-start(bf16[2,192,1792]{2,1,0:T(8,128)(2,1)} %pack.7), channel_id=1, source_target_pairs={{2,0},{4,2},{6,4},{3,1},{5,3},{7,5},{10,8},{12,10},{14,12},{11,9},... | collective-permute-start | bytes 4128776 | tf_op jit(solution)/shard_map/ppermute | solution.py:565
  107.4 35.7 %collective-permute-start.10 = (bf16[640,1280]{1,0:T(8,128)(2,1)}, bf16[640,1280]{1,0:T(8,128)(2,1)}, u32[]{:S(2)}, u32[]{:S(2)}) collective-permute-start(bf16[640,1280]{1,0:T(8,128)(2,1)} %collective-permute-done.6.refs_1_), channel_id=1, source_target_pairs={{0,16},{8,24},{16,0},{24,8},{1,17},{9,25},{17,1},{25,9},{2,18},{10... | collective-permute-start | bytes 4915208 | tf_op jit(solution)/shard_map/ppermute | solution.py:575
  109.0 35.7 %collective-permute-start.9 = (bf16[640,1280]{1,0:T(8,128)(2,1)}, bf16[640,1280]{1,0:T(8,128)(2,1)S(1)}, u32[]{:S(2)}, u32[]{:S(2)}) collective-permute-start(bf16[640,1280]{1,0:T(8,128)(2,1)} %collective-permute-done.6.refs_1_), channel_id=1, source_target_pairs={{0,8},{8,0},{16,24},{24,16},{1,9},{9,1},{17,25},{25,17},{2,10},{10... | collective-permute-start | bytes 4915208 | tf_op jit(solution)/shard_map/ppermute | solution.py:575
  110.2 42.8 %collective-permute-start.15 = (bf16[640,1280]{1,0:T(8,128)(2,1)}, bf16[640,1280]{1,0:T(8,128)(2,1)}, u32[]{:S(2)}, u32[]{:S(2)}) collective-permute-start(bf16[640,1280]{1,0:T(8,128)(2,1)} %collective-permute-done.6.refs_1_), channel_id=1, source_target_pairs={{0,2},{2,4},{4,6},{6,0},{1,3},{3,5},{5,7},{7,1},{8,10},{10,12},{12... | collective-permute-start | bytes 4915208 | tf_op jit(solution)/shard_map/ppermute | solution.py:570
  147.4 17.4 %collective-permute-start.13 = (bf16[320,1280]{1,0:T(8,128)(2,1)}, bf16[320,1280]{1,0:T(8,128)(2,1)}, u32[]{:S(2)}, u32[]{:S(2)}) collective-permute-start(bf16[320,1280]{1,0:T(8,128)(2,1)} %slice.31), channel_id=1, source_target_pairs={{0,8},{8,0},{16,24},{24,16},{1,9},{9,1},{17,25},{25,17},{2,10},{10... | collective-permute-start | bytes 2457608 | tf_op jit(solution)/shard_map/ppermute | solution.py:575
  149.5 17.1 %collective-permute-start.14 = (bf16[320,1280]{1,0:T(8,128)(2,1)}, bf16[320,1280]{1,0:T(8,128)(2,1)}, u32[]{:S(2)}, u32[]{:S(2)}) collective-permute-start(bf16[320,1280]{1,0:T(8,128)(2,1)} %slice.32), channel_id=1, source_target_pairs={{0,16},{8,24},{16,0},{24,8},{1,17},{9,25},{17,1},{25,9},{2,18},{10... | collective-permute-start | bytes 2457608 | tf_op jit(solution)/shard_map/ppermute | solution.py:575
  166.6 33.7 %collective-permute-start.18 = (bf16[640,1280]{1,0:T(8,128)(2,1)}, bf16[640,1280]{1,0:T(8,128)(2,1)}, u32[]{:S(2)}, u32[]{:S(2)}) collective-permute-start(bf16[640,1280]{1,0:T(8,128)(2,1)} %collective-permute-done.15.refs_0_), channel_id=1, source_target_pairs={{0,2},{2,4},{4,6},{6,0},{1,3},{3,5},{5,7},{7,1},{8,10},{10,12},{12... | collective-permute-start | bytes 4915208 | tf_op jit(solution)/shard_map/ppermute | solution.py:570
  166.8 33.5 %collective-permute-start.19 = (bf16[640,1280]{1,0:T(8,128)(2,1)}, bf16[640,1280]{1,0:T(8,128)(2,1)S(1)}, u32[]{:S(2)}, u32[]{:S(2)}) collective-permute-start(bf16[640,1280]{1,0:T(8,128)(2,1)} %collective-permute-done.15.refs_0_), channel_id=1, source_target_pairs={{0,8},{8,0},{16,24},{24,16},{1,9},{9,1},{17,25},{25,17},{2,10},{10... | collective-permute-start | bytes 4915208 | tf_op jit(solution)/shard_map/ppermute | solution.py:575
  167.1 33.3 %collective-permute-start.20 = (bf16[640,1280]{1,0:T(8,128)(2,1)}, bf16[640,1280]{1,0:T(8,128)(2,1)S(1)}, u32[]{:S(2)}, u32[]{:S(2)}) collective-permute-start(bf16[640,1280]{1,0:T(8,128)(2,1)} %collective-permute-done.15.refs_0_), channel_id=1, source_target_pairs={{0,16},{8,24},{16,0},{24,8},{1,17},{9,25},{17,1},{25,9},{2,18},{10... | collective-permute-start | bytes 4915208 | tf_op jit(solution)/shard_map/ppermute | solution.py:575
  168.0 31.1 %collective-permute-start.21 = (f32[1,2560]{1,0:T(1,128)S(1)}, f32[1,2560]{1,0:T(1,128)S(1)}, u32[]{:S(2)}, u32[]{:S(2)}) collective-permute-start(f32[1,2560]{1,0:T(1,128)S(1)} %get-tuple-element.113.own_gate), channel_id=1, source_target_pairs={{0,1},{1,0},{2,3},{3,2},{4,5},{5,4},{6,7},{7,6},{8,9},{9,8},{10,11... | collective-permute-start | bytes 30728 | tf_op jit(solution)/shard_map/ppermute | solution.py:575
  200.4 16.9 %collective-permute-start.22 = (bf16[384,2560]{1,0:T(8,128)(2,1)}, bf16[384,2560]{1,0:T(8,128)(2,1)}, u32[]{:S(2)}, u32[]{:S(2)}) collective-permute-start(bf16[384,2560]{1,0:T(8,128)(2,1)} %bitcast.24.own_hidden), channel_id=1, source_target_pairs={{0,1},{1,0},{2,3},{3,2},{4,5},{5,4},{6,7},{7,6},{8,9},{9,8},{10,11... | collective-permute-start | bytes 5898248 | tf_op jit(solution)/shard_map/ppermute | solution.py:575
  205.5 50.6 %collective-permute-start.23 = (bf16[640,1280]{1,0:T(8,128)(2,1)}, bf16[640,1280]{1,0:T(8,128)(2,1)}, u32[]{:S(2)}, u32[]{:S(2)}) collective-permute-start(bf16[640,1280]{1,0:T(8,128)(2,1)} %collective-permute-done.18.refs_3_), channel_id=1, source_target_pairs={{0,8},{8,0},{16,24},{24,16},{1,9},{9,1},{17,25},{25,17},{2,10},{10... | collective-permute-start | bytes 4915208 | tf_op jit(solution)/shard_map/ppermute | solution.py:575
  206.7 49.4 %collective-permute-start.24 = (bf16[640,1280]{1,0:T(8,128)(2,1)}, bf16[640,1280]{1,0:T(8,128)(2,1)}, u32[]{:S(2)}, u32[]{:S(2)}) collective-permute-start(bf16[640,1280]{1,0:T(8,128)(2,1)} %collective-permute-done.18.refs_3_), channel_id=1, source_target_pairs={{0,16},{8,24},{16,0},{24,8},{1,17},{9,25},{17,1},{25,9},{2,18},{10... | collective-permute-start | bytes 4915208 | tf_op jit(solution)/shard_map/ppermute | solution.py:575
  210.1 35.5 %collective-permute-start.16 = (bf16[2,192,1920]{2,1,0:T(8,128)(2,1)}, bf16[2,192,1920]{2,1,0:T(8,128)(2,1)S(1)}, u32[]{:S(2)}, u32[]{:S(2)}) collective-permute-start(bf16[2,192,1920]{2,1,0:T(8,128)(2,1)} %copy-done.15), channel_id=1, source_target_pairs={{0,2},{2,4},{4,6},{1,3},{3,5},{5,7},{8,10},{10,12},{12,14},{9,11},... | collective-permute-start | bytes 4423688 | tf_op jit(solution)/shard_map/ppermute | solution.py:565
  213.1 35.2 %collective-permute-start.17 = (bf16[2,192,1920]{2,1,0:T(8,128)(2,1)}, bf16[2,192,1920]{2,1,0:T(8,128)(2,1)}, u32[]{:S(2)}, u32[]{:S(2)}) collective-permute-start(bf16[2,192,1920]{2,1,0:T(8,128)(2,1)} %copy-done.14), channel_id=1, source_target_pairs={{2,0},{4,2},{6,4},{3,1},{5,3},{7,5},{10,8},{12,10},{14,12},{11,9},... | collective-permute-start | bytes 4423688 | tf_op jit(solution)/shard_map/ppermute | solution.py:565
  256.2 36.6 %collective-permute-start.25 = (bf16[640,1280]{1,0:T(8,128)(2,1)S(1)}, bf16[640,1280]{1,0:T(8,128)(2,1)S(1)}, u32[]{:S(2)}, u32[]{:S(2)}) collective-permute-start(bf16[640,1280]{1,0:T(8,128)(2,1)S(1)} %copy-done.5), channel_id=1, source_target_pairs={{0,16},{8,24},{16,0},{24,8},{1,17},{9,25},{17,1},{25,9},{2,18},{10... | collective-permute-start | bytes 4915208 | tf_op jit(solution)/shard_map/ppermute | solution.py:575
  256.8 36.5 %collective-permute-start.26 = (bf16[640,1280]{1,0:T(8,128)(2,1)}, bf16[640,1280]{1,0:T(8,128)(2,1)S(1)}, u32[]{:S(2)}, u32[]{:S(2)}) collective-permute-start(bf16[640,1280]{1,0:T(8,128)(2,1)} %collective-permute-done.24.refs_5_), channel_id=1, source_target_pairs={{0,8},{8,0},{16,24},{24,16},{1,9},{9,1},{17,25},{25,17},{2,10},{10... | collective-permute-start | bytes 4915208 | tf_op jit(solution)/shard_map/ppermute | solution.py:575
  265.4 8.6 %collective-permute-start.27 = (bf16[1,384,1280]{2,1,0:T(8,128)(2,1)S(1)}, bf16[1,384,1280]{2,1,0:T(8,128)(2,1)S(1)}, u32[]{:S(2)}, u32[]{:S(2)}) collective-permute-start(bf16[1,384,1280]{2,1,0:T(8,128)(2,1)S(1)} %get-tuple-element.133.refs_0_), channel_id=1, source_target_pairs={{0,1},{1,0},{2,3},{3,2},{4,5},{5,4},{6,7},{7,6},{8,9},{9,8},{10,11... | collective-permute-start | bytes 2949128 | tf_op jit(solution)/shard_map/ppermute | solution.py:575
  266.8 7.3 %collective-permute-start.28 = (bf16[1,384,1280]{2,1,0:T(8,128)(2,1)S(1)}, bf16[1,384,1280]{2,1,0:T(8,128)(2,1)S(1)}, u32[]{:S(2)}, u32[]{:S(2)}) collective-permute-start(bf16[1,384,1280]{2,1,0:T(8,128)(2,1)S(1)} %get-tuple-element.134.refs_1_), channel_id=1, source_target_pairs={{0,1},{1,0},{2,3},{3,2},{4,5},{5,4},{6,7},{7,6},{8,9},{9,8},{10,11... | collective-permute-start | bytes 2949128 | tf_op jit(solution)/shard_map/ppermute | solution.py:575
  297.9 4.9 %collective-permute-start.29 = (bf16[1,384,1280]{2,1,0:T(8,128)(2,1)S(1)}, bf16[1,384,1280]{2,1,0:T(8,128)(2,1)}, u32[]{:S(2)}, u32[]{:S(2)}) collective-permute-start(bf16[1,384,1280]{2,1,0:T(8,128)(2,1)S(1)} %get-tuple-element.147.refs_2_), channel_id=1, source_target_pairs={{0,1},{1,0},{2,3},{3,2},{4,5},{5,4},{6,7},{7,6},{8,9},{9,8},{10,11... | collective-permute-start | bytes 2949128 | tf_op jit(solution)/shard_map/ppermute | solution.py:575
  (24 other events, 602.4 us)

commit v3 on v2

--- a/solution.py
+++ b/solution.py
@@ -15,7 +15,7 @@
 LEVEL_STEP = 32
 
 EPSILON = 1e-06
-VMEM_LIMIT = 24 * 1024 * 1024
+VMEM_LIMIT = 28 * 1024 * 1024
 SMALL = pl.CostEstimate(flops=1, bytes_accessed=1, transcendentals=0)
 LARGE = pl.CostEstimate(flops=20_000_000_000, bytes_accessed=1, transcendentals=0)
 
@@ -96,7 +96,7 @@
     return pl.pallas_call(
         partial(pack_kernel, head_of=head_of, first=first, rows=rows),
         in_specs=[pl.BlockSpec(memory_space=pltpu.SMEM), anywhere],
-        out_specs=[anywhere] * len(rows),
+        out_specs=[pl.BlockSpec(memory_space=pltpu.VMEM)] * len(rows),
         out_shape=[
             jax.ShapeDtypeStruct((*source.shape[:-2], size, count * HD), source.dtype)
             for _, size in rows
@@ -338,7 +338,7 @@
         ),
         out_shape=jax.ShapeDtypeStruct((frames, tokens, plan.heads * HD), jnp.bfloat16),
         compiler_params=kernel_params(),
-        cost_estimate=SMALL,
+        cost_estimate=LARGE,
         name="combine",
     )(vector, near, near, *sides)
 
@@ -499,16 +499,17 @@
     )(hidden, gate, *own_parts, *other_parts)
 
 
-def finish_kernel(place, hidden, gate, scale, shift_by, sums, *refs, count, blocks):
-    early, refs = refs[:blocks], refs[blocks:]
-    own_parts, other_parts, (residual, ffn) = (
-        refs[:count],
-        refs[count : 2 * count],
-        refs[2 * count :],
-    )
-    width = hidden.shape[2]
-    others = gate.shape[0] - count
-    late = mixed_blocks(hidden, gate, others, own_parts, other_parts)
+def finish_kernel(place, gate, scale, shift_by, sums, early, *refs, count, blocks):
+    hidden, own_parts, other_parts = (refs[count * k : count * (k + 1)] for k in range(3))
+    residual, ffn = refs[3 * count :]
+    width = early.shape[2]
+    late = [
+        block
+        for index in range(count)
+        for block in mixed_blocks(
+            hidden[index], gate, 1 + index, own_parts[index : index + 1], other_parts[index : index + 1]
+        )
+    ]
     first = sums[:, 0:1]
     second = sums[:, 1:2]
     for mixed in late:
@@ -519,9 +520,9 @@
     inverse = lax.rsqrt(variance + EPSILON)
     for block in range(blocks):
         columns = slice(block * width, (block + 1) * width)
-        mixed = early[block][0].astype(jnp.float32)
+        mixed = early[0].astype(jnp.float32)
         for index in range(count):
-            mixed = jnp.where(place[2 * block] == others + index, late[index], mixed)
+            mixed = jnp.where(place[block] == 1 + index, late[index], mixed)
         residual[:, columns] = mixed.astype(jnp.bfloat16)
         ffn[:, columns] = (
             (mixed - average) * inverse * (1.0 + scale[:, columns]) + shift_by[:, columns]
@@ -531,24 +532,23 @@
 def finish(place, hidden, gate, scale, shift_by, sums, early, own_parts, other_parts):
     count = len(own_parts)
     _, tokens, width = hidden.shape
-    blocks = place.shape[0] // 2
+    blocks = place.shape[0]
     rows = 64 if tokens % 64 == 0 else tokens
     part = pl.BlockSpec((1, rows, width), lambda i, place: (0, i, 0))
-    several = pl.BlockSpec((count, rows, width), lambda i, place: (1, i, 0))
     whole = pl.BlockSpec((1, blocks * width), lambda i, place: (0, 0))
     row = pl.BlockSpec((rows, blocks * width), lambda i, place: (i, 0))
-    earlier = [
-        pl.BlockSpec((1, rows, width), lambda i, place, block=block: (place[2 * block + 1], i, 0))
-        for block in range(blocks)
+    later = [
+        pl.BlockSpec((1, rows, width), lambda i, place, index=index: (1 + index, i, 0))
+        for index in range(count)
     ]
     return pl.pallas_call(
         partial(finish_kernel, count=count, blocks=blocks),
         grid_spec=pltpu.PrefetchScalarGridSpec(
             num_scalar_prefetch=1,
             grid=(tokens // rows,),
-            in_specs=[several, pl.BlockSpec(gate.shape, lambda i, place: (0, 0, 0)), whole, whole]
-            + [pl.BlockSpec((rows, LANES), lambda i, place: (i, 0))]
-            + earlier
+            in_specs=[pl.BlockSpec(gate.shape, lambda i, place: (0, 0, 0)), whole, whole]
+            + [pl.BlockSpec((rows, LANES), lambda i, place: (i, 0)), part]
+            + later
             + [part] * (2 * count),
             out_specs=[row, row],
         ),
@@ -556,7 +556,7 @@
         compiler_params=kernel_params(),
         cost_estimate=SMALL,
         name="finish",
-    )(place, hidden, gate, scale, shift_by, sums, *[early] * blocks, *own_parts, *other_parts)
+    )(place, gate, scale, shift_by, sums, early, *[hidden] * count, *own_parts, *other_parts)
 
 
 def shift(block, axis, step):
@@ -643,10 +643,12 @@
     blocks = n_wa // 2
     depth = out_weight.shape[0] // 4
     width = out_weight.shape[1]
-    cut = depth // 2
-
-    share = lax.optimization_barrier(lax.dynamic_slice_in_dim(out_weight, ha * depth, depth, 0))
-    first = turn(share, "wa", 1)
+
+    def share(number):
+        return lax.dynamic_slice_in_dim(out_weight, number * depth, depth, 0)
+
+    mine = lax.optimization_barrier(share(ha))
+    first = turn(mine, "wa", 1)
     tokens = Tokens(queries, keys_values, windows, 4)
     vector = tokens.plan.vector
     top, bottom = tokens.halos(tokens.edge_rows(vector, 0))
@@ -654,38 +656,34 @@
     from_left = shift(queries, "wa", 1)
     from_right = shift(queries, "wa", -1)
 
-    first, top, bottom, vector = together(first, top, bottom, vector)
+    first, top, bottom, vector, mine = together(first, top, bottom, vector, mine)
     first_x = swap(first, "ha", 1)
     first_y = swap(first, "ha", 2)
-    second = turn(first, "wa", 1)
+    third = turn(mine, "wa", -1)
     halos = top, bottom, *tokens.rest_halos(vector)
     near = tokens.stay(vector, halos)
 
-    near, first_x, first_y, from_left, from_right = together(
-        near, first_x, first_y, from_left, from_right
-    )
-    first_far_x = swap(first_y[:cut], "ha", 1)
-    first_far_y = swap(first_x[cut:], "ha", 2)
-
-    first_far_x, first_far_y, second, from_left, from_right, gate = together(
-        first_far_x, first_far_y, second, from_left, from_right, picked[0:1]
-    )
-    third = turn(second, "wa", 1)
+    near, first_x, first_y, third, from_left, from_right, first, gate, hidden = together(
+        near, first_x, first_y, third, from_left, from_right, first, picked[0:1], hidden
+    )
+    third_x = swap(third, "ha", 1)
+    third_y = swap(third, "ha", 2)
+    second = turn(first, "wa", 1)
+    other_gate = swap(gate, "ta", 1)
+    other_hidden = swap(hidden, "ta", 1)
+    for_left, for_right = tokens.visit(vector, (from_left, from_right), halos)
+
+    for_left, for_right, other_gate, other_hidden = together(
+        for_left, for_right, other_gate, other_hidden
+    )
+    left = shift(for_right, "wa", 1)
+    right = shift(for_left, "wa", -1)
+
+    third_x, third_y, second, other_gate, vector = together(
+        third_x, third_y, second, other_gate, vector
+    )
     second_x = swap(second, "ha", 1)
     second_y = swap(second, "ha", 2)
-    other_gate = swap(gate, "ta", 1)
-    for_left, for_right = tokens.visit(vector, (from_left, from_right), halos)
-
-    for_left, for_right, first_far_x = together(for_left, for_right, first_far_x)
-    left = shift(for_right, "wa", 1)
-    right = shift(for_left, "wa", -1)
-
-    third, second_x, second_y, first_far_x, other_gate, hidden, vector = together(
-        third, second_x, second_y, first_far_x, other_gate, hidden, vector
-    )
-    third_x = swap(third, "ha", 1)
-    third_y = swap(third, "ha", 2)
-    other_hidden = swap(hidden, "ta", 1)
     rest_sides = tokens.rest_sides(vector, halos)
 
     def block_of(distance):
@@ -698,20 +696,17 @@
     left, right, base, gates = together(left, right, base, gates)
     attended = tokens.combine(vector, near, [left, right, *rest_sides])
 
-    third_x, third_y, second_x, attended = together(third_x, third_y, second_x, attended)
-    third_far = swap(third_y, "ha", 1)
+    second_x, second_y, first_y, attended = together(second_x, second_y, first_y, attended)
+    first_far = swap(first_y, "ha", 1)
     second_far = swap(second_x, "ha", 2)
+    third_far = turn(share(ha ^ 3), "wa", -1)
 
     turned = ha.reshape(1)
     sums = project(
         turned,
         attended,
-        [out_weight, first, first_x, first_y, first_far_x, first_far_y],
-        [
-            [(0, depth, number, True) for number in range(4)],
-            [(number, depth, 0, False) for number in range(1, 4)]
-            + [(4, cut, 0, False), (5, depth - cut, 0, False)],
-        ],
+        [out_weight],
+        [[(0, depth, number, True) for number in range(4)]],
         None,
         0,
         jnp.bfloat16,
@@ -720,29 +715,30 @@
     late = project(
         turned,
         attended,
-        [second, second_x, second_y, third, third_x, third_y],
-        [[(start + number, depth, 0, False) for number in range(3)] for start in (0, 3)],
+        [first, first_x, first_y, second, second_x, second_y, third, third_x, third_y],
+        [[(start + number, depth, 0, False) for number in range(3)] for start in (0, 3, 6)],
         None,
         0,
         jnp.float32,
     )
     early, totals = mix(base, gates, sums, other_sums)
 
-    second_far, third_far, early, totals, *late = together(
-        second_far, third_far, early, totals, *late
+    first_far, second_far, third_far, early, totals, *late = together(
+        first_far, second_far, third_far, early, totals, *late
     )
     late = project(
         turned,
         attended,
-        [second_far, third_far],
-        [[(0, depth, 0, False)], [(1, depth, 0, False)]],
+        [first_far, second_far, third_far],
+        [[(number, depth, 0, False)] for number in range(3)],
         late,
         3 * depth,
         jnp.bfloat16,
     )
     other_late = [swap(part, "ta", 1) for part in late]
-    mine = [lax.rem(wa - ta * blocks - block + 2 * n_wa, n_wa) for block in range(blocks)]
-    place = jnp.stack([value for slot in mine for value in (slot, jnp.minimum(slot, 1))])
+    place = jnp.stack(
+        [lax.rem(wa - ta * blocks - block + 2 * n_wa, n_wa) for block in range(blocks)]
+    )
     return finish(
         place, base, gates, picked[2:3], picked[1:2], totals, early, late, other_late
     )

time: 317 us -> 270 us (0.85)
  Pallas kernels: 147 us -> 94 us
  starting transfers between devices: 39 us -> 67.8 us
  waiting for transfers between devices: 99.4 us -> 79.4 us
    pallas_call x2, Pallas kernels: 59.2 us -> 4.47 us  [pack(): pl.pallas_call(partial(pack_kernel, head_of=head_of, first=first, rows=ro...]
    ppermute x16 -> x14, waiting for transfers between devices: 46.7 us -> 14.9 us  [swap(): return lax.ppermute(block, axis, [(i, i ^ bit) for i in range(count)])]
    ppermute x16 -> x14, starting transfers between devices: 21.4 us -> 47.8 us  [swap(): return lax.ppermute(block, axis, [(i, i ^ bit) for i in range(count)])]
    ppermute x3 -> x4, waiting for transfers between devices: 1.26 us -> 14.6 us  [turn(): lax.ppermute(block, axis, [(i, (i + step) % count) for i in range(count)])]
    unnamed x46 -> x36, local copies, waits for them, and re-layouts: 5.14 us -> 10.2 us
    slice x2 -> x0, local copies, waits for them, and re-layouts: 3.6 us -> none  [the longest x1 2.66 us: paired(): first_far_x = swap(first_y[:cut], 'ha', 1)]
    pallas_call x1, Pallas kernels: 4.74 us -> 1.51 us  [pick(): pl.pallas_call(pick_kernel, grid_spec=pltpu.PrefetchScalarGridSpec(num_sc...]
  transfers between devices with their start and end apart: 25 -> 24, of which waited for: 13 -> 10; matrix products, arithmetic and copies ran while one was open for 4% -> 3% of each run, Pallas kernels for 43% -> 30%
where the time goes in v3:
time: 270 us; the launch traced here: 269 us
  Pallas kernels  94 us (35%)
  waiting for transfers between devices  79.4 us (29%)
  starting transfers between devices  67.8 us (25%)
  local copies, waits for them, and re-layouts  19.7 us (7%)
  blocking collectives  3.92 us (1%)
  between operations  2.88 us (1%)
    ppermute x6, waiting for transfers between devices, shift(): return lax.ppermute(block, axis, pairs)  50 us
    pallas_call x2, Pallas kernels, attention(): pl.pallas_call(partial(attention_kernel, plan=plan, head_of=head_of, q_co...  49.5 us
    ppermute x14, starting transfers between devices, swap(): return lax.ppermute(block, axis, [(i, i ^ bit) for i in range(count)])  47.8 us
    pallas_call x3, Pallas kernels, project(): pl.pallas_call(partial(project_kernel, slots=slots, carried=carry is not...  21.3 us
    ppermute x6, starting transfers between devices, shift(): return lax.ppermute(block, axis, pairs)  15.9 us
    ppermute x14, waiting for transfers between devices, swap(): return lax.ppermute(block, axis, [(i, i ^ bit) for i in range(count)])  14.9 us
    ppermute x4, waiting for transfers between devices, turn(): lax.ppermute(block, axis, [(i, (i + step) % count) for i in range(count)])  14.6 us
    unnamed x36, local copies, waits for them, and re-layouts  10.2 us
  transfers between devices with their start and end apart: 24, of which 10 were waited for; matrix products, arithmetic and copies ran while one was open for 3% of the time, Pallas kernels for 30%

profile of v3, /device:TPU:17, one launch (start us, length us, event | category | flops | bytes accessed | tf_op | source)
XLA Modules:
  0.0 269.1 jit_solution(3886776411806818251)
XLA Ops:
  0.7 3.8 %constant_dynamic-slice_fusion = (bf16[640,1280]{1,0:T(8,128)(2,1)}, bf16[640,1280]{1,0:T(8,128)(2,1)}) fusion(bf16[2560,1280]{1,0:T(8,128)(2,1)} %refs_0_.1, s32[]{:T(128)S(6)} %select_n.40, s32[]{:T(128)S(6)} %select_n.32), kind=kLoop, calls=%fused_computation.9 | loop fusion | bytes 6553608 | tf_op jit(solution)/shard_map/dynamic_slice | solution.py:648
  7.3 2.4 pack.6
  9.7 4.1 %collective-permute-start.7 = (bf16[2,2,64,1792]{3,2,1,0:T(8,128)(2,1)S(1)}, bf16[2,2,64,1792]{3,2,1,0:T(8,128)(2,1)}, u32[]{:S(2)}, u32[]{:S(2)}) collective-permute-start(bf16[2,2,64,1792]{3,2,1,0:T(8,128)(2,1)S(1)} %get-tuple-element.92), channel_id=1, source_target_pairs={{0,8},{8,16},{16,24},{1,9},{9,17},{17,25},{2,10},{10,18},{18,26},{... | collective-permute-start | bytes 2752520 | tf_op jit(solution)/shard_map/ppermute | solution.py:565
  15.1 2.1 pack.7
  19.2 3.4 %collective-permute-start.13 = (bf16[2,192,1792]{2,1,0:T(8,128)(2,1)}, bf16[2,192,1792]{2,1,0:T(8,128)(2,1)}, u32[]{:S(2)}, u32[]{:S(2)}) collective-permute-start(bf16[2,192,1792]{2,1,0:T(8,128)(2,1)} %pack.7), channel_id=1, source_target_pairs={{2,0},{4,2},{6,4},{3,1},{5,3},{7,5},{10,8},{12,10},{14,12},{11,9},... | collective-permute-start | bytes 4128776 | tf_op jit(solution)/shard_map/ppermute | solution.py:565
  22.6 3.9 %pmax.7 = f32[2]{0:T(128)S(1)} all-reduce(f32[2]{0:T(128)S(1)} %subtract_reduce_fusion), channel_id=1, replica_groups=mesh['ha'=4,'wa'=4,'ta'=2] {'ta'}, use_global_device_ids=true, to_apply=%region_3.4 | all-reduce | flops 2 | bytes 16 | tf_op jit(solution)/shard_map/pmax | solution.py:48
  29.4 2.2 collective-permute-done.7.refs_2_.refs_3_
  31.5 21.7 %collective-permute-done.8.refs_3_.refs_4_ = bf16[2,2,64,1792]{3,2,1,0:T(8,128)(2,1)} collective-permute-done((bf16[2,2,64,1792]{3,2,1,0:T(8,128)(2,1)S(1)}, bf16[2,2,64,1792]{3,2,1,0:T(8,128)(2,1)}, u32[]{:S(2)}, u32[]{:S(2)}) %collective-permute-start.8) | collective-permute-done | bytes 917536 | tf_op jit(solution)/shard_map/ppermute | solution.py:565
  56.2 22.7 %attend_own.1.own.own_stat = bf16[2,192,2688]{2,1,0:T(8,128)(2,1)S(1)} custom-call(s32[125]{0:T(128)S(1)} %concatenate.10.vector, bf16[2,192,2560]{2,1,0:T(8,128)(2,1)} %bitcast.51, bf16[2,2,192,2560]{3,2,1,0:T(8,128)(2,1)} %bitcast.48, bf16[2,2,64,1792]{3,2,1,0:T(8,128)(2,1)} %collective-permute-done.7.refs_2_.refs_3_, ...), custom_call_target="tpu_custom_call" | custom-call | flops 20000000000 | bytes 1 | tf_op jit(solution)/shard_map/attend_own/pallas_call | solution.py:251
  80.3 8.7 %collective-permute-done.10.refs_2_ = bf16[640,1280]{1,0:T(8,128)(2,1)} collective-permute-done((bf16[640,1280]{1,0:T(8,128)(2,1)}, bf16[640,1280]{1,0:T(8,128)(2,1)}, u32[]{:S(2)}, u32[]{:S(2)}) %collective-permute-start.10) | collective-permute-done | bytes 1638432 | tf_op jit(solution)/shard_map/ppermute | solution.py:575
  91.7 14.6 %collective-permute-done.11.refs_6_ = bf16[640,1280]{1,0:T(8,128)(2,1)} collective-permute-done((bf16[640,1280]{1,0:T(8,128)(2,1)}, bf16[640,1280]{1,0:T(8,128)(2,1)}, u32[]{:S(2)}, u32[]{:S(2)}) %collective-permute-start.11) | collective-permute-done | bytes 1638432 | tf_op jit(solution)/shard_map/ppermute | solution.py:570
  106.3 2.5 collective-permute-start.15
  113.4 26.8 %attend_visitors.3 = (bf16[2,192,1920]{2,1,0:T(8,128)(2,1)}, bf16[2,192,1920]{2,1,0:T(8,128)(2,1)}) custom-call(s32[125]{0:T(128)S(1)} %concatenate.10.vector, bf16[2,192,1792]{2,1,0:T(8,128)(2,1)S(1)} %collective-permute-done.12.refs_0_, bf16[2,192,1792]{2,1,0:T(8,128)(2,1)} %collective-permute-done.13.refs_1_, bf16[2,2,192,2560]{3,2,1,0:T(8,128)(2,1)S(1)} %bitcast.50, ...), custom_call_target="tpu_custom_call" | custom-call | flops 1 | bytes 1 | tf_op jit(solution)/shard_map/attend_visitors/pallas_call | solution.py:251
  141.4 2.5 collective-permute-start.16
  144.0 2.7 %collective-permute-start.17 = (bf16[2,192,1920]{2,1,0:T(8,128)(2,1)}, bf16[2,192,1920]{2,1,0:T(8,128)(2,1)}, u32[]{:S(2)}, u32[]{:S(2)}) collective-permute-start(bf16[2,192,1920]{2,1,0:T(8,128)(2,1)} %get-tuple-element.108), channel_id=1, source_target_pairs={{2,0},{4,2},{6,4},{3,1},{5,3},{7,5},{10,8},{12,10},{14,12},{11,9},... | collective-permute-start | bytes 4423688 | tf_op jit(solution)/shard_map/ppermute | solution.py:565
  154.5 25.6 %collective-permute-done.16.left = bf16[2,192,1920]{2,1,0:T(8,128)(2,1)} collective-permute-done((bf16[2,192,1920]{2,1,0:T(8,128)(2,1)}, bf16[2,192,1920]{2,1,0:T(8,128)(2,1)}, u32[]{:S(2)}, u32[]{:S(2)}) %collective-permute-start.16) | collective-permute-done | bytes 1474592 | tf_op jit(solution)/shard_map/ppermute | solution.py:565
  180.6 8.6 %combine.1 = bf16[2,192,2560]{2,1,0:T(8,128)(2,1)S(1)} custom-call(s32[125]{0:T(128)S(1)} %concatenate.10.vector, bf16[2,192,2688]{2,1,0:T(8,128)(2,1)S(1)} %copy-done.12, bf16[2,192,2688]{2,1,0:T(8,128)(2,1)S(1)} %copy-done.12, bf16[2,192,1920]{2,1,0:T(8,128)(2,1)} %collective-permute-done.16.left, bf16[2,192,1920]{2,1,0:T(8,128)(2,1)} %collective-permute-done.17.right, ...), custom_call_target="tpu_custom_call" | custom-call | flops 20000000000 | bytes 1 | tf_op jit(solution)/shard_map/combine/pallas_call | solution.py:328
  189.7 4.5 %project.3.refs_0_ = bf16[1,384,1280]{2,1,0:T(8,128)(2,1)S(1)} custom-call(s32[1]{0:T(128)} %bitcast.7.place, bf16[384,2560]{1,0:T(8,128)(2,1)S(1)} %bitcast.39, bf16[2560,1280]{1,0:T(8,128)(2,1)S(1)} %bitcast.43), custom_call_target="tpu_custom_call" | custom-call | flops 1 | bytes 1 | tf_op jit(solution)/shard_map/project/pallas_call | solution.py:396
  194.2 35.9 %collective-permute-start.26 = (bf16[1,384,1280]{2,1,0:T(8,128)(2,1)S(1)}, bf16[1,384,1280]{2,1,0:T(8,128)(2,1)S(1)}, u32[]{:S(2)}, u32[]{:S(2)}) collective-permute-start(bf16[1,384,1280]{2,1,0:T(8,128)(2,1)S(1)} %project.3.refs_0_), channel_id=1, source_target_pairs={{0,1},{1,0},{2,3},{3,2},{4,5},{5,4},{6,7},{7,6},{8,9},{9,8},{10,11... | collective-permute-start | bytes 2949128 | tf_op jit(solution)/shard_map/ppermute | solution.py:575
  231.5 10.3 %project.4 = (f32[1,384,1280]{2,1,0:T(8,128)S(1)}, f32[1,384,1280]{2,1,0:T(8,128)S(1)}, f32[1,384,1280]{2,1,0:T(8,128)S(1)}) custom-call(s32[1]{0:T(128)} %bitcast.7.place, bf16[384,2560]{1,0:T(8,128)(2,1)S(1)} %bitcast.40, bf16[640,1280]{1,0:T(8,128)(2,1)} %collective-permute-done.6.refs_0_, bf16[640,1280]{1,0:T(8,128)(2,1)S(1)} %copy-done.6, ...), custom_call_target="tpu_custom_call" | custom-call | flops 1 | bytes 1 | tf_op jit(solution)/shard_map/project/pallas_call | solution.py:396
  243.0 6.6 %project.5 = (bf16[1,384,1280]{2,1,0:T(8,128)(2,1)}, bf16[1,384,1280]{2,1,0:T(8,128)(2,1)}, bf16[1,384,1280]{2,1,0:T(8,128)(2,1)}) custom-call(s32[1]{0:T(128)} %bitcast.7.place, bf16[384,2560]{1,0:T(8,128)(2,1)S(1)} %bitcast.41, bf16[640,1280]{1,0:T(8,128)(2,1)S(1)} %collective-permute-done.23.refs_0_, ...), custom_call_target="tpu_custom_call" | custom-call | flops 1 | bytes 1 | tf_op jit(solution)/shard_map/project/pallas_call | solution.py:396
  249.6 3.4 %collective-permute-start.27 = (bf16[1,384,1280]{2,1,0:T(8,128)(2,1)}, bf16[1,384,1280]{2,1,0:T(8,128)(2,1)S(1)}, u32[]{:S(2)}, u32[]{:S(2)}) collective-permute-start(bf16[1,384,1280]{2,1,0:T(8,128)(2,1)} %get-tuple-element.146.refs_3_), channel_id=1, source_target_pairs={{0,1},{1,0},{2,3},{3,2},{4,5},{5,4},{6,7},{7,6},{8,9},{9,8},{10,11... | collective-permute-start | bytes 2949128 | tf_op jit(solution)/shard_map/ppermute | solution.py:575
  258.2 2.1 copy-done.1
  261.5 7.6 %finish.1 = (bf16[384,2560]{1,0:T(8,128)(2,1)}, bf16[384,2560]{1,0:T(8,128)(2,1)}) custom-call(s32[2]{0:T(128)S(1)} %pad_add_fusion.1.place, f32[4,1,1280]{2,1,0:T(1,128)S(1)} %get-tuple-element.116.gate, f32[1,2560]{1,0:T(1,128)S(1)} %get-tuple-element.154.scale, f32[1,2560]{1,0:T(1,128)S(1)} %get-tuple-element.153.shift_by, ...), custom_call_target="tpu_custom_call" | custom-call | flops 1 | bytes 1 | tf_op jit(solution)/shard_map/finish/pallas_call | solution.py:544
  (99 shorter events, 41.1 us)
Async XLA Ops:
  4.5 48.7 %collective-permute-start.6 = (bf16[640,1280]{1,0:T(8,128)(2,1)}, bf16[640,1280]{1,0:T(8,128)(2,1)}, u32[]{:S(2)}, u32[]{:S(2)}) collective-permute-start(bf16[640,1280]{1,0:T(8,128)(2,1)} %get-tuple-element.100), channel_id=1, source_target_pairs={{0,2},{2,4},{4,6},{6,0},{1,3},{3,5},{5,7},{7,1},{8,10},{10,12},{12... | collective-permute-start | bytes 4915208 | tf_op jit(solution)/shard_map/ppermute | solution.py:570
  9.7 21.8 %collective-permute-start.7 = (bf16[2,2,64,1792]{3,2,1,0:T(8,128)(2,1)S(1)}, bf16[2,2,64,1792]{3,2,1,0:T(8,128)(2,1)}, u32[]{:S(2)}, u32[]{:S(2)}) collective-permute-start(bf16[2,2,64,1792]{3,2,1,0:T(8,128)(2,1)S(1)} %get-tuple-element.92), channel_id=1, source_target_pairs={{0,8},{8,16},{16,24},{1,9},{9,17},{17,25},{2,10},{10,18},{18,26},{... | collective-permute-start | bytes 2752520 | tf_op jit(solution)/shard_map/ppermute | solution.py:565
  13.8 39.5 %collective-permute-start.8 = (bf16[2,2,64,1792]{3,2,1,0:T(8,128)(2,1)S(1)}, bf16[2,2,64,1792]{3,2,1,0:T(8,128)(2,1)}, u32[]{:S(2)}, u32[]{:S(2)}) collective-permute-start(bf16[2,2,64,1792]{3,2,1,0:T(8,128)(2,1)S(1)} %get-tuple-element.93), channel_id=1, source_target_pairs={{8,0},{16,8},{24,16},{9,1},{17,9},{25,17},{10,2},{18,10},{26,18},{... | collective-permute-start | bytes 2752520 | tf_op jit(solution)/shard_map/ppermute | solution.py:565
  17.2 63.1 %collective-permute-start.12 = (bf16[2,192,1792]{2,1,0:T(8,128)(2,1)}, bf16[2,192,1792]{2,1,0:T(8,128)(2,1)S(1)}, u32[]{:S(2)}, u32[]{:S(2)}) collective-permute-start(bf16[2,192,1792]{2,1,0:T(8,128)(2,1)} %pack.7), channel_id=1, source_target_pairs={{0,2},{2,4},{4,6},{1,3},{3,5},{5,7},{8,10},{10,12},{12,14},{9,11},... | collective-permute-start | bytes 4128776 | tf_op jit(solution)/shard_map/ppermute | solution.py:565
  19.2 61.1 %collective-permute-start.13 = (bf16[2,192,1792]{2,1,0:T(8,128)(2,1)}, bf16[2,192,1792]{2,1,0:T(8,128)(2,1)}, u32[]{:S(2)}, u32[]{:S(2)}) collective-permute-start(bf16[2,192,1792]{2,1,0:T(8,128)(2,1)} %pack.7), channel_id=1, source_target_pairs={{2,0},{4,2},{6,4},{3,1},{5,3},{7,5},{10,8},{12,10},{14,12},{11,9},... | collective-permute-start | bytes 4128776 | tf_op jit(solution)/shard_map/ppermute | solution.py:565
  53.2 35.7 %collective-permute-start.10 = (bf16[640,1280]{1,0:T(8,128)(2,1)}, bf16[640,1280]{1,0:T(8,128)(2,1)}, u32[]{:S(2)}, u32[]{:S(2)}) collective-permute-start(bf16[640,1280]{1,0:T(8,128)(2,1)} %collective-permute-done.6.refs_0_), channel_id=1, source_target_pairs={{0,16},{8,24},{16,0},{24,8},{1,17},{9,25},{17,1},{25,9},{2,18},{10... | collective-permute-start | bytes 4915208 | tf_op jit(solution)/shard_map/ppermute | solution.py:575
  54.8 35.7 %collective-permute-start.9 = (bf16[640,1280]{1,0:T(8,128)(2,1)}, bf16[640,1280]{1,0:T(8,128)(2,1)S(1)}, u32[]{:S(2)}, u32[]{:S(2)}) collective-permute-start(bf16[640,1280]{1,0:T(8,128)(2,1)} %collective-permute-done.6.refs_0_), channel_id=1, source_target_pairs={{0,8},{8,0},{16,24},{24,16},{1,9},{9,1},{17,25},{25,17},{2,10},{10... | collective-permute-start | bytes 4915208 | tf_op jit(solution)/shard_map/ppermute | solution.py:575
  56.0 50.3 %collective-permute-start.11 = (bf16[640,1280]{1,0:T(8,128)(2,1)}, bf16[640,1280]{1,0:T(8,128)(2,1)}, u32[]{:S(2)}, u32[]{:S(2)}) collective-permute-start(bf16[640,1280]{1,0:T(8,128)(2,1)} %get-tuple-element.100), channel_id=1, source_target_pairs={{0,6},{2,0},{4,2},{6,4},{1,7},{3,1},{5,3},{7,5},{8,14},{10,8},{12,... | collective-permute-start | bytes 4915208 | tf_op jit(solution)/shard_map/ppermute | solution.py:570
  106.3 33.9 %collective-permute-start.15 = (bf16[384,2560]{1,0:T(8,128)(2,1)S(1)}, bf16[384,2560]{1,0:T(8,128)(2,1)S(1)}, u32[]{:S(2)}, u32[]{:S(2)}) collective-permute-start(bf16[384,2560]{1,0:T(8,128)(2,1)S(1)} %bitcast.44), channel_id=1, source_target_pairs={{0,1},{1,0},{2,3},{3,2},{4,5},{5,4},{6,7},{7,6},{8,9},{9,8},{10,11... | collective-permute-start | bytes 5898248 | tf_op jit(solution)/shard_map/ppermute | solution.py:575
  108.7 39.0 %collective-permute-start.18 = (bf16[640,1280]{1,0:T(8,128)(2,1)}, bf16[640,1280]{1,0:T(8,128)(2,1)}, u32[]{:S(2)}, u32[]{:S(2)}) collective-permute-start(bf16[640,1280]{1,0:T(8,128)(2,1)} %collective-permute-done.11.refs_6_), channel_id=1, source_target_pairs={{0,8},{8,0},{16,24},{24,16},{1,9},{9,1},{17,25},{25,17},{2,10},{10... | collective-permute-start | bytes 4915208 | tf_op jit(solution)/shard_map/ppermute | solution.py:575
  109.9 39.2 %collective-permute-start.19 = (bf16[640,1280]{1,0:T(8,128)(2,1)}, bf16[640,1280]{1,0:T(8,128)(2,1)}, u32[]{:S(2)}, u32[]{:S(2)}) collective-permute-start(bf16[640,1280]{1,0:T(8,128)(2,1)} %collective-permute-done.11.refs_6_), channel_id=1, source_target_pairs={{0,16},{8,24},{16,0},{24,8},{1,17},{9,25},{17,1},{25,9},{2,18},{10... | collective-permute-start | bytes 4915208 | tf_op jit(solution)/shard_map/ppermute | solution.py:575
  111.2 37.9 %collective-permute-start.20 = (bf16[640,1280]{1,0:T(8,128)(2,1)}, bf16[640,1280]{1,0:T(8,128)(2,1)}, u32[]{:S(2)}, u32[]{:S(2)}) collective-permute-start(bf16[640,1280]{1,0:T(8,128)(2,1)} %collective-permute-done.6.refs_0_), channel_id=1, source_target_pairs={{0,2},{2,4},{4,6},{6,0},{1,3},{3,5},{5,7},{7,1},{8,10},{10,12},{12... | collective-permute-start | bytes 4915208 | tf_op jit(solution)/shard_map/ppermute | solution.py:570
  112.5 27.7 %collective-permute-start.14 = (f32[1,2560]{1,0:T(1,128)S(1)}, f32[1,2560]{1,0:T(1,128)S(1)}, u32[]{:S(2)}, u32[]{:S(2)}) collective-permute-start(f32[1,2560]{1,0:T(1,128)S(1)} %get-tuple-element.105.own_gate), channel_id=1, source_target_pairs={{0,1},{1,0},{2,3},{3,2},{4,5},{5,4},{6,7},{7,6},{8,9},{9,8},{10,11... | collective-permute-start | bytes 30728 | tf_op jit(solution)/shard_map/ppermute | solution.py:575
  141.4 38.7 %collective-permute-start.16 = (bf16[2,192,1920]{2,1,0:T(8,128)(2,1)}, bf16[2,192,1920]{2,1,0:T(8,128)(2,1)}, u32[]{:S(2)}, u32[]{:S(2)}) collective-permute-start(bf16[2,192,1920]{2,1,0:T(8,128)(2,1)} %get-tuple-element.107), channel_id=1, source_target_pairs={{0,2},{2,4},{4,6},{1,3},{3,5},{5,7},{8,10},{10,12},{12,14},{9,11},... | collective-permute-start | bytes 4423688 | tf_op jit(solution)/shard_map/ppermute | solution.py:565
  144.0 36.6 %collective-permute-start.17 = (bf16[2,192,1920]{2,1,0:T(8,128)(2,1)}, bf16[2,192,1920]{2,1,0:T(8,128)(2,1)}, u32[]{:S(2)}, u32[]{:S(2)}) collective-permute-start(bf16[2,192,1920]{2,1,0:T(8,128)(2,1)} %get-tuple-element.108), channel_id=1, source_target_pairs={{2,0},{4,2},{6,4},{3,1},{5,3},{7,5},{10,8},{12,10},{14,12},{11,9},... | collective-permute-start | bytes 4423688 | tf_op jit(solution)/shard_map/ppermute | solution.py:565
  147.7 95.2 %collective-permute-start.25 = (bf16[640,1280]{1,0:T(8,128)(2,1)}, bf16[640,1280]{1,0:T(8,128)(2,1)}, u32[]{:S(2)}, u32[]{:S(2)}) collective-permute-start(bf16[640,1280]{1,0:T(8,128)(2,1)} %get-tuple-element.151), channel_id=1, source_target_pairs={{0,6},{2,0},{4,2},{6,4},{1,7},{3,1},{5,3},{7,5},{8,14},{10,8},{12,... | collective-permute-start | bytes 4915208 | tf_op jit(solution)/shard_map/ppermute | solution.py:570
  150.9 38.2 %collective-permute-start.21 = (bf16[640,1280]{1,0:T(8,128)(2,1)}, bf16[640,1280]{1,0:T(8,128)(2,1)}, u32[]{:S(2)}, u32[]{:S(2)}) collective-permute-start(bf16[640,1280]{1,0:T(8,128)(2,1)} %collective-permute-done.20.refs_3_), channel_id=1, source_target_pairs={{0,8},{8,0},{16,24},{24,16},{1,9},{9,1},{17,25},{25,17},{2,10},{10... | collective-permute-start | bytes 4915208 | tf_op jit(solution)/shard_map/ppermute | solution.py:575
  151.2 38.0 %collective-permute-start.22 = (bf16[640,1280]{1,0:T(8,128)(2,1)}, bf16[640,1280]{1,0:T(8,128)(2,1)S(1)}, u32[]{:S(2)}, u32[]{:S(2)}) collective-permute-start(bf16[640,1280]{1,0:T(8,128)(2,1)} %collective-permute-done.20.refs_3_), channel_id=1, source_target_pairs={{0,16},{8,24},{16,0},{24,8},{1,17},{9,25},{17,1},{25,9},{2,18},{10... | collective-permute-start | bytes 4915208 | tf_op jit(solution)/shard_map/ppermute | solution.py:575
  189.2 53.8 %collective-permute-start.23 = (bf16[640,1280]{1,0:T(8,128)(2,1)}, bf16[640,1280]{1,0:T(8,128)(2,1)S(1)}, u32[]{:S(2)}, u32[]{:S(2)}) collective-permute-start(bf16[640,1280]{1,0:T(8,128)(2,1)} %collective-permute-done.10.refs_2_), channel_id=1, source_target_pairs={{0,8},{8,0},{16,24},{24,16},{1,9},{9,1},{17,25},{25,17},{2,10},{10... | collective-permute-start | bytes 4915208 | tf_op jit(solution)/shard_map/ppermute | solution.py:575
  189.5 53.5 %collective-permute-start.24 = (bf16[640,1280]{1,0:T(8,128)(2,1)}, bf16[640,1280]{1,0:T(8,128)(2,1)S(1)}, u32[]{:S(2)}, u32[]{:S(2)}) collective-permute-start(bf16[640,1280]{1,0:T(8,128)(2,1)} %collective-permute-done.21.refs_4_), channel_id=1, source_target_pairs={{0,16},{8,24},{16,0},{24,8},{1,17},{9,25},{17,1},{25,9},{2,18},{10... | collective-permute-start | bytes 4915208 | tf_op jit(solution)/shard_map/ppermute | solution.py:575
  194.2 47.6 %collective-permute-start.26 = (bf16[1,384,1280]{2,1,0:T(8,128)(2,1)S(1)}, bf16[1,384,1280]{2,1,0:T(8,128)(2,1)S(1)}, u32[]{:S(2)}, u32[]{:S(2)}) collective-permute-start(bf16[1,384,1280]{2,1,0:T(8,128)(2,1)S(1)} %project.3.refs_0_), channel_id=1, source_target_pairs={{0,1},{1,0},{2,3},{3,2},{4,5},{5,4},{6,7},{7,6},{8,9},{9,8},{10,11... | collective-permute-start | bytes 2949128 | tf_op jit(solution)/shard_map/ppermute | solution.py:575
  249.6 5.8 %collective-permute-start.27 = (bf16[1,384,1280]{2,1,0:T(8,128)(2,1)}, bf16[1,384,1280]{2,1,0:T(8,128)(2,1)S(1)}, u32[]{:S(2)}, u32[]{:S(2)}) collective-permute-start(bf16[1,384,1280]{2,1,0:T(8,128)(2,1)} %get-tuple-element.146.refs_3_), channel_id=1, source_target_pairs={{0,1},{1,0},{2,3},{3,2},{4,5},{5,4},{6,7},{7,6},{8,9},{9,8},{10,11... | collective-permute-start | bytes 2949128 | tf_op jit(solution)/shard_map/ppermute | solution.py:575
  253.0 3.8 %collective-permute-start.28 = (bf16[1,384,1280]{2,1,0:T(8,128)(2,1)}, bf16[1,384,1280]{2,1,0:T(8,128)(2,1)S(1)}, u32[]{:S(2)}, u32[]{:S(2)}) collective-permute-start(bf16[1,384,1280]{2,1,0:T(8,128)(2,1)} %get-tuple-element.147.refs_4_), channel_id=1, source_target_pairs={{0,1},{1,0},{2,3},{3,2},{4,5},{5,4},{6,7},{7,6},{8,9},{9,8},{10,11... | collective-permute-start | bytes 2949128 | tf_op jit(solution)/shard_map/ppermute | solution.py:575
  253.1 5.1 %collective-permute-start.29 = (bf16[1,384,1280]{2,1,0:T(8,128)(2,1)}, bf16[1,384,1280]{2,1,0:T(8,128)(2,1)S(1)}, u32[]{:S(2)}, u32[]{:S(2)}) collective-permute-start(bf16[1,384,1280]{2,1,0:T(8,128)(2,1)} %get-tuple-element.148.refs_5_), channel_id=1, source_target_pairs={{0,1},{1,0},{2,3},{3,2},{4,5},{5,4},{6,7},{7,6},{8,9},{9,8},{10,11... | collective-permute-start | bytes 2949128 | tf_op jit(solution)/shard_map/ppermute | solution.py:575
  (18 other events, 316.2 us)

commit v4 on v3

--- a/solution.py
+++ b/solution.py
@@ -15,7 +15,7 @@
 LEVEL_STEP = 32
 
 EPSILON = 1e-06
-VMEM_LIMIT = 28 * 1024 * 1024
+VMEM_LIMIT = 24 * 1024 * 1024
 SMALL = pl.CostEstimate(flops=1, bytes_accessed=1, transcendentals=0)
 LARGE = pl.CostEstimate(flops=20_000_000_000, bytes_accessed=1, transcendentals=0)
 
@@ -347,8 +347,8 @@
     arrays = 1 + max(piece[0] for slot in slots for piece in slot)
     pieces, refs = refs[:arrays], refs[arrays:]
     if carried:
-        carry, refs = refs[: len(slots)], refs[len(slots) :]
-    outs, (rows, weight, rows_sem, weight_sem) = refs[: len(slots)], refs[len(slots) :]
+        carry, refs = refs[0], refs[1:]
+    out, rows, weight, rows_sem, weight_sem = refs
     columns = weight.shape[1]
     depth = weight.shape[2]
     rows_copy = pltpu.make_async_copy(
@@ -378,8 +378,8 @@
             total = jnp.dot(rows[...], weight[index, block], preferred_element_type=jnp.float32)
             here = pl.ds(pl.multiple_of(block * column, column), column)
             if carried:
-                total = total + carry[index][0, :, here]
-            outs[index][0, :, here] = total.astype(outs[index].dtype)
+                total = total + carry[index, :, here]
+            out[index, :, here] = total.astype(out.dtype)
             return 0
 
         lax.fori_loop(0, columns, body, 0)
@@ -399,9 +399,9 @@
         ),
         in_specs=[pl.BlockSpec(memory_space=pltpu.SMEM), anywhere]
         + [anywhere] * len(arrays)
-        + ([] if carry is None else [inside] * len(slots)),
-        out_specs=[inside] * len(slots),
-        out_shape=[jax.ShapeDtypeStruct((1, tokens, width), dtype)] * len(slots),
+        + ([] if carry is None else [inside]),
+        out_specs=inside,
+        out_shape=jax.ShapeDtypeStruct((len(slots), tokens, width), dtype),
         scratch_shapes=[
             pltpu.VMEM((tokens, depth), attended.dtype),
             pltpu.VMEM((len(slots), columns, depth, column), attended.dtype),
@@ -411,7 +411,7 @@
         compiler_params=pltpu.CompilerParams(vmem_limit_bytes=VMEM_LIMIT),
         cost_estimate=SMALL,
         name="project",
-    )(place, attended, *arrays, *([] if carry is None else carry))
+    )(place, attended, *arrays, *([] if carry is None else [carry]))
 
 
 def pick_kernel(place, own_hidden, other_hidden, own_gate, other_gate, hidden, gate):
@@ -454,49 +454,37 @@
     )(place, own_hidden, other_hidden, own_gate, other_gate)
 
 
-def mixed_blocks(hidden, gate, first, own_parts, other_parts):
-    return [
-        hidden[index].astype(jnp.float32)
-        + gate[first + index]
-        * (own_part[0].astype(jnp.float32) + other_part[0].astype(jnp.float32))
-        for index, (own_part, other_part) in enumerate(zip(own_parts, other_parts))
-    ]
-
-
-def mix_kernel(hidden, gate, *refs, count):
-    own_parts, other_parts, (mixed_ref, sums_ref) = (
-        refs[:count],
-        refs[count : 2 * count],
-        refs[2 * count :],
-    )
-    first = second = 0.0
-    for index, mixed in enumerate(mixed_blocks(hidden, gate, 0, own_parts, other_parts)):
-        mixed_ref[index] = mixed.astype(jnp.bfloat16)
-        first = first + jnp.sum(mixed, axis=1, keepdims=True)
-        second = second + jnp.sum(mixed * mixed, axis=1, keepdims=True)
+def mixed_block(hidden, gate, own_part, other_part):
+    parts = own_part[0].astype(jnp.float32) + other_part[0].astype(jnp.float32)
+    return hidden[0].astype(jnp.float32) + gate * parts
+
+
+def mix_kernel(hidden, gate, own_part, other_part, mixed_ref, sums_ref):
+    mixed = mixed_block(hidden, gate[0], own_part, other_part)
+    mixed_ref[0] = mixed.astype(jnp.bfloat16)
+    first = jnp.sum(mixed, axis=1, keepdims=True)
+    second = jnp.sum(mixed * mixed, axis=1, keepdims=True)
     lane = lax.broadcasted_iota(jnp.int32, sums_ref.shape, 1)
     sums_ref[...] = jnp.where(lane == 0, first, jnp.where(lane == 1, second, 0.0))
 
 
-def mix(hidden, gate, own_parts, other_parts):
-    count = len(own_parts)
+def mix(hidden, gate, own_part, other_part):
     _, tokens, width = hidden.shape
     rows = 64 if tokens % 64 == 0 else tokens
     part = pl.BlockSpec((1, rows, width), lambda i: (0, i, 0))
-    several = pl.BlockSpec((count, rows, width), lambda i: (0, i, 0))
     return pl.pallas_call(
-        partial(mix_kernel, count=count),
+        mix_kernel,
         grid=(tokens // rows,),
-        in_specs=[several, pl.BlockSpec(gate.shape, lambda i: (0, 0, 0))] + [part] * (2 * count),
-        out_specs=[several, pl.BlockSpec((rows, LANES), lambda i: (i, 0))],
+        in_specs=[part, pl.BlockSpec(gate.shape, lambda i: (0, 0, 0)), part, part],
+        out_specs=[part, pl.BlockSpec((rows, LANES), lambda i: (i, 0))],
         out_shape=[
-            jax.ShapeDtypeStruct((count, tokens, width), jnp.bfloat16),
+            jax.ShapeDtypeStruct((1, tokens, width), jnp.bfloat16),
             jax.ShapeDtypeStruct((tokens, LANES), jnp.float32),
         ],
         compiler_params=kernel_params(),
         cost_estimate=SMALL,
         name="mix",
-    )(hidden, gate, *own_parts, *other_parts)
+    )(hidden, gate, own_part, other_part)
 
 
 def finish_kernel(place, gate, scale, shift_by, sums, early, *refs, count, blocks):
@@ -504,11 +492,8 @@
     residual, ffn = refs[3 * count :]
     width = early.shape[2]
     late = [
-        block
+        mixed_block(hidden[index], gate[1 + index], own_parts[index], other_parts[index])
         for index in range(count)
-        for block in mixed_blocks(
-            hidden[index], gate, 1 + index, own_parts[index : index + 1], other_parts[index : index + 1]
-        )
     ]
     first = sums[:, 0:1]
     second = sums[:, 1:2]
@@ -530,16 +515,16 @@
 
 
 def finish(place, hidden, gate, scale, shift_by, sums, early, own_parts, other_parts):
-    count = len(own_parts)
+    count = own_parts.shape[0]
     _, tokens, width = hidden.shape
     blocks = place.shape[0]
     rows = 64 if tokens % 64 == 0 else tokens
     part = pl.BlockSpec((1, rows, width), lambda i, place: (0, i, 0))
     whole = pl.BlockSpec((1, blocks * width), lambda i, place: (0, 0))
     row = pl.BlockSpec((rows, blocks * width), lambda i, place: (i, 0))
-    later = [
-        pl.BlockSpec((1, rows, width), lambda i, place, index=index: (1 + index, i, 0))
-        for index in range(count)
+    parts = [
+        pl.BlockSpec((1, rows, width), lambda i, place, index=index: (index, i, 0))
+        for index in range(count + 1)
     ]
     return pl.pallas_call(
         partial(finish_kernel, count=count, blocks=blocks),
@@ -548,15 +533,18 @@
             grid=(tokens // rows,),
             in_specs=[pl.BlockSpec(gate.shape, lambda i, place: (0, 0, 0)), whole, whole]
             + [pl.BlockSpec((rows, LANES), lambda i, place: (i, 0)), part]
-            + later
-            + [part] * (2 * count),
+            + parts[1:]
+            + parts[:-1] * 2,
             out_specs=[row, row],
         ),
         out_shape=[jax.ShapeDtypeStruct((tokens, blocks * width), jnp.bfloat16)] * 2,
         compiler_params=kernel_params(),
         cost_estimate=SMALL,
         name="finish",
-    )(place, gate, scale, shift_by, sums, early, *[hidden] * count, *own_parts, *other_parts)
+    )(
+        *(place, gate, scale, shift_by, sums, early),
+        *([hidden] * count + [own_parts] * count + [other_parts] * count),
+    )
 
 
 def shift(block, axis, step):
@@ -649,26 +637,27 @@
 
     mine = lax.optimization_barrier(share(ha))
     first = turn(mine, "wa", 1)
+    third = turn(mine, "wa", -1)
     tokens = Tokens(queries, keys_values, windows, 4)
     vector = tokens.plan.vector
     top, bottom = tokens.halos(tokens.edge_rows(vector, 0))
     queries = tokens.leaving(vector, 0)
+
+    first, top, bottom, vector, queries = together(first, top, bottom, vector, queries)
+    first_x = swap(first, "ha", 1)
+    first_y = swap(first, "ha", 2)
     from_left = shift(queries, "wa", 1)
     from_right = shift(queries, "wa", -1)
-
-    first, top, bottom, vector, mine = together(first, top, bottom, vector, mine)
-    first_x = swap(first, "ha", 1)
-    first_y = swap(first, "ha", 2)
-    third = turn(mine, "wa", -1)
     halos = top, bottom, *tokens.rest_halos(vector)
     near = tokens.stay(vector, halos)
 
-    near, first_x, first_y, third, from_left, from_right, first, gate, hidden = together(
-        near, first_x, first_y, third, from_left, from_right, first, picked[0:1], hidden
+    near, first_x, first_y, third, first, gate, hidden = together(
+        near, first_x, first_y, third, first, picked[0:1], hidden
     )
     third_x = swap(third, "ha", 1)
     third_y = swap(third, "ha", 2)
     second = turn(first, "wa", 1)
+    from_left, from_right, gate, hidden = together(from_left, from_right, gate, hidden)
     other_gate = swap(gate, "ta", 1)
     other_hidden = swap(hidden, "ta", 1)
     for_left, for_right = tokens.visit(vector, (from_left, from_right), halos)
@@ -696,10 +685,13 @@
     left, right, base, gates = together(left, right, base, gates)
     attended = tokens.combine(vector, near, [left, right, *rest_sides])
 
-    second_x, second_y, first_y, attended = together(second_x, second_y, first_y, attended)
+    far = lax.optimization_barrier(share(ha ^ 3))
+    second_x, second_y, first_y, far, attended = together(
+        second_x, second_y, first_y, far, attended
+    )
     first_far = swap(first_y, "ha", 1)
     second_far = swap(second_x, "ha", 2)
-    third_far = turn(share(ha ^ 3), "wa", -1)
+    third_far = turn(far, "wa", -1)
 
     turned = ha.reshape(1)
     sums = project(
@@ -711,7 +703,7 @@
         0,
         jnp.bfloat16,
     )
-    other_sums = [swap(part, "ta", 1) for part in sums]
+    other_sums = swap(sums, "ta", 1)
     late = project(
         turned,
         attended,
@@ -723,8 +715,8 @@
     )
     early, totals = mix(base, gates, sums, other_sums)
 
-    first_far, second_far, third_far, early, totals, *late = together(
-        first_far, second_far, third_far, early, totals, *late
+    first_far, second_far, third_far, early, totals, late = together(
+        first_far, second_far, third_far, early, totals, late
     )
     late = project(
         turned,
@@ -735,7 +727,7 @@
         3 * depth,
         jnp.bfloat16,
     )
-    other_late = [swap(part, "ta", 1) for part in late]
+    other_late = swap(late, "ta", 1)
     place = jnp.stack(
         [lax.rem(wa - ta * blocks - block + 2 * n_wa, n_wa) for block in range(blocks)]
     )

time: 270 us -> 253 us (0.937)
  starting transfers between devices: 67.8 us -> 44.5 us
  waiting for transfers between devices: 79.4 us -> 90.7 us
    ppermute x14 -> x12, starting transfers between devices: 47.8 us -> 26.7 us  [swap(): return lax.ppermute(block, axis, [(i, i ^ bit) for i in range(count)])]
    ppermute x6, waiting for transfers between devices: 50 us -> 66.7 us  [shift(): return lax.ppermute(block, axis, pairs)]
    ppermute x4, waiting for transfers between devices: 14.6 us -> 0.74 us  [turn(): lax.ppermute(block, axis, [(i, (i + step) % count) for i in range(count)])]
    ppermute x14 -> x12, waiting for transfers between devices: 14.9 us -> 23.2 us  [swap(): return lax.ppermute(block, axis, [(i, i ^ bit) for i in range(count)])]
    unnamed x36 -> x30, local copies, waits for them, and re-layouts: 10.2 us -> 7.52 us
  transfers between devices with their start and end apart: 24 -> 22, of which waited for: 10 -> 9; matrix products, arithmetic and copies ran while one was open for 3% -> 3% of each run, Pallas kernels for 30% -> 31%
where the time goes in v4:
time: 253 us; the launch traced here: 251 us
  Pallas kernels  91.4 us (36%)
  waiting for transfers between devices  90.7 us (36%)
  starting transfers between devices  44.5 us (18%)
  local copies, waits for them, and re-layouts  17.2 us (7%)
  blocking collectives  3.64 us (1%)
  between operations  2.87 us (1%)
    ppermute x6, waiting for transfers between devices, shift(): return lax.ppermute(block, axis, pairs)  66.7 us
    pallas_call x2, Pallas kernels, attention(): pl.pallas_call(partial(attention_kernel, plan=plan, head_of=head_of, q_co...  49.3 us
    ppermute x12, starting transfers between devices, swap(): return lax.ppermute(block, axis, [(i, i ^ bit) for i in range(count)])  26.7 us
    ppermute x12, waiting for transfers between devices, swap(): return lax.ppermute(block, axis, [(i, i ^ bit) for i in range(count)])  23.2 us
    pallas_call x3, Pallas kernels, project(): pl.pallas_call(partial(project_kernel, slots=slots, carried=carry is not...  20.2 us
    ppermute x6, starting transfers between devices, shift(): return lax.ppermute(block, axis, pairs)  16.3 us
    pallas_call x1, Pallas kernels, combine(): pl.pallas_call(partial(combine_kernel, plan=plan, heads=heads), grid_spec...  8.24 us
    pallas_call x1, Pallas kernels, finish(): pl.pallas_call(partial(finish_kernel, count=count, blocks=blocks), grid_s...  7.56 us
  transfers between devices with their start and end apart: 22, of which 9 were waited for; matrix products, arithmetic and copies ran while one was open for 3% of the time, Pallas kernels for 31%

profile of v4, /device:TPU:17, one launch (start us, length us, event | category | flops | bytes accessed | tf_op | source)
XLA Modules:
  0.0 251.5 jit_solution(235377517819216166)
XLA Ops:
  0.7 3.8 %constant_dynamic-slice_fusion = (bf16[640,1280]{1,0:T(8,128)(2,1)}, bf16[640,1280]{1,0:T(8,128)(2,1)}) fusion(bf16[2560,1280]{1,0:T(8,128)(2,1)} %refs_0_.1, s32[]{:T(128)S(6)} %select_n.40, s32[]{:T(128)S(6)} %select_n.32), kind=kLoop, calls=%fused_computation.9 | loop fusion | bytes 6553608 | tf_op jit(solution)/shard_map/dynamic_slice | solution.py:636
  7.3 2.4 pack.6
  9.7 4.1 %collective-permute-start.7 = (bf16[2,2,64,1792]{3,2,1,0:T(8,128)(2,1)S(1)}, bf16[2,2,64,1792]{3,2,1,0:T(8,128)(2,1)}, u32[]{:S(2)}, u32[]{:S(2)}) collective-permute-start(bf16[2,2,64,1792]{3,2,1,0:T(8,128)(2,1)S(1)} %get-tuple-element.87), channel_id=1, source_target_pairs={{0,8},{8,16},{16,24},{1,9},{9,17},{17,25},{2,10},{10,18},{18,26},{... | collective-permute-start | bytes 2752520 | tf_op jit(solution)/shard_map/ppermute | solution.py:553
  16.4 3.6 %pmax.7 = f32[2]{0:T(128)S(1)} all-reduce(f32[2]{0:T(128)S(1)} %subtract_reduce_fusion), channel_id=1, replica_groups=mesh['ha'=4,'wa'=4,'ta'=2] {'ta'}, use_global_device_ids=true, to_apply=%region_3.4 | all-reduce | flops 2 | bytes 16 | tf_op jit(solution)/shard_map/pmax | solution.py:48
  22.9 8.6 %collective-permute-done.7.refs_2_.refs_3_ = bf16[2,2,64,1792]{3,2,1,0:T(8,128)(2,1)} collective-permute-done((bf16[2,2,64,1792]{3,2,1,0:T(8,128)(2,1)S(1)}, bf16[2,2,64,1792]{3,2,1,0:T(8,128)(2,1)}, u32[]{:S(2)}, u32[]{:S(2)}) %collective-permute-start.7) | collective-permute-done | bytes 917536 | tf_op jit(solution)/shard_map/ppermute | solution.py:553
  31.5 21.7 %collective-permute-done.8.refs_3_.refs_4_ = bf16[2,2,64,1792]{3,2,1,0:T(8,128)(2,1)} collective-permute-done((bf16[2,2,64,1792]{3,2,1,0:T(8,128)(2,1)S(1)}, bf16[2,2,64,1792]{3,2,1,0:T(8,128)(2,1)}, u32[]{:S(2)}, u32[]{:S(2)}) %collective-permute-start.8) | collective-permute-done | bytes 917536 | tf_op jit(solution)/shard_map/ppermute | solution.py:553
  58.1 3.3 %collective-permute-start.9 = (bf16[2,192,1792]{2,1,0:T(8,128)(2,1)S(1)}, bf16[2,192,1792]{2,1,0:T(8,128)(2,1)S(1)}, u32[]{:S(2)}, u32[]{:S(2)}) collective-permute-start(bf16[2,192,1792]{2,1,0:T(8,128)(2,1)S(1)} %pack.7), channel_id=1, source_target_pairs={{0,2},{2,4},{4,6},{1,3},{3,5},{5,7},{8,10},{10,12},{12,14},{9,11},... | collective-permute-start | bytes 4128776 | tf_op jit(solution)/shard_map/ppermute | solution.py:553
  61.4 23.2 %attend_own.1.own.own_stat = bf16[2,192,2688]{2,1,0:T(8,128)(2,1)S(1)} custom-call(s32[125]{0:T(128)S(1)} %concatenate.10.vector, bf16[2,192,2560]{2,1,0:T(8,128)(2,1)} %bitcast.51, bf16[2,2,192,2560]{3,2,1,0:T(8,128)(2,1)} %bitcast.48, bf16[2,2,64,1792]{3,2,1,0:T(8,128)(2,1)} %collective-permute-done.7.refs_2_.refs_3_, ...), custom_call_target="tpu_custom_call" | custom-call | flops 20000000000 | bytes 1 | tf_op jit(solution)/shard_map/attend_own/pallas_call | solution.py:251
  86.0 12.2 %collective-permute-done.10.refs_1_ = bf16[2,192,1792]{2,1,0:T(8,128)(2,1)S(1)} collective-permute-done((bf16[2,192,1792]{2,1,0:T(8,128)(2,1)S(1)}, bf16[2,192,1792]{2,1,0:T(8,128)(2,1)S(1)}, u32[]{:S(2)}, u32[]{:S(2)}) %collective-permute-start.10) | collective-permute-done | bytes 1376288 | tf_op jit(solution)/shard_map/ppermute | solution.py:553
  98.1 13.7 %collective-permute-start.15 = (bf16[384,2560]{1,0:T(8,128)(2,1)S(1)}, bf16[384,2560]{1,0:T(8,128)(2,1)S(1)}, u32[]{:S(2)}, u32[]{:S(2)}) collective-permute-start(bf16[384,2560]{1,0:T(8,128)(2,1)S(1)} %bitcast.44), channel_id=1, source_target_pairs={{0,1},{1,0},{2,3},{3,2},{4,5},{5,4},{6,7},{7,6},{8,9},{9,8},{10,11... | collective-permute-start | bytes 5898248 | tf_op jit(solution)/shard_map/ppermute | solution.py:563
  113.0 26.2 %attend_visitors.3 = (bf16[2,192,1920]{2,1,0:T(8,128)(2,1)}, bf16[2,192,1920]{2,1,0:T(8,128)(2,1)}) custom-call(s32[125]{0:T(128)S(1)} %concatenate.10.vector, bf16[2,192,1792]{2,1,0:T(8,128)(2,1)S(1)} %collective-permute-done.9.refs_0_, bf16[2,192,1792]{2,1,0:T(8,128)(2,1)S(1)} %collective-permute-done.10.refs_1_, bf16[2,2,192,2560]{3,2,1,0:T(8,128)(2,1)S(1)} %bitcast.50, ...), custom_call_target="tpu_custom_call" | custom-call | flops 1 | bytes 1 | tf_op jit(solution)/shard_map/attend_visitors/pallas_call | solution.py:251
  140.5 2.9 %collective-permute-start.16 = (bf16[2,192,1920]{2,1,0:T(8,128)(2,1)}, bf16[2,192,1920]{2,1,0:T(8,128)(2,1)}, u32[]{:S(2)}, u32[]{:S(2)}) collective-permute-start(bf16[2,192,1920]{2,1,0:T(8,128)(2,1)} %get-tuple-element.104), channel_id=1, source_target_pairs={{0,2},{2,4},{4,6},{1,3},{3,5},{5,7},{8,10},{10,12},{12,14},{9,11},... | collective-permute-start | bytes 4423688 | tf_op jit(solution)/shard_map/ppermute | solution.py:553
  143.4 2.7 %collective-permute-start.17 = (bf16[2,192,1920]{2,1,0:T(8,128)(2,1)}, bf16[2,192,1920]{2,1,0:T(8,128)(2,1)}, u32[]{:S(2)}, u32[]{:S(2)}) collective-permute-start(bf16[2,192,1920]{2,1,0:T(8,128)(2,1)} %get-tuple-element.105), channel_id=1, source_target_pairs={{2,0},{4,2},{6,4},{3,1},{5,3},{7,5},{10,8},{12,10},{14,12},{11,9},... | collective-permute-start | bytes 4423688 | tf_op jit(solution)/shard_map/ppermute | solution.py:553
  147.1 2.5 collective-permute-done.18.refs_7_
  156.8 24.2 %collective-permute-done.16.left = bf16[2,192,1920]{2,1,0:T(8,128)(2,1)} collective-permute-done((bf16[2,192,1920]{2,1,0:T(8,128)(2,1)}, bf16[2,192,1920]{2,1,0:T(8,128)(2,1)}, u32[]{:S(2)}, u32[]{:S(2)}) %collective-permute-start.16) | collective-permute-done | bytes 1474592 | tf_op jit(solution)/shard_map/ppermute | solution.py:553
  181.0 8.2 %combine.1 = bf16[2,192,2560]{2,1,0:T(8,128)(2,1)S(1)} custom-call(s32[125]{0:T(128)S(1)} %concatenate.10.vector, bf16[2,192,2688]{2,1,0:T(8,128)(2,1)S(1)} %copy-done.8, bf16[2,192,2688]{2,1,0:T(8,128)(2,1)S(1)} %copy-done.8, bf16[2,192,1920]{2,1,0:T(8,128)(2,1)} %collective-permute-done.16.left, bf16[2,192,1920]{2,1,0:T(8,128)(2,1)} %collective-permute-done.17.right, ...), custom_call_target="tpu_custom_call" | custom-call | flops 20000000000 | bytes 1 | tf_op jit(solution)/shard_map/combine/pallas_call | solution.py:328
  191.8 4.5 %project.3.own_part = bf16[1,384,1280]{2,1,0:T(8,128)(2,1)S(1)} custom-call(s32[1]{0:T(128)} %bitcast.7.place, bf16[384,2560]{1,0:T(8,128)(2,1)S(1)} %bitcast.39, bf16[2560,1280]{1,0:T(8,128)(2,1)S(1)} %bitcast.43), custom_call_target="tpu_custom_call" | custom-call | flops 1 | bytes 1 | tf_op jit(solution)/shard_map/project/pallas_call | solution.py:396
  196.3 2.5 collective-permute-start.26
  198.8 10.4 %project.4.refs_3_ = f32[3,384,1280]{2,1,0:T(8,128)S(1)} custom-call(s32[1]{0:T(128)} %bitcast.7.place, bf16[384,2560]{1,0:T(8,128)(2,1)S(1)} %bitcast.40, bf16[640,1280]{1,0:T(8,128)(2,1)} %collective-permute-done.6.refs_0_, bf16[640,1280]{1,0:T(8,128)(2,1)} %collective-permute-done.11.refs_1_, bf16[640,1280]{1,0:T(8,128)(2,1)} %collective-permute-done.12.refs_2_, ...), custom_call_target="tpu_custom_call" | custom-call | flops 1 | bytes 1 | tf_op jit(solution)/shard_map/project/pallas_call | solution.py:396
  210.3 14.7 %collective-permute-done.23.refs_0_ = bf16[640,1280]{1,0:T(8,128)(2,1)S(1)} collective-permute-done((bf16[640,1280]{1,0:T(8,128)(2,1)}, bf16[640,1280]{1,0:T(8,128)(2,1)S(1)}, u32[]{:S(2)}, u32[]{:S(2)}) %collective-permute-start.23) | collective-permute-done | bytes 1638432 | tf_op jit(solution)/shard_map/ppermute | solution.py:563
  226.7 5.4 %project.5.refs_3_.refs_4_.refs_5_ = bf16[3,384,1280]{2,1,0:T(8,128)(2,1)S(1)} custom-call(s32[1]{0:T(128)} %bitcast.7.place, bf16[384,2560]{1,0:T(8,128)(2,1)S(1)} %bitcast.41, bf16[640,1280]{1,0:T(8,128)(2,1)S(1)} %collective-permute-done.23.refs_0_, bf16[640,1280]{1,0:T(8,128)(2,1)S(1)} %collective-permute-done.24.refs_1_, ...), custom_call_target="tpu_custom_call" | custom-call | flops 1 | bytes 1 | tf_op jit(solution)/shard_map/project/pallas_call | solution.py:396
  232.1 3.4 %collective-permute-start.27 = (bf16[3,384,1280]{2,1,0:T(8,128)(2,1)S(1)}, bf16[3,384,1280]{2,1,0:T(8,128)(2,1)}, u32[]{:S(2)}, u32[]{:S(2)}) collective-permute-start(bf16[3,384,1280]{2,1,0:T(8,128)(2,1)S(1)} %project.5.refs_3_.refs_4_.refs_5_), channel_id=1, source_target_pairs={{0,1},{1,0},{2,3},{3,2},{4,5},{5,4},{6,7},{7,6},{8,9},{9,8},{10,11... | collective-permute-start | bytes 8847368 | tf_op jit(solution)/shard_map/ppermute | solution.py:563
  235.6 5.1 %collective-permute-done.27.refs_6_.refs_7_.refs_8_ = bf16[3,384,1280]{2,1,0:T(8,128)(2,1)} collective-permute-done((bf16[3,384,1280]{2,1,0:T(8,128)(2,1)S(1)}, bf16[3,384,1280]{2,1,0:T(8,128)(2,1)}, u32[]{:S(2)}, u32[]{:S(2)}) %collective-permute-start.27) | collective-permute-done | bytes 2949152 | tf_op jit(solution)/shard_map/ppermute | solution.py:563
  243.9 7.6 %finish.1 = (bf16[384,2560]{1,0:T(8,128)(2,1)}, bf16[384,2560]{1,0:T(8,128)(2,1)}) custom-call(s32[2]{0:T(128)S(1)} %pad_add_fusion.1.place, f32[4,1,1280]{2,1,0:T(1,128)S(1)} %get-tuple-element.113.gate, f32[1,2560]{1,0:T(1,128)S(1)} %get-tuple-element.144.scale, f32[1,2560]{1,0:T(1,128)S(1)} %get-tuple-element.143.shift_by, ...), custom_call_target="tpu_custom_call" | custom-call | flops 1 | bytes 1 | tf_op jit(solution)/shard_map/finish/pallas_call | solution.py:529
  (89 shorter events, 35.3 us)
Async XLA Ops:
  4.5 48.7 %collective-permute-start.6 = (bf16[640,1280]{1,0:T(8,128)(2,1)}, bf16[640,1280]{1,0:T(8,128)(2,1)}, u32[]{:S(2)}, u32[]{:S(2)}) collective-permute-start(bf16[640,1280]{1,0:T(8,128)(2,1)} %get-tuple-element.142), channel_id=1, source_target_pairs={{0,2},{2,4},{4,6},{6,0},{1,3},{3,5},{5,7},{7,1},{8,10},{10,12},{12... | collective-permute-start | bytes 4915208 | tf_op jit(solution)/shard_map/ppermute | solution.py:558
  9.7 21.8 %collective-permute-start.7 = (bf16[2,2,64,1792]{3,2,1,0:T(8,128)(2,1)S(1)}, bf16[2,2,64,1792]{3,2,1,0:T(8,128)(2,1)}, u32[]{:S(2)}, u32[]{:S(2)}) collective-permute-start(bf16[2,2,64,1792]{3,2,1,0:T(8,128)(2,1)S(1)} %get-tuple-element.87), channel_id=1, source_target_pairs={{0,8},{8,16},{16,24},{1,9},{9,17},{17,25},{2,10},{10,18},{18,26},{... | collective-permute-start | bytes 2752520 | tf_op jit(solution)/shard_map/ppermute | solution.py:553
  13.8 39.5 %collective-permute-start.8 = (bf16[2,2,64,1792]{3,2,1,0:T(8,128)(2,1)S(1)}, bf16[2,2,64,1792]{3,2,1,0:T(8,128)(2,1)}, u32[]{:S(2)}, u32[]{:S(2)}) collective-permute-start(bf16[2,2,64,1792]{3,2,1,0:T(8,128)(2,1)S(1)} %get-tuple-element.88), channel_id=1, source_target_pairs={{8,0},{16,8},{24,16},{9,1},{17,9},{25,17},{10,2},{18,10},{26,18},{... | collective-permute-start | bytes 2752520 | tf_op jit(solution)/shard_map/ppermute | solution.py:553
  15.1 70.9 %collective-permute-start.13 = (bf16[640,1280]{1,0:T(8,128)(2,1)}, bf16[640,1280]{1,0:T(8,128)(2,1)}, u32[]{:S(2)}, u32[]{:S(2)}) collective-permute-start(bf16[640,1280]{1,0:T(8,128)(2,1)} %get-tuple-element.142), channel_id=1, source_target_pairs={{0,6},{2,0},{4,2},{6,4},{1,7},{3,1},{5,3},{7,5},{8,14},{10,8},{12,... | collective-permute-start | bytes 4915208 | tf_op jit(solution)/shard_map/ppermute | solution.py:558
  53.2 32.7 %collective-permute-start.11 = (bf16[640,1280]{1,0:T(8,128)(2,1)}, bf16[640,1280]{1,0:T(8,128)(2,1)}, u32[]{:S(2)}, u32[]{:S(2)}) collective-permute-start(bf16[640,1280]{1,0:T(8,128)(2,1)} %collective-permute-done.6.refs_0_), channel_id=1, source_target_pairs={{0,8},{8,0},{16,24},{24,16},{1,9},{9,1},{17,25},{25,17},{2,10},{10... | collective-permute-start | bytes 4915208 | tf_op jit(solution)/shard_map/ppermute | solution.py:563
  54.5 31.5 %collective-permute-start.12 = (bf16[640,1280]{1,0:T(8,128)(2,1)}, bf16[640,1280]{1,0:T(8,128)(2,1)}, u32[]{:S(2)}, u32[]{:S(2)}) collective-permute-start(bf16[640,1280]{1,0:T(8,128)(2,1)} %collective-permute-done.6.refs_0_), channel_id=1, source_target_pairs={{0,16},{8,24},{16,0},{24,8},{1,17},{9,25},{17,1},{25,9},{2,18},{10... | collective-permute-start | bytes 4915208 | tf_op jit(solution)/shard_map/ppermute | solution.py:563
  56.0 42.1 %collective-permute-start.10 = (bf16[2,192,1792]{2,1,0:T(8,128)(2,1)S(1)}, bf16[2,192,1792]{2,1,0:T(8,128)(2,1)S(1)}, u32[]{:S(2)}, u32[]{:S(2)}) collective-permute-start(bf16[2,192,1792]{2,1,0:T(8,128)(2,1)S(1)} %pack.7), channel_id=1, source_target_pairs={{2,0},{4,2},{6,4},{3,1},{5,3},{7,5},{10,8},{12,10},{14,12},{11,9},... | collective-permute-start | bytes 4128776 | tf_op jit(solution)/shard_map/ppermute | solution.py:553
  58.1 40.0 %collective-permute-start.9 = (bf16[2,192,1792]{2,1,0:T(8,128)(2,1)S(1)}, bf16[2,192,1792]{2,1,0:T(8,128)(2,1)S(1)}, u32[]{:S(2)}, u32[]{:S(2)}) collective-permute-start(bf16[2,192,1792]{2,1,0:T(8,128)(2,1)S(1)} %pack.7), channel_id=1, source_target_pairs={{0,2},{2,4},{4,6},{1,3},{3,5},{5,7},{8,10},{10,12},{12,14},{9,11},... | collective-permute-start | bytes 4128776 | tf_op jit(solution)/shard_map/ppermute | solution.py:553
  61.4 51.6 %copy-start.9 = (bf16[2,2,24,8,2560]{4,3,2,1,0:T(8,128)(2,1)S(1)}, bf16[2,2,24,8,2560]{4,3,2,1,0:T(8,128)(2,1)}, u32[]{:S(2)}) copy-start(bf16[2,2,24,8,2560]{4,3,2,1,0:T(8,128)(2,1)} %param.13) | copy-start | bytes 11796484
  98.1 41.1 %collective-permute-start.15 = (bf16[384,2560]{1,0:T(8,128)(2,1)S(1)}, bf16[384,2560]{1,0:T(8,128)(2,1)S(1)}, u32[]{:S(2)}, u32[]{:S(2)}) collective-permute-start(bf16[384,2560]{1,0:T(8,128)(2,1)S(1)} %bitcast.44), channel_id=1, source_target_pairs={{0,1},{1,0},{2,3},{3,2},{4,5},{5,4},{6,7},{7,6},{8,9},{9,8},{10,11... | collective-permute-start | bytes 5898248 | tf_op jit(solution)/shard_map/ppermute | solution.py:563
  111.9 37.7 %collective-permute-start.18 = (bf16[640,1280]{1,0:T(8,128)(2,1)}, bf16[640,1280]{1,0:T(8,128)(2,1)}, u32[]{:S(2)}, u32[]{:S(2)}) collective-permute-start(bf16[640,1280]{1,0:T(8,128)(2,1)} %collective-permute-done.13.refs_6_), channel_id=1, source_target_pairs={{0,8},{8,0},{16,24},{24,16},{1,9},{9,1},{17,25},{25,17},{2,10},{10... | collective-permute-start | bytes 4915208 | tf_op jit(solution)/shard_map/ppermute | solution.py:563
  112.1 37.4 %collective-permute-start.19 = (bf16[640,1280]{1,0:T(8,128)(2,1)}, bf16[640,1280]{1,0:T(8,128)(2,1)}, u32[]{:S(2)}, u32[]{:S(2)}) collective-permute-start(bf16[640,1280]{1,0:T(8,128)(2,1)} %collective-permute-done.13.refs_6_), channel_id=1, source_target_pairs={{0,16},{8,24},{16,0},{24,8},{1,17},{9,25},{17,1},{25,9},{2,18},{10... | collective-permute-start | bytes 4915208 | tf_op jit(solution)/shard_map/ppermute | solution.py:563
  112.4 37.2 %collective-permute-start.20 = (bf16[640,1280]{1,0:T(8,128)(2,1)}, bf16[640,1280]{1,0:T(8,128)(2,1)}, u32[]{:S(2)}, u32[]{:S(2)}) collective-permute-start(bf16[640,1280]{1,0:T(8,128)(2,1)} %collective-permute-done.6.refs_0_), channel_id=1, source_target_pairs={{0,2},{2,4},{4,6},{6,0},{1,3},{3,5},{5,7},{7,1},{8,10},{10,12},{12... | collective-permute-start | bytes 4915208 | tf_op jit(solution)/shard_map/ppermute | solution.py:558
  112.4 26.8 %collective-permute-start.14 = (f32[1,2560]{1,0:T(1,128)S(1)}, f32[1,2560]{1,0:T(1,128)S(1)}, u32[]{:S(2)}, u32[]{:S(2)}) collective-permute-start(f32[1,2560]{1,0:T(1,128)S(1)} %get-tuple-element.102.own_gate), channel_id=1, source_target_pairs={{0,1},{1,0},{2,3},{3,2},{4,5},{5,4},{6,7},{7,6},{8,9},{9,8},{10,11... | collective-permute-start | bytes 30728 | tf_op jit(solution)/shard_map/ppermute | solution.py:563
  140.5 40.5 %collective-permute-start.16 = (bf16[2,192,1920]{2,1,0:T(8,128)(2,1)}, bf16[2,192,1920]{2,1,0:T(8,128)(2,1)}, u32[]{:S(2)}, u32[]{:S(2)}) collective-permute-start(bf16[2,192,1920]{2,1,0:T(8,128)(2,1)} %get-tuple-element.104), channel_id=1, source_target_pairs={{0,2},{2,4},{4,6},{1,3},{3,5},{5,7},{8,10},{10,12},{12,14},{9,11},... | collective-permute-start | bytes 4423688 | tf_op jit(solution)/shard_map/ppermute | solution.py:553
  143.4 37.6 %collective-permute-start.17 = (bf16[2,192,1920]{2,1,0:T(8,128)(2,1)}, bf16[2,192,1920]{2,1,0:T(8,128)(2,1)}, u32[]{:S(2)}, u32[]{:S(2)}) collective-permute-start(bf16[2,192,1920]{2,1,0:T(8,128)(2,1)} %get-tuple-element.105), channel_id=1, source_target_pairs={{2,0},{4,2},{6,4},{3,1},{5,3},{7,5},{10,8},{12,10},{14,12},{11,9},... | collective-permute-start | bytes 4423688 | tf_op jit(solution)/shard_map/ppermute | solution.py:553
  149.6 39.7 %collective-permute-start.21 = (bf16[640,1280]{1,0:T(8,128)(2,1)}, bf16[640,1280]{1,0:T(8,128)(2,1)}, u32[]{:S(2)}, u32[]{:S(2)}) collective-permute-start(bf16[640,1280]{1,0:T(8,128)(2,1)} %collective-permute-done.20.refs_3_), channel_id=1, source_target_pairs={{0,8},{8,0},{16,24},{24,16},{1,9},{9,1},{17,25},{25,17},{2,10},{10... | collective-permute-start | bytes 4915208 | tf_op jit(solution)/shard_map/ppermute | solution.py:563
  152.6 36.7 %collective-permute-start.22 = (bf16[640,1280]{1,0:T(8,128)(2,1)}, bf16[640,1280]{1,0:T(8,128)(2,1)S(1)}, u32[]{:S(2)}, u32[]{:S(2)}) collective-permute-start(bf16[640,1280]{1,0:T(8,128)(2,1)} %collective-permute-done.20.refs_3_), channel_id=1, source_target_pairs={{0,16},{8,24},{16,0},{24,8},{1,17},{9,25},{17,1},{25,9},{2,18},{10... | collective-permute-start | bytes 4915208 | tf_op jit(solution)/shard_map/ppermute | solution.py:563
  156.8 52.4 %copy-start = (bf16[4,384,1280]{2,1,0:T(8,128)(2,1)}, bf16[4,384,1280]{2,1,0:T(8,128)(2,1)S(1)}, u32[]{:S(2)}) copy-start(bf16[4,384,1280]{2,1,0:T(8,128)(2,1)S(1)} %get-tuple-element.125.hidden.refs_0_.refs_1_.refs_2_) | copy-start | bytes 11796484
  189.3 35.7 %collective-permute-start.23 = (bf16[640,1280]{1,0:T(8,128)(2,1)}, bf16[640,1280]{1,0:T(8,128)(2,1)S(1)}, u32[]{:S(2)}, u32[]{:S(2)}) collective-permute-start(bf16[640,1280]{1,0:T(8,128)(2,1)} %collective-permute-done.12.refs_2_), channel_id=1, source_target_pairs={{0,8},{8,0},{16,24},{24,16},{1,9},{9,1},{17,25},{25,17},{2,10},{10... | collective-permute-start | bytes 4915208 | tf_op jit(solution)/shard_map/ppermute | solution.py:563
  190.6 35.4 %collective-permute-start.24 = (bf16[640,1280]{1,0:T(8,128)(2,1)}, bf16[640,1280]{1,0:T(8,128)(2,1)S(1)}, u32[]{:S(2)}, u32[]{:S(2)}) collective-permute-start(bf16[640,1280]{1,0:T(8,128)(2,1)} %collective-permute-done.21.refs_4_), channel_id=1, source_target_pairs={{0,16},{8,24},{16,0},{24,8},{1,17},{9,25},{17,1},{25,9},{2,18},{10... | collective-permute-start | bytes 4915208 | tf_op jit(solution)/shard_map/ppermute | solution.py:563
  191.8 34.9 %collective-permute-start.25 = (bf16[640,1280]{1,0:T(8,128)(2,1)S(1)}, bf16[640,1280]{1,0:T(8,128)(2,1)S(1)}, u32[]{:S(2)}, u32[]{:S(2)}) collective-permute-start(bf16[640,1280]{1,0:T(8,128)(2,1)S(1)} %copy-done.11), channel_id=1, source_target_pairs={{0,6},{2,0},{4,2},{6,4},{1,7},{3,1},{5,3},{7,5},{8,14},{10,8},{12,... | collective-permute-start | bytes 4915208 | tf_op jit(solution)/shard_map/ppermute | solution.py:558
  196.3 12.8 %collective-permute-start.26 = (bf16[1,384,1280]{2,1,0:T(8,128)(2,1)S(1)}, bf16[1,384,1280]{2,1,0:T(8,128)(2,1)S(1)}, u32[]{:S(2)}, u32[]{:S(2)}) collective-permute-start(bf16[1,384,1280]{2,1,0:T(8,128)(2,1)S(1)} %project.3.own_part), channel_id=1, source_target_pairs={{0,1},{1,0},{2,3},{3,2},{4,5},{5,4},{6,7},{7,6},{8,9},{9,8},{10,11... | collective-permute-start | bytes 2949128 | tf_op jit(solution)/shard_map/ppermute | solution.py:563
  232.1 8.5 %collective-permute-start.27 = (bf16[3,384,1280]{2,1,0:T(8,128)(2,1)S(1)}, bf16[3,384,1280]{2,1,0:T(8,128)(2,1)}, u32[]{:S(2)}, u32[]{:S(2)}) collective-permute-start(bf16[3,384,1280]{2,1,0:T(8,128)(2,1)S(1)} %project.5.refs_3_.refs_4_.refs_5_), channel_id=1, source_target_pairs={{0,1},{1,0},{2,3},{3,2},{4,5},{5,4},{6,7},{7,6},{8,9},{9,8},{10,11... | collective-permute-start | bytes 8847368 | tf_op jit(solution)/shard_map/ppermute | solution.py:563
  (13 other events, 137.4 us)

commit v5 on v4

--- a/solution.py
+++ b/solution.py
@@ -637,13 +637,19 @@
 
     mine = lax.optimization_barrier(share(ha))
     first = turn(mine, "wa", 1)
-    third = turn(mine, "wa", -1)
+    gate = picked[0:1]
+    other_gate = swap(gate, "ta", 1)
     tokens = Tokens(queries, keys_values, windows, 4)
     vector = tokens.plan.vector
     top, bottom = tokens.halos(tokens.edge_rows(vector, 0))
     queries = tokens.leaving(vector, 0)
 
-    first, top, bottom, vector, queries = together(first, top, bottom, vector, queries)
+    top, mine = together(top, mine)
+    third = turn(mine, "wa", -1)
+
+    first, top, bottom, other_gate, vector, queries = together(
+        first, top, bottom, other_gate, vector, queries
+    )
     first_x = swap(first, "ha", 1)
     first_y = swap(first, "ha", 2)
     from_left = shift(queries, "wa", 1)
@@ -651,38 +657,21 @@
     halos = top, bottom, *tokens.rest_halos(vector)
     near = tokens.stay(vector, halos)
 
-    near, first_x, first_y, third, first, gate, hidden = together(
-        near, first_x, first_y, third, first, picked[0:1], hidden
-    )
+    near, first_x, first_y, third, first = together(near, first_x, first_y, third, first)
     third_x = swap(third, "ha", 1)
     third_y = swap(third, "ha", 2)
     second = turn(first, "wa", 1)
-    from_left, from_right, gate, hidden = together(from_left, from_right, gate, hidden)
-    other_gate = swap(gate, "ta", 1)
-    other_hidden = swap(hidden, "ta", 1)
     for_left, for_right = tokens.visit(vector, (from_left, from_right), halos)
 
-    for_left, for_right, other_gate, other_hidden = together(
-        for_left, for_right, other_gate, other_hidden
-    )
     left = shift(for_right, "wa", 1)
     right = shift(for_left, "wa", -1)
 
-    third_x, third_y, second, other_gate, vector = together(
-        third_x, third_y, second, other_gate, vector
-    )
+    third_x, third_y, second, vector, hidden = together(third_x, third_y, second, vector, hidden)
     second_x = swap(second, "ha", 1)
     second_y = swap(second, "ha", 2)
+    other_hidden = swap(hidden, "ta", 1)
     rest_sides = tokens.rest_sides(vector, halos)
 
-    def block_of(distance):
-        return lax.rem(wa - distance + n_wa, n_wa)
-
-    owners = jnp.stack([block_of(distance) // blocks == ta for distance in range(n_wa)])
-    inner = jnp.stack([lax.rem(block_of(distance), blocks) for distance in range(n_wa)])
-    place = jnp.stack([owners.astype(jnp.int32), inner], axis=1).reshape(-1)
-    base, gates = pick(place, hidden, other_hidden, gate, other_gate, width)
-    left, right, base, gates = together(left, right, base, gates)
     attended = tokens.combine(vector, near, [left, right, *rest_sides])
 
     far = lax.optimization_barrier(share(ha ^ 3))
@@ -713,6 +702,14 @@
         0,
         jnp.float32,
     )
+    def block_of(distance):
+        return lax.rem(wa - distance + n_wa, n_wa)
+
+    owners = jnp.stack([block_of(distance) // blocks == ta for distance in range(n_wa)])
+    inner = jnp.stack([lax.rem(block_of(distance), blocks) for distance in range(n_wa)])
+    place = jnp.stack([owners.astype(jnp.int32), inner], axis=1).reshape(-1)
+    late, place, other_hidden = together(late, place, other_hidden)
+    base, gates = pick(place, hidden, other_hidden, gate, other_gate, width)
     early, totals = mix(base, gates, sums, other_sums)
 
     first_far, second_far, third_far, early, totals, late = together(

time: 253 us -> 261 us (1.032); the launches traced: 251 us -> 256 us
  waiting for transfers between devices: 90.7 us -> 46.2 us
  starting transfers between devices: 44.5 us -> 73.2 us
  Pallas kernels: 91.4 us -> 104 us
  local copies, waits for them, and re-layouts: 17.2 us -> 25.9 us
    ppermute x6, waiting for transfers between devices: 66.7 us -> 40.9 us  [shift(): return lax.ppermute(block, axis, pairs)]
    ppermute x12, starting transfers between devices: 26.7 us -> 45.7 us  [swap(): return lax.ppermute(block, axis, [(i, i ^ bit) for i in range(count)])]
    ppermute x12, waiting for transfers between devices: 23.2 us -> 5.34 us  [swap(): return lax.ppermute(block, axis, [(i, i ^ bit) for i in range(count)])]
    unnamed x30 -> x46, local copies, waits for them, and re-layouts: 7.52 us -> 16.2 us
    ppermute x6, starting transfers between devices: 16.3 us -> 23.1 us  [shift(): return lax.ppermute(block, axis, pairs)]
    pallas_call x1, Pallas kernels: 1.13 us -> 4.57 us  [mix(): pl.pallas_call(mix_kernel, grid=(tokens // rows,), in_specs=[part, pl.Blo...]
    pallas_call x2, Pallas kernels: 3.36 us -> 6.46 us  [pack(): pl.pallas_call(partial(pack_kernel, head_of=head_of, first=first, rows=ro...]
    pallas_call x1, Pallas kernels: 1.51 us -> 4.45 us  [pick(): pl.pallas_call(pick_kernel, grid_spec=pltpu.PrefetchScalarGridSpec(num_sc...]
  transfers between devices with their start and end apart: 22 -> 22, of which waited for: 9 -> 4; matrix products, arithmetic and copies ran while one was open for 3% -> 3% of each run, Pallas kernels for 31% -> 35%
where the time goes in v5:
time: 261 us; the launch traced here: 256 us
  Pallas kernels  104 us (40%)
  starting transfers between devices  73.2 us (28%)
  waiting for transfers between devices  46.2 us (18%)
  local copies, waits for them, and re-layouts  25.9 us (10%)
  between operations  2.91 us (1%)
    pallas_call x2, Pallas kernels, attention(): pl.pallas_call(partial(attention_kernel, plan=plan, head_of=head_of, q_co...  51.5 us
    ppermute x12, starting transfers between devices, swap(): return lax.ppermute(block, axis, [(i, i ^ bit) for i in range(count)])  45.7 us
    ppermute x6, waiting for transfers between devices, shift(): return lax.ppermute(block, axis, pairs)  40.9 us
    ppermute x6, starting transfers between devices, shift(): return lax.ppermute(block, axis, pairs)  23.1 us
    pallas_call x3, Pallas kernels, project(): pl.pallas_call(partial(project_kernel, slots=slots, carried=carry is not...  21 us
    unnamed x46, local copies, waits for them, and re-layouts  16.2 us
    pallas_call x1, Pallas kernels, combine(): pl.pallas_call(partial(combine_kernel, plan=plan, heads=heads), grid_spec...  8.7 us
    pallas_call x1, Pallas kernels, finish(): pl.pallas_call(partial(finish_kernel, count=count, blocks=blocks), grid_s...  7.61 us
  transfers between devices with their start and end apart: 22, of which 4 were waited for; matrix products, arithmetic and copies ran while one was open for 3% of the time, Pallas kernels for 35%

profile of v5, /device:TPU:17, one launch (start us, length us, event | category | flops | bytes accessed | tf_op | source)
XLA Modules:
  0.0 256.2 jit_solution(17359009034016180417)
XLA Ops:
  0.7 3.8 %constant_dynamic-slice_fusion = (bf16[640,1280]{1,0:T(8,128)(2,1)}, bf16[640,1280]{1,0:T(8,128)(2,1)}) fusion(bf16[2560,1280]{1,0:T(8,128)(2,1)} %refs_0_.1, s32[]{:T(128)S(6)} %select_n.36, s32[]{:T(128)S(6)} %select_n.32), kind=kLoop, calls=%fused_computation.9 | loop fusion | bytes 6553608 | tf_op jit(solution)/shard_map/dynamic_slice | solution.py:636
  7.3 3.3 %pack.6 = (bf16[2,2,64,1792]{3,2,1,0:T(8,128)(2,1)S(1)}, bf16[2,2,64,1792]{3,2,1,0:T(8,128)(2,1)}) custom-call(s32[125]{0:T(128)S(1)} %concatenate.10.vector, bf16[2,2,192,2560]{3,2,1,0:T(8,128)(2,1)} %bitcast.44), custom_call_target="tpu_custom_call" | custom-call | flops 1 | bytes 1 | tf_op jit(solution)/shard_map/pack/pallas_call | solution.py:96
  10.6 4.0 %collective-permute-start.7 = (bf16[2,2,64,1792]{3,2,1,0:T(8,128)(2,1)S(1)}, bf16[2,2,64,1792]{3,2,1,0:T(8,128)(2,1)}, u32[]{:S(2)}, u32[]{:S(2)}) collective-permute-start(bf16[2,2,64,1792]{3,2,1,0:T(8,128)(2,1)S(1)} %get-tuple-element.79), channel_id=1, source_target_pairs={{0,8},{8,16},{16,24},{1,9},{9,17},{17,25},{2,10},{10,18},{18,26},{... | collective-permute-start | bytes 2752520 | tf_op jit(solution)/shard_map/ppermute | solution.py:553
  19.0 2.5 pmax.7
  22.1 3.2 %pack.7 = bf16[2,192,1792]{2,1,0:T(8,128)(2,1)} custom-call(s32[125]{0:T(128)S(1)} %concatenate.10.vector, bf16[2,192,2560]{2,1,0:T(8,128)(2,1)} %bitcast.49), custom_call_target="tpu_custom_call" | custom-call | flops 1 | bytes 1 | tf_op jit(solution)/shard_map/pack/pallas_call | solution.py:96
  25.9 6.5 %collective-permute-done.7.refs_2_.refs_3_ = bf16[2,2,64,1792]{3,2,1,0:T(8,128)(2,1)} collective-permute-done((bf16[2,2,64,1792]{3,2,1,0:T(8,128)(2,1)S(1)}, bf16[2,2,64,1792]{3,2,1,0:T(8,128)(2,1)}, u32[]{:S(2)}, u32[]{:S(2)}) %collective-permute-start.7) | collective-permute-done | bytes 917536 | tf_op jit(solution)/shard_map/ppermute | solution.py:553
  32.6 21.5 %collective-permute-done.8.refs_3_.refs_4_ = bf16[2,2,64,1792]{3,2,1,0:T(8,128)(2,1)} collective-permute-done((bf16[2,2,64,1792]{3,2,1,0:T(8,128)(2,1)}, bf16[2,2,64,1792]{3,2,1,0:T(8,128)(2,1)}, u32[]{:S(2)}, u32[]{:S(2)}) %collective-permute-start.8) | collective-permute-done | bytes 917536 | tf_op jit(solution)/shard_map/ppermute | solution.py:553
  56.2 4.3 %collective-permute-start.18 = (bf16[2,192,1792]{2,1,0:T(8,128)(2,1)}, bf16[2,192,1792]{2,1,0:T(8,128)(2,1)}, u32[]{:S(2)}, u32[]{:S(2)}) collective-permute-start(bf16[2,192,1792]{2,1,0:T(8,128)(2,1)} %pack.7), channel_id=1, source_target_pairs={{0,2},{2,4},{4,6},{1,3},{3,5},{5,7},{8,10},{10,12},{12,14},{9,11},... | collective-permute-start | bytes 4128776 | tf_op jit(solution)/shard_map/ppermute | solution.py:553
  63.3 23.1 %attend_own.1.own.own_stat = bf16[2,192,2688]{2,1,0:T(8,128)(2,1)S(1)} custom-call(s32[125]{0:T(128)S(1)} %concatenate.10.vector, bf16[2,192,2560]{2,1,0:T(8,128)(2,1)} %bitcast.50, bf16[2,2,192,2560]{3,2,1,0:T(8,128)(2,1)} %bitcast.46, bf16[2,2,64,1792]{3,2,1,0:T(8,128)(2,1)} %collective-permute-done.7.refs_2_.refs_3_, ...), custom_call_target="tpu_custom_call" | custom-call | flops 20000000000 | bytes 1 | tf_op jit(solution)/shard_map/attend_own/pallas_call | solution.py:251
  90.7 12.8 %collective-permute-done.19.refs_1_ = bf16[2,192,1792]{2,1,0:T(8,128)(2,1)} collective-permute-done((bf16[2,192,1792]{2,1,0:T(8,128)(2,1)}, bf16[2,192,1792]{2,1,0:T(8,128)(2,1)}, u32[]{:S(2)}, u32[]{:S(2)}) %collective-permute-start.19) | collective-permute-done | bytes 1376288 | tf_op jit(solution)/shard_map/ppermute | solution.py:553
  103.6 28.4 %attend_visitors.3 = (bf16[2,192,1920]{2,1,0:T(8,128)(2,1)}, bf16[2,192,1920]{2,1,0:T(8,128)(2,1)}) custom-call(s32[125]{0:T(128)S(1)} %concatenate.10.vector, bf16[2,192,1792]{2,1,0:T(8,128)(2,1)} %collective-permute-done.18.refs_0_, bf16[2,192,1792]{2,1,0:T(8,128)(2,1)} %collective-permute-done.19.refs_1_, bf16[2,2,192,2560]{3,2,1,0:T(8,128)(2,1)S(1)} %bitcast.47, ...), custom_call_target="tpu_custom_call" | custom-call | flops 1 | bytes 1 | tf_op jit(solution)/shard_map/attend_visitors/pallas_call | solution.py:251
  133.9 9.5 %collective-permute-start.21 = (bf16[2,192,1920]{2,1,0:T(8,128)(2,1)}, bf16[2,192,1920]{2,1,0:T(8,128)(2,1)}, u32[]{:S(2)}, u32[]{:S(2)}) collective-permute-start(bf16[2,192,1920]{2,1,0:T(8,128)(2,1)} %get-tuple-element.97), channel_id=1, source_target_pairs={{2,0},{4,2},{6,4},{3,1},{5,3},{7,5},{10,8},{12,10},{14,12},{11,9},... | collective-permute-start | bytes 4423688 | tf_op jit(solution)/shard_map/ppermute | solution.py:553
  148.9 14.9 %collective-permute-start.22 = (bf16[384,2560]{1,0:T(8,128)(2,1)}, bf16[384,2560]{1,0:T(8,128)(2,1)}, u32[]{:S(2)}, u32[]{:S(2)}) collective-permute-start(bf16[384,2560]{1,0:T(8,128)(2,1)} %bitcast.13.own_hidden), channel_id=1, source_target_pairs={{0,1},{1,0},{2,3},{3,2},{4,5},{5,4},{6,7},{7,6},{8,9},{9,8},{10,11... | collective-permute-start | bytes 5898248 | tf_op jit(solution)/shard_map/ppermute | solution.py:563
  165.6 8.7 %combine.1 = bf16[2,192,2560]{2,1,0:T(8,128)(2,1)S(1)} custom-call(s32[125]{0:T(128)S(1)} %concatenate.10.vector, bf16[2,192,2688]{2,1,0:T(8,128)(2,1)S(1)} %copy-done.17, bf16[2,192,2688]{2,1,0:T(8,128)(2,1)S(1)} %copy-done.17, bf16[2,192,1920]{2,1,0:T(8,128)(2,1)} %collective-permute-done.20.left, bf16[2,192,1920]{2,1,0:T(8,128)(2,1)} %collective-permute-done.21.right, ...), custom_call_target="tpu_custom_call" | custom-call | flops 20000000000 | bytes 1 | tf_op jit(solution)/shard_map/combine/pallas_call | solution.py:328
  174.3 2.9 %collective-permute-start.25 = (bf16[640,1280]{1,0:T(8,128)(2,1)}, bf16[640,1280]{1,0:T(8,128)(2,1)}, u32[]{:S(2)}, u32[]{:S(2)}) collective-permute-start(bf16[640,1280]{1,0:T(8,128)(2,1)} %get-tuple-element.112), channel_id=1, source_target_pairs={{0,6},{2,0},{4,2},{6,4},{1,7},{3,1},{5,3},{7,5},{8,14},{10,8},{12,... | collective-permute-start | bytes 4915208 | tf_op jit(solution)/shard_map/ppermute | solution.py:558
  180.0 4.5 %project.4.own_part = bf16[1,384,1280]{2,1,0:T(8,128)(2,1)S(1)} custom-call(s32[1]{0:T(128)} %bitcast.2.place, bf16[384,2560]{1,0:T(8,128)(2,1)S(1)} %bitcast.39, bf16[2560,1280]{1,0:T(8,128)(2,1)S(1)} %bitcast.43), custom_call_target="tpu_custom_call" | custom-call | flops 1 | bytes 1 | tf_op jit(solution)/shard_map/project/pallas_call | solution.py:396
  184.5 21.1 %collective-permute-start.26 = (bf16[1,384,1280]{2,1,0:T(8,128)(2,1)S(1)}, bf16[1,384,1280]{2,1,0:T(8,128)(2,1)}, u32[]{:S(2)}, u32[]{:S(2)}) collective-permute-start(bf16[1,384,1280]{2,1,0:T(8,128)(2,1)S(1)} %project.4.own_part), channel_id=1, source_target_pairs={{0,1},{1,0},{2,3},{3,2},{4,5},{5,4},{6,7},{7,6},{8,9},{9,8},{10,11... | collective-permute-start | bytes 2949128 | tf_op jit(solution)/shard_map/ppermute | solution.py:563
  213.1 10.4 %project.3.refs_3_ = f32[3,384,1280]{2,1,0:T(8,128)S(1)} custom-call(s32[1]{0:T(128)} %bitcast.2.place, bf16[384,2560]{1,0:T(8,128)(2,1)S(1)} %bitcast.40, bf16[640,1280]{1,0:T(8,128)(2,1)S(1)} %copy-done.5, bf16[640,1280]{1,0:T(8,128)(2,1)S(1)} %copy-done.9, bf16[640,1280]{1,0:T(8,128)(2,1)} %collective-permute-done.11.refs_2_, ...), custom_call_target="tpu_custom_call" | custom-call | flops 1 | bytes 1 | tf_op jit(solution)/shard_map/project/pallas_call | solution.py:396
  223.5 4.4 %pick.1 = (bf16[4,384,1280]{2,1,0:T(8,128)(2,1)S(1)}, f32[4,1,1280]{2,1,0:T(1,128)S(1)}) custom-call(s32[8]{0:T(128)S(1)} %reshape.118.place, bf16[384,2560]{1,0:T(8,128)(2,1)} %bitcast.13.own_hidden, bf16[384,2560]{1,0:T(8,128)(2,1)} %collective-permute-done.22.other_hidden, f32[1,2560]{1,0:T(1,128)S(1)} %get-tuple-element.129.own_gate, ...), custom_call_target="tpu_custom_call" | custom-call | flops 1 | bytes 1 | tf_op jit(solution)/shard_map/pick/pallas_call | solution.py:436
  228.0 4.6 %mix.1 = (bf16[1,384,1280]{2,1,0:T(8,128)(2,1)S(1)}, f32[384,128]{1,0:T(8,128)S(1)}) custom-call(bf16[4,384,1280]{2,1,0:T(8,128)(2,1)S(1)} %get-tuple-element.113.hidden.refs_0_.refs_1_.refs_2_, f32[4,1,1280]{2,1,0:T(1,128)S(1)} %get-tuple-element.111.gate, bf16[1,384,1280]{2,1,0:T(8,128)(2,1)S(1)} %project.4.own_part, ...), custom_call_target="tpu_custom_call" | custom-call | flops 1 | bytes 1 | tf_op jit(solution)/shard_map/mix/pallas_call | solution.py:475
  233.6 6.1 %project.5.refs_3_.refs_4_.refs_5_ = bf16[3,384,1280]{2,1,0:T(8,128)(2,1)S(1)} custom-call(s32[1]{0:T(128)} %bitcast.2.place, bf16[384,2560]{1,0:T(8,128)(2,1)S(1)} %bitcast.41, bf16[640,1280]{1,0:T(8,128)(2,1)} %collective-permute-done.23.refs_0_, bf16[640,1280]{1,0:T(8,128)(2,1)} %collective-permute-done.24.refs_1_, ...), custom_call_target="tpu_custom_call" | custom-call | flops 1 | bytes 1 | tf_op jit(solution)/shard_map/project/pallas_call | solution.py:396
  239.9 5.3 %collective-permute-done.27.refs_6_.refs_7_.refs_8_ = bf16[3,384,1280]{2,1,0:T(8,128)(2,1)} collective-permute-done((bf16[3,384,1280]{2,1,0:T(8,128)(2,1)S(1)}, bf16[3,384,1280]{2,1,0:T(8,128)(2,1)}, u32[]{:S(2)}, u32[]{:S(2)}) %collective-permute-start.27) | collective-permute-done | bytes 2949152 | tf_op jit(solution)/shard_map/ppermute | solution.py:563
  245.2 2.1 copy-done.1
  248.6 7.6 %finish.1 = (bf16[384,2560]{1,0:T(8,128)(2,1)}, bf16[384,2560]{1,0:T(8,128)(2,1)}) custom-call(s32[2]{0:T(128)S(1)} %pad_add_fusion.1.place, f32[4,1,1280]{2,1,0:T(1,128)S(1)} %get-tuple-element.111.gate, f32[1,2560]{1,0:T(1,128)S(1)} %get-tuple-element.128.scale, f32[1,2560]{1,0:T(1,128)S(1)} %get-tuple-element.127.shift_by, ...), custom_call_target="tpu_custom_call" | custom-call | flops 1 | bytes 1 | tf_op jit(solution)/shard_map/finish/pallas_call | solution.py:529
  (105 shorter events, 41.1 us)
Async XLA Ops:
  4.5 49.6 %collective-permute-start.6 = (bf16[640,1280]{1,0:T(8,128)(2,1)}, bf16[640,1280]{1,0:T(8,128)(2,1)S(1)}, u32[]{:S(2)}, u32[]{:S(2)}) collective-permute-start(bf16[640,1280]{1,0:T(8,128)(2,1)} %get-tuple-element.88), channel_id=1, source_target_pairs={{0,2},{2,4},{4,6},{6,0},{1,3},{3,5},{5,7},{7,1},{8,10},{10,12},{12... | collective-permute-start | bytes 4915208 | tf_op jit(solution)/shard_map/ppermute | solution.py:558
  10.6 21.8 %collective-permute-start.7 = (bf16[2,2,64,1792]{3,2,1,0:T(8,128)(2,1)S(1)}, bf16[2,2,64,1792]{3,2,1,0:T(8,128)(2,1)}, u32[]{:S(2)}, u32[]{:S(2)}) collective-permute-start(bf16[2,2,64,1792]{3,2,1,0:T(8,128)(2,1)S(1)} %get-tuple-element.79), channel_id=1, source_target_pairs={{0,8},{8,16},{16,24},{1,9},{9,17},{17,25},{2,10},{10,18},{18,26},{... | collective-permute-start | bytes 2752520 | tf_op jit(solution)/shard_map/ppermute | solution.py:553
  14.7 39.5 %collective-permute-start.8 = (bf16[2,2,64,1792]{3,2,1,0:T(8,128)(2,1)}, bf16[2,2,64,1792]{3,2,1,0:T(8,128)(2,1)}, u32[]{:S(2)}, u32[]{:S(2)}) collective-permute-start(bf16[2,2,64,1792]{3,2,1,0:T(8,128)(2,1)} %get-tuple-element.81), channel_id=1, source_target_pairs={{8,0},{16,8},{24,16},{9,1},{17,9},{25,17},{10,2},{18,10},{26,18},{... | collective-permute-start | bytes 2752520 | tf_op jit(solution)/shard_map/ppermute | solution.py:553
  17.7 14.9 %collective-permute-start.9 = (f32[1,2560]{1,0:T(1,128)S(1)}, f32[1,2560]{1,0:T(1,128)S(1)}, u32[]{:S(2)}, u32[]{:S(2)}) collective-permute-start(f32[1,2560]{1,0:T(1,128)S(1)} %get-tuple-element.129.own_gate), channel_id=1, source_target_pairs={{0,1},{1,0},{2,3},{3,2},{4,5},{5,4},{6,7},{7,6},{8,9},{9,8},{10,11... | collective-permute-start | bytes 30728 | tf_op jit(solution)/shard_map/ppermute | solution.py:563
  32.4 55.4 %collective-permute-start.12 = (bf16[640,1280]{1,0:T(8,128)(2,1)}, bf16[640,1280]{1,0:T(8,128)(2,1)S(1)}, u32[]{:S(2)}, u32[]{:S(2)}) collective-permute-start(bf16[640,1280]{1,0:T(8,128)(2,1)} %get-tuple-element.88), channel_id=1, source_target_pairs={{0,6},{2,0},{4,2},{6,4},{1,7},{3,1},{5,3},{7,5},{8,14},{10,8},{12,... | collective-permute-start | bytes 4915208 | tf_op jit(solution)/shard_map/ppermute | solution.py:558
  54.1 49.4 %collective-permute-start.19 = (bf16[2,192,1792]{2,1,0:T(8,128)(2,1)}, bf16[2,192,1792]{2,1,0:T(8,128)(2,1)}, u32[]{:S(2)}, u32[]{:S(2)}) collective-permute-start(bf16[2,192,1792]{2,1,0:T(8,128)(2,1)} %pack.7), channel_id=1, source_target_pairs={{2,0},{4,2},{6,4},{3,1},{5,3},{7,5},{10,8},{12,10},{14,12},{11,9},... | collective-permute-start | bytes 4128776 | tf_op jit(solution)/shard_map/ppermute | solution.py:553
  56.2 47.4 %collective-permute-start.18 = (bf16[2,192,1792]{2,1,0:T(8,128)(2,1)}, bf16[2,192,1792]{2,1,0:T(8,128)(2,1)}, u32[]{:S(2)}, u32[]{:S(2)}) collective-permute-start(bf16[2,192,1792]{2,1,0:T(8,128)(2,1)} %pack.7), channel_id=1, source_target_pairs={{0,2},{2,4},{4,6},{1,3},{3,5},{5,7},{8,10},{10,12},{12,14},{9,11},... | collective-permute-start | bytes 4128776 | tf_op jit(solution)/shard_map/ppermute | solution.py:553
  62.1 25.7 %collective-permute-start.11 = (bf16[640,1280]{1,0:T(8,128)(2,1)S(1)}, bf16[640,1280]{1,0:T(8,128)(2,1)}, u32[]{:S(2)}, u32[]{:S(2)}) collective-permute-start(bf16[640,1280]{1,0:T(8,128)(2,1)S(1)} %collective-permute-done.6.refs_0_), channel_id=1, source_target_pairs={{0,16},{8,24},{16,0},{24,8},{1,17},{9,25},{17,1},{25,9},{2,18},{10... | collective-permute-start | bytes 4915208 | tf_op jit(solution)/shard_map/ppermute | solution.py:563
  62.1 25.7 %collective-permute-start.10 = (bf16[640,1280]{1,0:T(8,128)(2,1)S(1)}, bf16[640,1280]{1,0:T(8,128)(2,1)S(1)}, u32[]{:S(2)}, u32[]{:S(2)}) collective-permute-start(bf16[640,1280]{1,0:T(8,128)(2,1)S(1)} %collective-permute-done.6.refs_0_), channel_id=1, source_target_pairs={{0,8},{8,0},{16,24},{24,16},{1,9},{9,1},{17,25},{25,17},{2,10},{10... | collective-permute-start | bytes 4915208 | tf_op jit(solution)/shard_map/ppermute | solution.py:563
  87.8 57.6 %copy-start.19 = (bf16[2,24,8,2560]{3,2,1,0:T(8,128)(2,1)S(1)}, bf16[2,24,8,2560]{3,2,1,0:T(8,128)(2,1)}, u32[]{:S(2)}) copy-start(bf16[2,24,8,2560]{3,2,1,0:T(8,128)(2,1)} %param.12) | copy-start | bytes 5898244
  87.8 44.2 %copy-start.6 = (bf16[640,1280]{1,0:T(8,128)(2,1)}, bf16[640,1280]{1,0:T(8,128)(2,1)S(1)}, u32[]{:S(2)}) copy-start(bf16[640,1280]{1,0:T(8,128)(2,1)S(1)} %collective-permute-done.12.refs_6_) | copy-start | bytes 4915204
  89.0 55.0 %collective-permute-start.15 = (bf16[640,1280]{1,0:T(8,128)(2,1)S(1)}, bf16[640,1280]{1,0:T(8,128)(2,1)}, u32[]{:S(2)}, u32[]{:S(2)}) collective-permute-start(bf16[640,1280]{1,0:T(8,128)(2,1)S(1)} %collective-permute-done.6.refs_0_), channel_id=1, source_target_pairs={{0,2},{2,4},{4,6},{6,0},{1,3},{3,5},{5,7},{7,1},{8,10},{10,12},{12... | collective-permute-start | bytes 4915208 | tf_op jit(solution)/shard_map/ppermute | solution.py:558
  89.0 55.0 %collective-permute-start.14 = (bf16[640,1280]{1,0:T(8,128)(2,1)S(1)}, bf16[640,1280]{1,0:T(8,128)(2,1)S(1)}, u32[]{:S(2)}, u32[]{:S(2)}) collective-permute-start(bf16[640,1280]{1,0:T(8,128)(2,1)S(1)} %collective-permute-done.12.refs_6_), channel_id=1, source_target_pairs={{0,16},{8,24},{16,0},{24,8},{1,17},{9,25},{17,1},{25,9},{2,18},{10... | collective-permute-start | bytes 4915208 | tf_op jit(solution)/shard_map/ppermute | solution.py:563
  90.5 53.5 %collective-permute-start.13 = (bf16[640,1280]{1,0:T(8,128)(2,1)S(1)}, bf16[640,1280]{1,0:T(8,128)(2,1)S(1)}, u32[]{:S(2)}, u32[]{:S(2)}) collective-permute-start(bf16[640,1280]{1,0:T(8,128)(2,1)S(1)} %collective-permute-done.12.refs_6_), channel_id=1, source_target_pairs={{0,8},{8,0},{16,24},{24,16},{1,9},{9,1},{17,25},{25,17},{2,10},{10... | collective-permute-start | bytes 4915208 | tf_op jit(solution)/shard_map/ppermute | solution.py:563
  131.9 31.9 %collective-permute-start.20 = (bf16[2,192,1920]{2,1,0:T(8,128)(2,1)}, bf16[2,192,1920]{2,1,0:T(8,128)(2,1)}, u32[]{:S(2)}, u32[]{:S(2)}) collective-permute-start(bf16[2,192,1920]{2,1,0:T(8,128)(2,1)} %get-tuple-element.96), channel_id=1, source_target_pairs={{0,2},{2,4},{4,6},{1,3},{3,5},{5,7},{8,10},{10,12},{12,14},{9,11},... | collective-permute-start | bytes 4423688 | tf_op jit(solution)/shard_map/ppermute | solution.py:553
  133.9 30.0 %collective-permute-start.21 = (bf16[2,192,1920]{2,1,0:T(8,128)(2,1)}, bf16[2,192,1920]{2,1,0:T(8,128)(2,1)}, u32[]{:S(2)}, u32[]{:S(2)}) collective-permute-start(bf16[2,192,1920]{2,1,0:T(8,128)(2,1)} %get-tuple-element.97), channel_id=1, source_target_pairs={{2,0},{4,2},{6,4},{3,1},{5,3},{7,5},{10,8},{12,10},{14,12},{11,9},... | collective-permute-start | bytes 4423688 | tf_op jit(solution)/shard_map/ppermute | solution.py:553
  144.0 30.2 %collective-permute-start.17 = (bf16[640,1280]{1,0:T(8,128)(2,1)}, bf16[640,1280]{1,0:T(8,128)(2,1)}, u32[]{:S(2)}, u32[]{:S(2)}) collective-permute-start(bf16[640,1280]{1,0:T(8,128)(2,1)} %collective-permute-done.15.refs_3_), channel_id=1, source_target_pairs={{0,16},{8,24},{16,0},{24,8},{1,17},{9,25},{17,1},{25,9},{2,18},{10... | collective-permute-start | bytes 4915208 | tf_op jit(solution)/shard_map/ppermute | solution.py:563
  147.7 26.6 %collective-permute-start.16 = (bf16[640,1280]{1,0:T(8,128)(2,1)}, bf16[640,1280]{1,0:T(8,128)(2,1)}, u32[]{:S(2)}, u32[]{:S(2)}) collective-permute-start(bf16[640,1280]{1,0:T(8,128)(2,1)} %collective-permute-done.15.refs_3_), channel_id=1, source_target_pairs={{0,8},{8,0},{16,24},{24,16},{1,9},{9,1},{17,25},{25,17},{2,10},{10... | collective-permute-start | bytes 4915208 | tf_op jit(solution)/shard_map/ppermute | solution.py:563
  148.9 74.6 %collective-permute-start.22 = (bf16[384,2560]{1,0:T(8,128)(2,1)}, bf16[384,2560]{1,0:T(8,128)(2,1)}, u32[]{:S(2)}, u32[]{:S(2)}) collective-permute-start(bf16[384,2560]{1,0:T(8,128)(2,1)} %bitcast.13.own_hidden), channel_id=1, source_target_pairs={{0,1},{1,0},{2,3},{3,2},{4,5},{5,4},{6,7},{7,6},{8,9},{9,8},{10,11... | collective-permute-start | bytes 5898248 | tf_op jit(solution)/shard_map/ppermute | solution.py:563
  174.3 59.3 %collective-permute-start.25 = (bf16[640,1280]{1,0:T(8,128)(2,1)}, bf16[640,1280]{1,0:T(8,128)(2,1)}, u32[]{:S(2)}, u32[]{:S(2)}) collective-permute-start(bf16[640,1280]{1,0:T(8,128)(2,1)} %get-tuple-element.112), channel_id=1, source_target_pairs={{0,6},{2,0},{4,2},{6,4},{1,7},{3,1},{5,3},{7,5},{8,14},{10,8},{12,... | collective-permute-start | bytes 4915208 | tf_op jit(solution)/shard_map/ppermute | solution.py:558
  177.2 56.4 %collective-permute-start.23 = (bf16[640,1280]{1,0:T(8,128)(2,1)}, bf16[640,1280]{1,0:T(8,128)(2,1)}, u32[]{:S(2)}, u32[]{:S(2)}) collective-permute-start(bf16[640,1280]{1,0:T(8,128)(2,1)} %collective-permute-done.11.refs_2_), channel_id=1, source_target_pairs={{0,8},{8,0},{16,24},{24,16},{1,9},{9,1},{17,25},{25,17},{2,10},{10... | collective-permute-start | bytes 4915208 | tf_op jit(solution)/shard_map/ppermute | solution.py:563
  179.0 54.6 %collective-permute-start.24 = (bf16[640,1280]{1,0:T(8,128)(2,1)}, bf16[640,1280]{1,0:T(8,128)(2,1)}, u32[]{:S(2)}, u32[]{:S(2)}) collective-permute-start(bf16[640,1280]{1,0:T(8,128)(2,1)} %collective-permute-done.16.refs_4_), channel_id=1, source_target_pairs={{0,16},{8,24},{16,0},{24,8},{1,17},{9,25},{17,1},{25,9},{2,18},{10... | collective-permute-start | bytes 4915208 | tf_op jit(solution)/shard_map/ppermute | solution.py:563
  184.5 43.5 %collective-permute-start.26 = (bf16[1,384,1280]{2,1,0:T(8,128)(2,1)S(1)}, bf16[1,384,1280]{2,1,0:T(8,128)(2,1)}, u32[]{:S(2)}, u32[]{:S(2)}) collective-permute-start(bf16[1,384,1280]{2,1,0:T(8,128)(2,1)S(1)} %project.4.own_part), channel_id=1, source_target_pairs={{0,1},{1,0},{2,3},{3,2},{4,5},{5,4},{6,7},{7,6},{8,9},{9,8},{10,11... | collective-permute-start | bytes 2949128 | tf_op jit(solution)/shard_map/ppermute | solution.py:563
  239.7 5.6 %collective-permute-start.27 = (bf16[3,384,1280]{2,1,0:T(8,128)(2,1)S(1)}, bf16[3,384,1280]{2,1,0:T(8,128)(2,1)}, u32[]{:S(2)}, u32[]{:S(2)}) collective-permute-start(bf16[3,384,1280]{2,1,0:T(8,128)(2,1)S(1)} %project.5.refs_3_.refs_4_.refs_5_), channel_id=1, source_target_pairs={{0,1},{1,0},{2,3},{3,2},{4,5},{5,4},{6,7},{7,6},{8,9},{9,8},{10,11... | collective-permute-start | bytes 8847368 | tf_op jit(solution)/shard_map/ppermute | solution.py:563
  (21 other events, 170.3 us)
